TPU v7x, 32 devices: a whole 2x2x4 slice. The times are simulated.
32 devices in a mesh: seq: 16 (over z, x, core), head: 2 (over y).
Axes of the slice: x: 2, y: 2, z: 4, core: 2. Of those that a mesh axis runs over, the one named last changes fastest.
Arguments:
- layer_input: bfloat16 [4096, 768], P(('seq', 'head')), may hold values from -6 to 6
- doc_ids: int32 [4096], P(('seq', 'head')), may hold values from -1 to 3, as said below
- cotangent: bfloat16 [4096, 768], P(('seq', 'head')), may hold values from -6 to 6
- ln1_gain: float32 [768], replicated, may hold values from 0.5 to 1.5
- ln1_bias: float32 [768], replicated, may hold values from -1.75 to 1.75
- w_qkv: bfloat16 [768, 3, 768], P(None, None, 'head'), may hold values from -0.21875 to 0.21875
- bias_qv: float32 [2, 768], P(None, 'head'), may hold values from -1.75 to 1.75
- w_out: bfloat16 [768, 768], P('head'), may hold values from -3.5 to 3.5
- b_out: float32 [768], replicated, may hold values from -1.75 to 1.75
- ln2_gain: float32 [768], replicated, may hold values from 0.5 to 1.5
- ln2_bias: float32 [768], replicated, may hold values from -1.75 to 1.75
- w_up: bfloat16 [768, 3072], P('seq', 'head'), may hold values from -0.21875 to 0.21875
- b_up: float32 [3072], replicated, may hold values from -1.75 to 1.75
- w_down: bfloat16 [3072, 768], P('head', 'seq'), may hold values from -0.109375 to 0.109375
- b_down: float32 [768], replicated, may hold values from -1.75 to 1.75
Outputs:
- layer_output: bfloat16 [4096, 768], P(('seq', 'head'))
- grad_input: float32 [4096, 768], P(('seq', 'head'))
- grad_ln1_gain: float32 [768], replicated
- grad_ln1_bias: float32 [768], replicated
- grad_w_qkv: float32 [768, 3, 768], P(None, None, 'head')
- grad_bias_qv: float32 [2, 768], P(None, 'head')
- grad_w_out: float32 [768, 768], P('head')
- grad_b_out: float32 [768], replicated
- grad_ln2_gain: float32 [768], replicated
- grad_ln2_bias: float32 [768], replicated
- grad_w_up: float32 [768, 3072], P('seq', 'head')
- grad_b_up: float32 [3072], replicated
- grad_w_down: float32 [3072, 768], P('head', 'seq')
- grad_b_down: float32 [768], replicated
Inputs may be any that keep to these rules, and one draw needn't show every extreme that they name: `doc_ids`: ids do not fall along the row until its last positions, which hold -1 (padding); there are at most four documents, and the one with id 2 begins within the first 128 positions and ends within the last 256 positions.
All inputs are finite; a program needn't handle non-finite values.
Results may differ from a plain program's by a relative error of at most 0.017.
Values may be sent and summed in bfloat16 or wider, within the bound.
A program may use at most 320 MiB of HBM per device.

v0:
```python
import jax
import jax.numpy as jnp
from jax import lax
from jax.sharding import PartitionSpec as P

HEADS = 12
HEAD_DIM = 64
SEG = 2048


LEVELS = ((1, 1), (2, 2), (4, 4), (8, 6), (16, 12))
EPS = 1e-05
NEGATIVE = -1e30
block_limit = 2048


def from_behind(value, axis, by):
    length = lax.axis_size(axis)
    pairs = [(i, i + by) for i in range(length) if 0 <= i + by < length]
    return lax.ppermute(value, axis, pairs)


def layer_norm(values, gain, shift):
    mean = jnp.mean(values, axis=-1, keepdims=True)
    centred = values - mean
    spread = jnp.mean(centred * centred, axis=-1, keepdims=True)
    return centred * lax.rsqrt(spread + EPS) * gain + shift


def gelu_tanh(values):
    return jax.nn.gelu(values, approximate=True)


def pick_block(length, limit):
    chosen = 1
    for candidate in range(1, min(length, limit) + 1):
        if length % candidate == 0:
            chosen = candidate
    return chosen


def pair_counts(query_pos, key_pos, head_ids):
    total = None
    for factor, rate in LEVELS:
        width = SEG * factor
        same = query_pos[:, :, None] // width == key_pos[:, None, :] // width
        offset = (head_ids % rate)[:, None]
        pick_query = query_pos % width % rate == offset
        pick_key = key_pos % width % rate == offset
        joint = (same & pick_query[:, :, None] & pick_key[:, None, :]).astype(jnp.float32)
        total = joint if total is None else total + joint
    return total


def block_terms(
    query_blk, query_pos, query_doc, key_blk, key_pos, key_doc, head_ids, nearby, scale
):
    scores = (
        jnp.einsum("qhe,khe->hqk", query_blk, key_blk, preferred_element_type=jnp.float32) * scale
    )
    counts = pair_counts(query_pos, key_pos, head_ids)
    same_segment = query_pos[:, :, None] // SEG == key_pos[:, None, :] // SEG
    keep = same_segment if nearby else jnp.logical_not(same_segment)
    allowed = (
        keep
        & (key_pos[:, None, :] <= query_pos[:, :, None])
        & (query_doc[:, :, None] == key_doc[:, None, :])
    )
    return (scores, counts * allowed.astype(jnp.float32))


def per_device(
    layer_input,
    doc_ids,
    cotangent,
    ln1_gain,
    ln1_bias,
    w_qkv,
    bias_qv,
    w_out,
    b_out,
    ln2_gain,
    ln2_bias,
    w_up,
    b_up,
    w_down,
    b_down,
):
    seq_count = lax.axis_size("seq")
    local_heads = HEADS // lax.axis_size("head")
    local_width = local_heads * HEAD_DIM
    scale = HEAD_DIM ** (-0.5)
    f32 = jnp.float32
    b16 = jnp.bfloat16
    x_float = layer_input.astype(f32)
    norm_one = layer_norm(x_float, ln1_gain, ln1_bias)
    norm_rows, row_doc = (
        lax.all_gather(norm_one.astype(b16), "head", axis=0, tiled=True),
        lax.all_gather(doc_ids, "head", axis=0, tiled=True),
    )
    seq_tokens = norm_rows.shape[0]
    half = seq_tokens // 2
    total_tokens = seq_tokens * seq_count
    total_half = total_tokens // 2
    first_pos = lax.axis_index("seq") * seq_tokens
    last_pos = first_pos + seq_tokens - 1
    local_offsets = jnp.arange(seq_tokens, dtype=jnp.int32)
    query_pos = (first_pos + local_offsets)[None, :]
    query_doc = row_doc[None, :]
    head_ids = lax.axis_index("head") * local_heads + jnp.arange(local_heads, dtype=jnp.int32)
    parity = head_ids % 2
    pick_even = parity == 0

    def compact(rows):
        paired = rows.reshape((half, 2) + rows.shape[1:])
        mask = pick_even.reshape((1, local_heads) + (1,) * (rows.ndim - 2))
        return jnp.where(mask, paired[:, 0], paired[:, 1])

    def expand(rows):
        mask = pick_even.reshape((1, local_heads) + (1,) * (rows.ndim - 2))
        zeros = jnp.zeros_like(rows)
        paired = jnp.stack([jnp.where(mask, rows, zeros), jnp.where(mask, zeros, rows)], axis=1)
        return paired.reshape((seq_tokens,) + rows.shape[1:])

    mixed = jnp.einsum("td,dch->tch", norm_rows, w_qkv, preferred_element_type=f32)
    zero_row = jnp.zeros((1, local_width), f32)
    bias_all = jnp.concatenate([bias_qv[0:1], zero_row, bias_qv[1:2]], axis=0)
    qkv = (mixed + bias_all[None]).astype(b16)
    queries = qkv[:, 0]
    query_heads = queries.reshape(seq_tokens, local_heads, HEAD_DIM)
    key_heads = qkv[:, 1].reshape(seq_tokens, local_heads, HEAD_DIM)
    value_heads = qkv[:, 2].reshape(seq_tokens, local_heads, HEAD_DIM)
    local_keys_c = compact(key_heads)
    local_values_c = compact(value_heads)
    far_keys_all, far_values_all, doc_all = (
        lax.all_gather(local_keys_c, "seq", axis=0, tiled=True),
        lax.all_gather(local_values_c, "seq", axis=0, tiled=True),
        lax.all_gather(row_doc, "seq", axis=0, tiled=True),
    )
    segment_count = SEG // seq_tokens
    own_pair = jnp.stack([key_heads, value_heads], axis=1)
    pair_pieces = [own_pair]
    for step in range(1, segment_count):
        pair_pieces.append(from_behind(own_pair, "seq", step))
    near_pairs = jnp.concatenate(pair_pieces, axis=0)
    near_keys = near_pairs[:, 0]
    near_values = near_pairs[:, 1]
    near_flat = jnp.concatenate(
        [first_pos - step * seq_tokens + local_offsets for step in range(segment_count)]
    )
    near_doc = jnp.take(doc_all, jnp.clip(near_flat, 0, total_tokens - 1))[None, :]
    near_pos = near_flat[None, :]
    far_pos = 2 * jnp.arange(total_half, dtype=jnp.int32)[None, :] + parity[:, None]
    doc_pairs = doc_all.reshape(total_half, 2)
    far_doc = jnp.where(pick_even[:, None], doc_pairs[:, 0][None, :], doc_pairs[:, 1][None, :])
    key_block = pick_block(total_half, block_limit)
    blocks = total_half // key_block
    far_key_blocks = far_keys_all.reshape(blocks, key_block, local_heads, HEAD_DIM)
    far_value_blocks = far_values_all.reshape(blocks, key_block, local_heads, HEAD_DIM)
    far_pos_blocks = far_pos.reshape(local_heads, blocks, key_block).transpose(1, 0, 2)
    far_doc_blocks = far_doc.reshape(local_heads, blocks, key_block).transpose(1, 0, 2)
    far_begin = jnp.arange(blocks, dtype=jnp.int32) * (2 * key_block)

    def merge_stats(current, key_blk, key_pos, key_doc, nearby):
        peak, running = current
        scores, counts = block_terms(
            query_heads, query_pos, query_doc, key_blk, key_pos, key_doc, head_ids, nearby, scale
        )
        live = counts > 0
        new_peak = jnp.maximum(peak, jnp.max(jnp.where(live, scores, NEGATIVE), axis=2))
        terms = jnp.where(live, counts * jnp.exp(scores - new_peak[:, :, None]), 0.0)
        return (new_peak, running * jnp.exp(peak - new_peak) + jnp.sum(terms, axis=2))

    start_state = (
        jnp.full((local_heads, seq_tokens), NEGATIVE, f32),
        jnp.zeros((local_heads, seq_tokens), f32),
    )
    near_state = merge_stats(start_state, near_keys, near_pos, near_doc, True)

    def stats_step(state, item):
        key_blk, pos_blk, doc_blk, begin = item
        return (
            lax.cond(
                begin <= last_pos,
                lambda current: merge_stats(current, key_blk, pos_blk, doc_blk, False),
                lambda current: current,
                state,
            ),
            None,
        )

    (peak_all, running_all), _ = lax.scan(
        stats_step, near_state, (far_key_blocks, far_pos_blocks, far_doc_blocks, far_begin)
    )
    lse = peak_all + jnp.log(running_all)

    def add_output(current, key_blk, value_blk, key_pos, key_doc, nearby):
        scores, counts = block_terms(
            query_heads, query_pos, query_doc, key_blk, key_pos, key_doc, head_ids, nearby, scale
        )
        probs = jnp.where(counts > 0, counts * jnp.exp(scores - lse[:, :, None]), 0.0).astype(b16)
        return current + jnp.einsum("hqk,khe->qhe", probs, value_blk, preferred_element_type=f32)

    zero_heads = jnp.zeros((seq_tokens, local_heads, HEAD_DIM), f32)
    near_output = add_output(zero_heads, near_keys, near_values, near_pos, near_doc, True)

    def output_step(accum, item):
        key_blk, value_blk, pos_blk, doc_blk, begin = item
        return (
            lax.cond(
                begin <= last_pos,
                lambda current: add_output(current, key_blk, value_blk, pos_blk, doc_blk, False),
                lambda current: current,
                accum,
            ),
            None,
        )

    attn_exact, _ = lax.scan(
        output_step,
        near_output,
        (far_key_blocks, far_value_blocks, far_pos_blocks, far_doc_blocks, far_begin),
    )
    attn_low = attn_exact.reshape(seq_tokens, local_width).astype(b16)
    branch = lax.psum_scatter(
        jnp.dot(attn_low, w_out, preferred_element_type=f32).astype(jnp.bfloat16),
        "head",
        scatter_dimension=0,
        tiled=True,
    ).astype(jnp.float32)
    hidden_one = x_float + branch + b_out
    norm_two = layer_norm(hidden_one, ln2_gain, ln2_bias)
    norm_low = norm_two.astype(b16)
    dy_low = (cotangent.astype(f32) * (doc_ids >= 0).astype(f32)[:, None]).astype(b16)
    dy_float = dy_low.astype(f32)
    up_rows, down_rows = (
        lax.all_gather(w_up, "seq", axis=0, tiled=True),
        lax.all_gather(w_down, "seq", axis=1, tiled=True),
    )
    up_full, down_full = (
        lax.all_gather(up_rows, "head", axis=1, tiled=True),
        lax.all_gather(down_rows, "head", axis=0, tiled=True),
    )
    pre_act = jnp.dot(norm_low, up_full, preferred_element_type=f32) + b_up
    act_low = gelu_tanh(pre_act).astype(b16)
    ffn_result = jnp.dot(act_low, down_full, preferred_element_type=f32)
    d_act = jnp.einsum("td,fd->tf", dy_low, down_full, preferred_element_type=f32)
    _, gelu_back = jax.vjp(gelu_tanh, pre_act)
    d_pre = gelu_back(d_act)[0]
    d_pre_low = d_pre.astype(b16)
    bias_up_grad = jnp.sum(d_pre, axis=0)
    up_parts = jnp.einsum("td,tf->df", norm_low, d_pre_low, preferred_element_type=f32)
    down_parts = jnp.einsum("tf,td->fd", act_low, dy_low, preferred_element_type=f32)
    up_grad, down_grad = (
        lax.psum_scatter(
            up_parts.astype(jnp.bfloat16), "head", scatter_dimension=1, tiled=True
        ).astype(jnp.float32),
        lax.psum_scatter(
            down_parts.astype(jnp.bfloat16), "head", scatter_dimension=0, tiled=True
        ).astype(jnp.float32),
    )
    d_norm_two = jnp.einsum("tf,df->td", d_pre_low, up_full, preferred_element_type=f32)
    layer_output = (hidden_one + ffn_result + b_down).astype(b16)
    w_up_grad, w_down_grad = (
        lax.psum_scatter(up_grad, "seq", scatter_dimension=0, tiled=True),
        lax.psum_scatter(down_grad, "seq", scatter_dimension=1, tiled=True),
    )
    _, norm_two_back = jax.vjp(layer_norm, hidden_one, ln2_gain, ln2_bias)
    d_hidden_norm, gain_two_grad, bias_two_grad = norm_two_back(d_norm_two)
    d_hidden = dy_float + d_hidden_norm
    bias_out_grad = jnp.sum(d_hidden, axis=0)
    bias_down_grad = jnp.sum(dy_float, axis=0)
    hidden_rows = lax.all_gather(d_hidden.astype(b16), "head", axis=0, tiled=True)
    w_out_part = jnp.einsum("tc,td->cd", attn_low, hidden_rows, preferred_element_type=f32)
    d_attn = jnp.einsum("td,cd->tc", hidden_rows, w_out, preferred_element_type=f32).astype(b16)
    d_attn_heads = d_attn.reshape(seq_tokens, local_heads, HEAD_DIM)
    delta_rows = jnp.sum(d_attn_heads.astype(f32) * attn_exact, axis=2)
    delta = delta_rows.T

    def score_grads(key_blk, value_blk, key_pos, key_doc, nearby):
        scores, counts = block_terms(
            query_heads, query_pos, query_doc, key_blk, key_pos, key_doc, head_ids, nearby, scale
        )
        exact = jnp.where(counts > 0, counts * jnp.exp(scores - lse[:, :, None]), 0.0)
        d_prob = jnp.einsum("qhe,khe->hqk", d_attn_heads, value_blk, preferred_element_type=f32)
        d_score = (exact * (d_prob - delta[:, :, None])).astype(b16)
        return (exact, d_score)

    exact_near, d_score_near = score_grads(near_keys, near_values, near_pos, near_doc, True)
    d_query_near = jnp.einsum("hqk,khe->qhe", d_score_near, near_keys, preferred_element_type=f32)
    near_key_grad = jnp.einsum(
        "hqk,qhe->khe", d_score_near, query_heads, preferred_element_type=f32
    )
    near_value_grad = jnp.einsum(
        "hqk,qhe->khe", exact_near.astype(b16), d_attn_heads, preferred_element_type=f32
    )
    near_pair_grads = jnp.stack([near_key_grad, near_value_grad], axis=1)
    pair_grad = near_pair_grads[:seq_tokens]
    for step in range(1, segment_count):
        piece = near_pair_grads[step * seq_tokens : (step + 1) * seq_tokens]
        pair_grad = pair_grad + from_behind(piece.astype(jnp.bfloat16), "seq", -step).astype(
            piece.dtype
        )

    def query_grad_step(accum, item):
        key_blk, value_blk, pos_blk, doc_blk, begin = item

        def query_compute(current):
            _, d_score = score_grads(key_blk, value_blk, pos_blk, doc_blk, False)
            return current + jnp.einsum(
                "hqk,khe->qhe", d_score, key_blk, preferred_element_type=f32
            )

        return (lax.cond(begin <= last_pos, query_compute, lambda current: current, accum), None)

    d_query, _ = lax.scan(
        query_grad_step,
        d_query_near,
        (far_key_blocks, far_value_blocks, far_pos_blocks, far_doc_blocks, far_begin),
    )
    d_query = d_query * scale
    stats_rows = jnp.stack([compact(lse.T), compact(delta_rows)], axis=1)
    stats_all = lax.all_gather(stats_rows, "seq", axis=0, tiled=True)
    local_key_pos = first_pos + 2 * jnp.arange(half, dtype=jnp.int32)[None, :] + parity[:, None]
    local_key_doc = compact(jnp.broadcast_to(row_doc[:, None], (seq_tokens, local_heads))).T
    zero_compact = jnp.zeros((half, local_heads, HEAD_DIM), f32)
    query_piece = lax.all_gather(compact(query_heads), "seq", axis=0, tiled=True)
    grad_piece = lax.all_gather(compact(d_attn_heads), "seq", axis=0, tiled=True)
    length = query_piece.shape[0]
    size = pick_block(length, block_limit)
    number = length // size
    pos_piece = 2 * jnp.arange(length, dtype=jnp.int32)[None, :] + parity[:, None]
    items = (
        query_piece.reshape(number, size, local_heads, HEAD_DIM),
        grad_piece.reshape(number, size, local_heads, HEAD_DIM),
        stats_all.reshape(number, size, 2, local_heads),
        pos_piece.reshape(local_heads, number, size).transpose(1, 0, 2),
        far_doc.reshape(local_heads, number, size).transpose(1, 0, 2),
    )

    def one_step(current, item):
        query_blk, grad_blk, stats_blk, pos_blk, doc_blk = item

        def one_compute(pair):
            key_grad, value_grad = pair
            scores, counts = block_terms(
                query_blk,
                pos_blk,
                doc_blk,
                local_keys_c,
                local_key_pos,
                local_key_doc,
                head_ids,
                False,
                scale,
            )
            exact = jnp.where(
                counts > 0, counts * jnp.exp(scores - stats_blk[:, 0].T[:, :, None]), 0.0
            )
            d_prob = jnp.einsum(
                "qhe,khe->hqk", grad_blk, local_values_c, preferred_element_type=f32
            )
            d_score = (exact * (d_prob - stats_blk[:, 1].T[:, :, None])).astype(b16)
            key_grad = key_grad + jnp.einsum(
                "hqk,qhe->khe", d_score, query_blk, preferred_element_type=f32
            )
            value_grad = value_grad + jnp.einsum(
                "hqk,qhe->khe", exact.astype(b16), grad_blk, preferred_element_type=f32
            )
            return (key_grad, value_grad)

        return (
            lax.cond(jnp.max(pos_blk) >= first_pos, one_compute, lambda pair: pair, current),
            None,
        )

    result, _ = lax.scan(one_step, (zero_compact, zero_compact), items)
    far_key_grad, far_value_grad = result
    d_key = (pair_grad[:, 0] + expand(far_key_grad)) * scale
    d_value = pair_grad[:, 1] + expand(far_value_grad)
    d_qkv = jnp.stack(
        [
            d_query.reshape(seq_tokens, local_width),
            d_key.reshape(seq_tokens, local_width),
            d_value.reshape(seq_tokens, local_width),
        ],
        axis=1,
    ).astype(b16)
    d_qkv_float = d_qkv.astype(f32)
    bias_qv_part = jnp.stack(
        [jnp.sum(d_qkv_float[:, 0], axis=0), jnp.sum(d_qkv_float[:, 2], axis=0)], axis=0
    )
    w_qkv_part = jnp.einsum("td,tch->dch", norm_rows, d_qkv, preferred_element_type=f32)
    d_norm_one = lax.psum_scatter(
        jnp.einsum("tch,dch->td", d_qkv, w_qkv, preferred_element_type=f32).astype(jnp.bfloat16),
        "head",
        scatter_dimension=0,
        tiled=True,
    ).astype(jnp.float32)
    _, norm_one_back = jax.vjp(layer_norm, x_float, ln1_gain, ln1_bias)
    d_x_norm, gain_one_grad, bias_one_grad = norm_one_back(d_norm_one)
    grad_input = d_hidden + d_x_norm
    w_qkv_grad, bias_qv_grad, w_out_grad = lax.psum((w_qkv_part, bias_qv_part, w_out_part), "seq")
    summed = lax.psum(
        (
            gain_one_grad,
            bias_one_grad,
            gain_two_grad,
            bias_two_grad,
            bias_out_grad,
            bias_up_grad,
            bias_down_grad,
        ),
        ("seq", "head"),
    )
    return (
        layer_output,
        grad_input,
        summed[0],
        summed[1],
        w_qkv_grad,
        bias_qv_grad,
        w_out_grad,
        summed[4],
        summed[2],
        summed[3],
        w_up_grad,
        summed[5],
        w_down_grad,
        summed[6],
    )


def solution(mesh):
    in_specs = (
        P(("seq", "head"), None),
        P(("seq", "head")),
        P(("seq", "head"), None),
        P(),
        P(),
        P(None, None, "head"),
        P(None, "head"),
        P("head", None),
        P(),
        P(),
        P(),
        P("seq", "head"),
        P(),
        P("head", "seq"),
        P(),
    )
    out_specs = (
        P(("seq", "head"), None),
        P(("seq", "head"), None),
        P(),
        P(),
        P(None, None, "head"),
        P(None, "head"),
        P("head", None),
        P(),
        P(),
        P(),
        P("seq", "head"),
        P(),
        P("head", "seq"),
        P(),
    )
    return jax.shard_map(
        per_device, mesh=mesh, in_specs=in_specs, out_specs=out_specs, check_vma=False
    )
```

profile of v0, /device:TPU:0, one launch (start us, length us, event | category | flops | bytes accessed | tf_op | source)
XLA Modules:
  0.0 985.3 jit_solution(671337161789888563)
XLA Ops:
  12.0 8.5 all_gather.39
  51.6 37.6 %all-gather.1 = s32[16,1,256]{2,1,0:T(1,128)S(1)} all-gather(s32[1,1,256]{2,1,0:T(1,128)S(1)} %bitcast.223), channel_id=1, replica_groups=mesh['seq'=16,'head'=2] {'seq'}, dimensions={0}, use_global_device_ids=true | all-gather | bytes 17408 | tf_op jit(solution)/shard_map/all_gather | solution.py:138
  89.4 11.8 %gather_fusion = s32[2048]{0:T(1024)S(1)} fusion(s32[4096]{0:T(1024)S(1)} %bitcast.196, s32[2048]{0:T(1024)S(1)} %broadcast_clamp_fusion), kind=kCustom, calls=%fused_computation | custom fusion | bytes 24576 | tf_op jit(solution)/shard_map/jit(_take)/gather | solution.py:151
  116.2 10.7 %collective-permute-start.5 = (bf16[256,2,6,64]{0,3,2,1:T(8,128)(2,1)}, bf16[256,2,6,64]{0,3,2,1:T(8,128)(2,1)S(1)}, u32[]{:S(2)}, u32[]{:S(2)}) collective-permute-start(bf16[256,2,6,64]{0,3,2,1:T(8,128)(2,1)} %get-tuple-element.812), channel_id=1, source_target_pairs={{0,12},{2,14},{4,16},{6,18},{8,20},{10,22},{12,24},{14,26},{16,28}... | collective-permute-start | bytes 1179656 | tf_op jit(solution)/shard_map/ppermute | solution.py:20
  140.9 5.9 collective-permute-done.6
  147.6 12.1 %select_reduce_fusion.3 = (f32[6,256]{1,0:T(8,128)S(1)}, f32[6,256,2048]{2,1,0:T(8,128)S(1)}) fusion(f32[256,2048]{1,0:T(8,128)S(1)} %copy-done.8, pred[6,2048]{1,0:T(8,128)(4,1)S(1)} %broadcast_compare_fusion.28, pred[6,256]{1,0:T(8,128)(4,1)S(1)} %broadcast_compare_fusion.32, pred[256,2048]{1,0:T(8,128)(4,1)S(1)} %broadcast_compare_fusion.24, ...), kind=kOutput, calls=%fused_computation.462 | convolution fusion | flops 468711936 | bytes 20705280 | tf_op jit(solution)/shard_map/qhe,khe->hqk/dot_general | solution.py:59
  159.8 13.8 %select_reduce_fusion.2 = f32[6,256]{1,0:T(8,128)S(1)} fusion(f32[6,256,2048]{2,1,0:T(8,128)S(1)} %get-tuple-element.839, f32[6,256]{1,0:T(8,128)S(1)} %broadcast_maximum_fusion, f32[256,2048]{1,0:T(8,128)S(1)} %copy-done.8, pred[6,2048]{1,0:T(8,128)(4,1)S(1)} %broadcast_compare_fusion.28, pred[6,256]{1,0:T(8,128)(4,1)S(1)} %broadcast_compare_fusion.32, ...), kind=kLoop, calls=%fused_computation.461 | loop fusion | flops 72350208 | bytes 18941952 | tf_op jit(solution)/shard_map/reduce_sum | solution.py:172
  174.2 44.8 %conditional.4 = ((f32[6,256]{1,0:T(8,128)S(1)}, f32[6,256]{1,0:T(8,128)})) conditional(s32[]{:T(128)} %convert_element_type.249, (f32[6,256]{1,0:T(8,128)S(1)}, f32[6,256]{1,0:T(8,128)}) %tuple.67, (s32[256]{0:T(256)S(1)}, s32[6,2048]{1,0:T(8,128)S(1)}, s32[256]{0:T(256)}, s32[6,2048]{1,0:T(8,128)S(1)}, s32[1,256]{1,0:T(1,128)}, ...), branch_computations={%region_4.5_spmd, %region_5.8_spmd} | conditional | flops 611886016 | bytes 28248940 | solution.py:183
  176.2 19.7 %select_reduce_fusion.1 = (f32[6,256]{1,0:T(8,128)S(1)}, f32[6,256,2048]{2,1,0:T(8,128)S(1)}) fusion(pred[6,2048]{1,0:T(8,128)(4,1)S(1)} %get-tuple-element.726, pred[6,256]{1,0:T(8,128)(4,1)S(1)} %get-tuple-element.741, s32[6,2048]{1,0:T(8,128)S(1)} %get-tuple-element.722, s32[256]{0:T(256)S(1)} %get-tuple-element.730, ...), kind=kOutput, calls=%fused_computation.9 | convolution fusion | flops 503314944 | bytes 14765056 | tf_op jit(solution)/shard_map/while/body/eval_jaxpr/cond/branch_1_fun/qhe,khe->hqk/dot_general | solution.py:59
  195.8 21.9 %select_reduce_fusion = f32[6,256]{1,0:T(8,128)S(1)} fusion(f32[6,256,2048]{2,1,0:T(8,128)S(1)} %get-tuple-element.740, f32[6,256]{1,0:T(8,128)S(1)} %max.7, pred[6,2048]{1,0:T(8,128)(4,1)S(1)} %get-tuple-element.726, pred[6,256]{1,0:T(8,128)(4,1)S(1)} %get-tuple-element.741, s32[6,2048]{1,0:T(8,128)S(1)} %get-tuple-element.722, ...), kind=kLoop, calls=%fused_computation.8 | loop fusion | flops 106953216 | bytes 13001728 | tf_op jit(solution)/shard_map/while/body/eval_jaxpr/cond/branch_1_fun/reduce_sum | solution.py:172
  219.7 16.5 %multiply_select_fusion.1 = f32[6,256,2048]{2,1,0:T(8,128)S(1)} fusion(f32[6,256,2048]{2,1,0:T(8,128)} %copy-done.3, f32[6,256]{1,0:T(8,128)S(1)} %log_add_fusion, f32[256,2048]{1,0:T(8,128)} %get-tuple-element.815, pred[6,2048]{1,0:T(8,128)(4,1)} %copy-done.43, pred[6,256]{1,0:T(8,128)(4,1)S(1)} %broadcast_compare_fusion.32, ...), kind=kLoop, calls=%fused_computation.460 | loop fusion | flops 69206016 | bytes 31518720 | tf_op jit(solution)/shard_map/jit(_where)/select_n | solution.py:201
  242.9 21.3 %conditional.5 = (f32[256,6,64]{0,2,1:T(8,128)S(1)}) conditional(s32[]{:T(128)} %convert_element_type.249, f32[256,6,64]{0,2,1:T(8,128)S(1)} %fusion.163, (s32[256]{0:T(256)S(1)}, s32[6,2048]{1,0:T(8,128)S(1)}, s32[256]{0:T(256)S(1)}, s32[6,2048]{1,0:T(8,128)S(1)}, s32[1,256]{1,0:T(1,128)S(1)}, /*index=5*/s32[6]{0:T(128)S(1)}, ...), branch_computations={%region_8.9_spmd, %region_9.10_spmd} | conditional | flops 913971136 | bytes 4958016 | solution.py:210
  243.5 20.6 %fusion.34 = f32[256,6,64]{0,2,1:T(8,128)S(1)} fusion(f32[256,6,64]{0,2,1:T(8,128)S(1)} %get-tuple-element.352, bf16[2048,6,64]{0,2,1:T(8,128)(2,1)} %get-tuple-element.362, f32[6,256]{1,0:T(8,128)} %get-tuple-element.361, s32[6,2048]{1,0:T(8,128)S(1)} %get-tuple-element.753, s32[6,2048]{1,0:T(8,128)S(1)} %get-tuple-element.752, ...), kind=kOutput, calls=%fused_computation.120 | convolution fusion | flops 912359424 | bytes 4541440 | tf_op jit(solution)/shard_map/while/body/eval_jaxpr/cond/branch_1_fun/hqk,khe->qhe/dot_general | solution.py:202
  269.5 37.9 %reduce-scatter.9.cloned.1.call-done = bf16[128,768]{1,0:T(8,128)(2,1)} async-done(((bf16[256,768]{1,0:T(8,128)(2,1)}), bf16[128,768]{1,0:T(8,128)(2,1)}) %reduce-scatter.9.cloned.1.call-update) | async-done | bytes 196624 | tf_op jit(solution)/shard_map/reduce_scatter | solution.py:225
  310.2 61.4 %all-gather.17.cloned.1.call-done = bf16[768,3072]{1,0:T(8,128)(2,1)} async-done(((bf16[768,1536]{1,0:T(8,128)(2,1)}), bf16[768,3072]{1,0:T(8,128)(2,1)}) %all-gather.17.cloned.1.call-update) | async-done | bytes 4718608 | tf_op jit(solution)/shard_map/all_gather | solution.py:241
  374.9 61.1 %all-gather.21.cloned.1.call-done = bf16[3072,768]{0,1:T(8,128)(2,1)} async-done(((bf16[1536,768]{0,1:T(8,128)(2,1)}), bf16[3072,768]{0,1:T(8,128)(2,1)}) %all-gather.21.cloned.1.call-update) | async-done | bytes 4718608 | tf_op jit(solution)/shard_map/all_gather | solution.py:242
  444.6 7.3 all_gather.48
  478.1 7.2 multiply_convert_fusion.7
  505.2 6.1 fusion.166
  511.3 36.8 %conditional.6 = (f32[256,6,64]{0,2,1:T(8,128)}) conditional(s32[]{:T(128)} %convert_element_type.249, f32[256,6,64]{0,2,1:T(8,128)} %fusion.166, (s32[256]{0:T(256)S(1)}, s32[6,2048]{1,0:T(8,128)}, s32[256]{0:T(256)}, s32[6,2048]{1,0:T(8,128)}, s32[1,256]{1,0:T(1,128)}, /*index=5*/s32[6]{0:T(128)}, bf16[256,6,64]{0,2,1:T(8,128)(2,1)}, ...), branch_computations={%region_16.17_spmd, %region_17.18_spmd} | conditional | flops 1322915840 | bytes 32100340 | solution.py:314
  511.3 8.0 fusion.232
  523.4 24.7 %fusion.64 = f32[256,6,64]{0,2,1:T(8,128)} fusion(f32[256,6,64]{0,2,1:T(8,128)} %get-tuple-element.363, bf16[2048,6,64]{0,2,1:T(8,128)(2,1)} %get-tuple-element.371, f32[6,256,2048]{2,1,0:T(8,128)} %fusion.232, f32[6,256]{1,0:T(8,128)S(1)} %get-tuple-element.375, f32[6,256]{1,0:T(8,128)} %get-tuple-element.372, s32[6,2048]{1,0:T(8,128)} %get-tuple-element.778, ...), kind=kOutput, calls=%fused_computation.229 | convolution fusion | flops 918650880 | bytes 17130496 | tf_op jit(solution)/shard_map/while/body/eval_jaxpr/cond/branch_1_fun/hqk,khe->qhe/dot_general | solution.py:310
  554.9 31.4 %all_gather.50 = f32[2048,2,6]{0,1,2:T(2,128)} all-gather(f32[128,2,6]{0,1,2:T(2,128)S(1)} %pad_maximum_fusion.6), channel_id=1, replica_groups=mesh['seq'=16,'head'=2] {'seq'}, dimensions={0}, use_global_device_ids=true | all-gather | bytes 104448 | tf_op jit(solution)/shard_map/all_gather | solution.py:323
  594.0 46.8 %conditional.7 = (f32[128,6,64]{0,2,1:T(8,128)}, f32[128,6,64]{0,2,1:T(8,128)}) conditional(s32[]{:T(128)} %convert_element_type.282, (f32[128,6,64]{2,1,0:T(8,128)}) %tuple.97, (s32[6,2048]{1,0:T(8,128)}, s32[]{:T(128)}, s32[1,128]{1,0:T(1,128)}, s32[6]{0:T(128)S(1)}, s32[6,2048]{1,0:T(8,128)}, /*index=5*/pred[6]{0:T(512)(128)(4,1)S(1)}, ...), branch_computations={%region_19.20_spmd, %region_20.21_spmd} | conditional | flops 865274560 | bytes 27876738 | solution.py:373
  605.0 23.9 %multiply_select_fusion = f32[6,2048,128]{2,1,0:T(8,128)} fusion(bf16[2048,6,64]{0,2,1:T(8,128)(2,1)} %get-tuple-element.385, f32[6,2048]{1,0:T(8,128)} %get-tuple-element.693, s32[6,128]{1,0:T(8,128)S(1)} %get-tuple-element.708, s32[6,2048]{1,0:T(8,128)S(1)} %get-tuple-element.702, s32[6,128]{1,0:T(8,128)S(1)} %get-tuple-element.709, ...), kind=kOutput, calls=%fused_computation.333 | convolution fusion | flops 253231104 | bytes 8429568 | tf_op jit(solution)/shard_map/while/body/eval_jaxpr/cond/branch_1_fun/qhe,khe->hqk/dot_general | solution.py:59
  628.9 7.2 fusion.100
  671.6 5.2 reduce-scatter.17.cloned.1.call-done
  686.7 35.1 %psum.73 = f32[2,384]{1,0:T(2,128)} all-reduce(f32[2,384]{1,0:T(2,128)S(1)} %pad_maximum_fusion.7), channel_id=1, replica_groups=mesh['seq'=16,'head'=2] {'seq'}, use_global_device_ids=true, to_apply=%region_31.32 | all-reduce | flops 768 | bytes 6144 | tf_op jit(solution)/shard_map/psum | solution.py:403
  726.9 38.5 %all-reduce = (f32[768]{0:T(1024)}, f32[768]{0:T(1024)}, f32[768]{0:T(1024)}, f32[768]{0:T(1024)}, f32[768]{0:T(1024)}, /*index=5*/f32[3072]{0:T(1024)}, f32[768]{0:T(1024)}) all-reduce(f32[768]{0:T(1024)S(1)} %get-tuple-element.668, f32[768]{0:T(1024)S(1)} %get-tuple-element.673, ...), channel_id=1, replica_groups=mesh['seq'=16,'head'=2] {'seq','head'}, use_global_device_ids=true, to_apply=%region_25.26 | all-reduce | flops 7680 | bytes 61440 | tf_op jit(solution)/shard_map/psum | solution.py:404
  765.4 48.7 %all-reduce.4.cloned.1.call-done = (f32[768,3,384]{2,0,1:T(8,128)}, f32[384,768]{1,0:T(8,128)}) async-done(((f32[768,3,384]{2,0,1:T(8,128)}, f32[384,768]{1,0:T(8,128)}), (f32[768,3,384]{2,0,1:T(8,128)}, f32[384,768]{1,0:T(8,128)})) %all-reduce.4.cloned.1.call-update) | async-done | bytes 4718608 | tf_op jit(solution)/shard_map/psum | solution.py:403
  814.1 79.7 %reduce-scatter.15.cloned.1.call-done = f32[48,1536]{1,0:T(8,128)} async-done(((f32[768,1536]{1,0:T(8,128)}), f32[48,1536]{1,0:T(8,128)}) %reduce-scatter.15.cloned.1.call-update) | async-done | bytes 294928 | tf_op jit(solution)/shard_map/reduce_scatter | solution.py:265
  893.8 79.4 %reduce-scatter.19.cloned.1.call-done = f32[48,1536]{1,0:T(8,128)} async-done(((f32[768,1536]{1,0:T(8,128)}), f32[48,1536]{1,0:T(8,128)}) %reduce-scatter.19.cloned.1.call-update) | async-done | bytes 294928
  (460 shorter events, 226.4 us)
Async XLA Ops:
  7.2 167.0 %all-gather.11.cloned.1.call-start = ((), (), s32[]{:S(2)}) async-start(), calls=%async_computation.6 | async-start | bytes 1671168 | tf_op jit(solution)/shard_map/all_gather | solution.py:136
  26.1 216.7 %all-gather.13.cloned.1.call-start = ((), (), s32[]{:S(2)}) async-start(), calls=%async_computation.7 | async-start | bytes 1671168 | tf_op jit(solution)/shard_map/all_gather | solution.py:137
  27.0 239.2 %all-gather.15.cloned.1.call-start = ((), (), s32[]{:S(2)}) async-start(), calls=%async_computation.9 | async-start | bytes 2506752 | tf_op jit(solution)/shard_map/all_gather | solution.py:237
  27.7 239.1 %all-gather.19.cloned.1.call-start = ((), (), s32[]{:S(2)}) async-start(), calls=%async_computation.11 | async-start | bytes 2506752 | tf_op jit(solution)/shard_map/all_gather | solution.py:238
  29.0 87.2 %collective-permute-start = (bf16[256,2,6,64]{0,3,2,1:T(8,128)(2,1)}, bf16[256,2,6,64]{0,3,2,1:T(8,128)(2,1)}, u32[]{:S(2)}, u32[]{:S(2)}) collective-permute-start(bf16[256,2,6,64]{0,3,2,1:T(8,128)(2,1)} %get-tuple-element.812), channel_id=1, source_target_pairs={{0,2},{2,4},{4,6},{6,8},{8,10},{10,12},{12,14},{14,16},{16,18},{18... | collective-permute-start | bytes 1179656 | tf_op jit(solution)/shard_map/ppermute | solution.py:20
  31.0 97.7 %collective-permute-start.1 = (bf16[256,2,6,64]{0,3,2,1:T(8,128)(2,1)}, bf16[256,2,6,64]{0,3,2,1:T(8,128)(2,1)}, u32[]{:S(2)}, u32[]{:S(2)}) collective-permute-start(bf16[256,2,6,64]{0,3,2,1:T(8,128)(2,1)} %get-tuple-element.812), channel_id=1, source_target_pairs={{0,4},{2,6},{4,8},{6,10},{8,12},{10,14},{12,16},{14,18},{16,20},{1... | collective-permute-start | bytes 1179656 | tf_op jit(solution)/shard_map/ppermute | solution.py:20
  35.3 99.5 %collective-permute-start.2 = (bf16[256,2,6,64]{0,3,2,1:T(8,128)(2,1)}, bf16[256,2,6,64]{0,3,2,1:T(8,128)(2,1)}, u32[]{:S(2)}, u32[]{:S(2)}) collective-permute-start(bf16[256,2,6,64]{0,3,2,1:T(8,128)(2,1)} %get-tuple-element.812), channel_id=1, source_target_pairs={{0,6},{2,8},{4,10},{6,12},{8,14},{10,16},{12,18},{14,20},{16,22},{... | collective-permute-start | bytes 1179656 | tf_op jit(solution)/shard_map/ppermute | solution.py:20
  39.7 96.8 %collective-permute-start.3 = (bf16[256,2,6,64]{0,3,2,1:T(8,128)(2,1)}, bf16[256,2,6,64]{0,3,2,1:T(8,128)(2,1)}, u32[]{:S(2)}, u32[]{:S(2)}) collective-permute-start(bf16[256,2,6,64]{0,3,2,1:T(8,128)(2,1)} %get-tuple-element.812), channel_id=1, source_target_pairs={{0,8},{2,10},{4,12},{6,14},{8,16},{10,18},{12,20},{14,22},{16,24},... | collective-permute-start | bytes 1179656 | tf_op jit(solution)/shard_map/ppermute | solution.py:20
  43.2 95.1 %collective-permute-start.4 = (bf16[256,2,6,64]{0,3,2,1:T(8,128)(2,1)}, bf16[256,2,6,64]{0,3,2,1:T(8,128)(2,1)}, u32[]{:S(2)}, u32[]{:S(2)}) collective-permute-start(bf16[256,2,6,64]{0,3,2,1:T(8,128)(2,1)} %get-tuple-element.812), channel_id=1, source_target_pairs={{0,10},{2,12},{4,14},{6,16},{8,18},{10,20},{12,22},{14,24},{16,26}... | collective-permute-start | bytes 1179656 | tf_op jit(solution)/shard_map/ppermute | solution.py:20
  45.3 262.2 %reduce-scatter.9.cloned.1.call-start = ((), (), s32[]{:S(2)}) async-start(), calls=%async_computation.8 | async-start | bytes 589824 | tf_op jit(solution)/shard_map/reduce_scatter | solution.py:225
  104.3 138.5 %copy-start.12 = (s32[6,2048]{1,0:T(8,128)}, s32[6,2048]{1,0:T(8,128)S(1)}, u32[]{:S(2)}) copy-start(s32[6,2048]{1,0:T(8,128)S(1)} %get-tuple-element.817) | copy-start | bytes 147460
  109.3 133.5 %copy-start.41 = (s32[6,2048]{1,0:T(8,128)}, s32[6,2048]{1,0:T(8,128)S(1)}, u32[]{:S(2)}) copy-start(s32[6,2048]{1,0:T(8,128)S(1)} %broadcast_select_fusion.3) | copy-start | bytes 147460
  116.2 23.9 %collective-permute-start.5 = (bf16[256,2,6,64]{0,3,2,1:T(8,128)(2,1)}, bf16[256,2,6,64]{0,3,2,1:T(8,128)(2,1)S(1)}, u32[]{:S(2)}, u32[]{:S(2)}) collective-permute-start(bf16[256,2,6,64]{0,3,2,1:T(8,128)(2,1)} %get-tuple-element.812), channel_id=1, source_target_pairs={{0,12},{2,14},{4,16},{6,18},{8,20},{10,22},{12,24},{14,26},{16,28}... | collective-permute-start | bytes 1179656 | tf_op jit(solution)/shard_map/ppermute | solution.py:20
  128.7 18.1 %collective-permute-start.6 = (bf16[256,2,6,64]{0,3,2,1:T(8,128)(2,1)}, bf16[256,2,6,64]{0,3,2,1:T(8,128)(2,1)S(1)}, u32[]{:S(2)}, u32[]{:S(2)}) collective-permute-start(bf16[256,2,6,64]{0,3,2,1:T(8,128)(2,1)} %get-tuple-element.812), channel_id=1, source_target_pairs={{0,14},{2,16},{4,18},{6,20},{8,22},{10,24},{12,26},{14,28},{16,30}... | collective-permute-start | bytes 1179656 | tf_op jit(solution)/shard_map/ppermute | solution.py:20
  266.1 105.5 %copy-start.42 = (f32[768]{0:T(1024)S(1)}, f32[768]{0:T(1024)}, u32[]{:S(2)}) copy-start(f32[768]{0:T(1024)} %param.32) | copy-start | bytes 9220
  266.1 105.5 %all-gather.17.cloned.1.call-start = ((), (), s32[]{:S(2)}) async-start(), calls=%async_computation.10 | async-start | bytes 7077888 | tf_op jit(solution)/shard_map/all_gather | solution.py:241
  266.7 169.2 %all-gather.21.cloned.1.call-start = ((), (), s32[]{:S(2)}) async-start(), calls=%async_computation.12 | async-start | bytes 7077888 | tf_op jit(solution)/shard_map/all_gather | solution.py:242
  267.4 326.1 %all-gather.23.cloned.1.call-start = ((), (), s32[]{:S(2)}) async-start(), calls=%async_computation.13 | async-start | bytes 1671168 | tf_op jit(solution)/shard_map/all_gather | solution.py:327
  459.7 133.8 %all-gather.25.cloned.1.call-start = ((), (), s32[]{:S(2)}) async-start(), calls=%async_computation.14 | async-start | bytes 1671168 | tf_op jit(solution)/shard_map/all_gather | solution.py:328
  461.5 205.5 %reduce-scatter.13.cloned.1.call-start = ((), (), s32[]{:S(2)}) async-start(), calls=%async_computation.16 | async-start | bytes 7077888 | tf_op jit(solution)/shard_map/reduce_scatter | solution.py:255
  466.5 210.2 %reduce-scatter.17.cloned.1.call-start = ((), (), s32[]{:S(2)}) async-start(), calls=%async_computation.18 | async-start | bytes 7077888 | tf_op jit(solution)/shard_map/reduce_scatter | solution.py:258
  472.0 249.8 %reduce-scatter.11.cloned.1.call-start = ((), (), s32[]{:S(2)}) async-start(), calls=%async_computation.15 | async-start | bytes 589824 | tf_op jit(solution)/shard_map/reduce_scatter | solution.py:394
  494.9 53.2 %collective-permute-start.13 = (bf16[256,2,6,64]{0,3,2,1:T(8,128)(2,1)}, bf16[256,2,6,64]{0,3,2,1:T(8,128)(2,1)}, u32[]{:S(2)}, u32[]{:S(2)}) collective-permute-start(bf16[256,2,6,64]{0,3,2,1:T(8,128)(2,1)} %get-tuple-element.796), channel_id=1, source_target_pairs={{14,0},{16,2},{18,4},{20,6},{22,8},{24,10},{26,12},{28,14},{30,16}... | collective-permute-start | bytes 1179656 | tf_op jit(solution)/shard_map/ppermute | solution.py:20
  496.2 53.2 %collective-permute-start.12 = (bf16[256,2,6,64]{0,3,2,1:T(8,128)(2,1)}, bf16[256,2,6,64]{0,3,2,1:T(8,128)(2,1)}, u32[]{:S(2)}, u32[]{:S(2)}) collective-permute-start(bf16[256,2,6,64]{0,3,2,1:T(8,128)(2,1)} %get-tuple-element.797), channel_id=1, source_target_pairs={{12,0},{14,2},{16,4},{18,6},{20,8},{22,10},{24,12},{26,14},{28,16}... | collective-permute-start | bytes 1179656 | tf_op jit(solution)/shard_map/ppermute | solution.py:20
  497.5 88.8 %collective-permute-start.11 = (bf16[256,2,6,64]{0,3,2,1:T(8,128)(2,1)}, bf16[256,2,6,64]{0,3,2,1:T(8,128)(2,1)}, u32[]{:S(2)}, u32[]{:S(2)}) collective-permute-start(bf16[256,2,6,64]{0,3,2,1:T(8,128)(2,1)} %get-tuple-element.798), channel_id=1, source_target_pairs={{10,0},{12,2},{14,4},{16,6},{18,8},{20,10},{22,12},{24,14},{26,16}... | collective-permute-start | bytes 1179656 | tf_op jit(solution)/shard_map/ppermute | solution.py:20
  498.8 87.5 %collective-permute-start.10 = (bf16[256,2,6,64]{0,3,2,1:T(8,128)(2,1)}, bf16[256,2,6,64]{0,3,2,1:T(8,128)(2,1)}, u32[]{:S(2)}, u32[]{:S(2)}) collective-permute-start(bf16[256,2,6,64]{0,3,2,1:T(8,128)(2,1)} %get-tuple-element.799), channel_id=1, source_target_pairs={{8,0},{10,2},{12,4},{14,6},{16,8},{18,10},{20,12},{22,14},{24,16},... | collective-permute-start | bytes 1179656 | tf_op jit(solution)/shard_map/ppermute | solution.py:20
  500.1 86.2 %collective-permute-start.9 = (bf16[256,2,6,64]{0,3,2,1:T(8,128)(2,1)}, bf16[256,2,6,64]{0,3,2,1:T(8,128)(2,1)}, u32[]{:S(2)}, u32[]{:S(2)}) collective-permute-start(bf16[256,2,6,64]{0,3,2,1:T(8,128)(2,1)} %get-tuple-element.800), channel_id=1, source_target_pairs={{6,0},{8,2},{10,4},{12,6},{14,8},{16,10},{18,12},{20,14},{22,16},{... | collective-permute-start | bytes 1179656 | tf_op jit(solution)/shard_map/ppermute | solution.py:20
  548.1 38.2 %collective-permute-start.8 = (bf16[256,2,6,64]{0,3,2,1:T(8,128)(2,1)}, bf16[256,2,6,64]{0,3,2,1:T(8,128)(2,1)}, u32[]{:S(2)}, u32[]{:S(2)}) collective-permute-start(bf16[256,2,6,64]{0,3,2,1:T(8,128)(2,1)} %get-tuple-element.801), channel_id=1, source_target_pairs={{4,0},{6,2},{8,4},{10,6},{12,8},{14,10},{16,12},{18,14},{20,16},{2... | collective-permute-start | bytes 1179656 | tf_op jit(solution)/shard_map/ppermute | solution.py:20
  549.4 36.9 %collective-permute-start.7 = (bf16[256,2,6,64]{0,3,2,1:T(8,128)(2,1)}, bf16[256,2,6,64]{0,3,2,1:T(8,128)(2,1)}, u32[]{:S(2)}, u32[]{:S(2)}) collective-permute-start(bf16[256,2,6,64]{0,3,2,1:T(8,128)(2,1)} %get-tuple-element.795), channel_id=1, source_target_pairs={{2,0},{4,2},{6,4},{8,6},{10,8},{12,10},{14,12},{16,14},{18,16},{20... | collective-permute-start | bytes 1179656 | tf_op jit(solution)/shard_map/ppermute | solution.py:20
  660.7 153.4 %all-reduce.4.cloned.1.call-start = ((), (), s32[]{:S(2)}) async-start(), calls=%async_computation.20 | async-start | bytes 9437184 | tf_op jit(solution)/shard_map/psum | solution.py:403
  666.9 226.8 %reduce-scatter.15.cloned.1.call-start = ((), (), s32[]{:S(2)}) async-start(), calls=%async_computation.17 | async-start | bytes 5013504 | tf_op jit(solution)/shard_map/reduce_scatter | solution.py:265
  671.5 301.7 %reduce-scatter.19.cloned.1.call-start = ((), (), s32[]{:S(2)}) async-start(), calls=%async_computation.19 | async-start | bytes 5013504
  (96 other events, 1717.1 us)
Sparse Core Ops, SparseCore 0:
  26.2 43.9 all-gather.10
  72.4 40.3 all-gather.12
  115.1 60.0 all-gather.14
  177.3 43.0 all-gather.18
  266.2 41.1 reduce-scatter.8
  308.9 62.6 all-gather.16
  373.2 62.6 all-gather.20
  459.8 38.9 all-gather.22
  501.2 51.8 all-gather.24
  555.4 58.9 reduce-scatter.12
  616.7 59.9 reduce-scatter.16
  678.9 13.1 reduce-scatter.10
  696.4 117.6 all-reduce.3
  818.3 75.3 reduce-scatter.14
  898.5 74.5 reduce-scatter.18
where the time goes:
time: 994 us; the launch traced here: 985 us
  waiting for transfers between devices  381 us (38%)
  matrix products  175 us (18%)
  blocking collectives  163 us (16%)
  other arithmetic  114 us (11%)
  local copies, waits for them, and re-layouts  93.1 us (9%)
  starting transfers between devices  41.4 us (4%)
  between operations  16.5 us (2%)
    unnamed x16, waiting for transfers between devices  81.4 us
    reduce_scatter x1, waiting for transfers between devices, per_device(): lax.psum_scatter(up_grad, 'seq', scatter_dimension=0, tiled=True)  79.7 us
    dot_general x4, matrix products, block_terms(): jnp.einsum('qhe,khe->hqk', query_blk, key_blk, preferred_element_type=jnp...  63.7 us
    all_gather x1, waiting for transfers between devices, per_device(): lax.all_gather(up_rows, 'head', axis=1, tiled=True)  61.4 us
    all_gather x1, waiting for transfers between devices, per_device(): lax.all_gather(down_rows, 'head', axis=0, tiled=True)  61.1 us
    psum x1, waiting for transfers between devices, per_device(): lax.psum((w_qkv_part, bias_qv_part, w_out_part), 'seq')  48.7 us
    ppermute x14, starting transfers between devices, from_behind(): return lax.ppermute(value, axis, pairs)  40.2 us
    psum x1, blocking collectives, per_device(): lax.psum((gain_one_grad, bias_one_grad, gain_two_grad, bias_two_grad, bia...  38.5 us
  transfers between devices with their start and end apart: 29, of which 8 were waited for; matrix products, arithmetic and copies ran while one was open for 34% of the time, Pallas kernels for 0%

commit v1 on v0

--- a/solution.py
+++ b/solution.py
@@ -1,6 +1,12 @@
+import functools
+
 import jax
 import jax.numpy as jnp
+import ml_dtypes
+import numpy as np
 from jax import lax
+from jax.experimental import pallas as pl
+from jax.experimental.pallas import tpu as pltpu
 from jax.sharding import PartitionSpec as P
 
 HEADS = 12
@@ -12,6 +18,865 @@
 EPS = 1e-05
 NEGATIVE = -1e30
 block_limit = 2048
+TOKENS = 4096
+
+
+MESH = pl.DeviceIdType.MESH
+VMEM = pltpu.VMEM
+LIMIT = 58 << 20
+F32 = jnp.float32
+B16 = jnp.bfloat16
+
+
+def dot(a, b):
+    return jnp.dot(a, b, preferred_element_type=F32)
+
+
+def dot_nt(a, b):
+    return lax.dot_general(a, b, (((1,), (1,)), ((), ())), preferred_element_type=F32)
+
+
+def sid(z, x, c):
+    return z * 4 + x * 2 + c
+
+
+class Place:
+    def __init__(self):
+        s = lax.axis_index("seq")
+        self.s, self.y = s, lax.axis_index("head")
+        self.z, self.x, self.c = s // 4, (s // 2) % 2, s % 2
+        self.seg, self.zl = self.z // 2, self.z % 2
+        self.u = s % 8
+        self.b = self.u * 2 + self.y
+        self.unit = jnp.logical_and(self.u != 3, self.u != 5)
+        self.hl = self.u - self.u // 4 - self.u // 6
+        self.head = self.y * 6 + self.hl
+        self.parity = self.head % 2
+        z, x, c, y = self.z, self.x, self.c, self.y
+        self.zf = z + 1 - 2 * self.zl
+        self.nx, self.ny = (sid(z, 1 - x, c), y), (s, 1 - y)
+        self.nz, self.nc = (sid(self.zf, x, c), y), (sid(z, x, 1 - c), y)
+        self.far = (sid((z + 2) % 4, x, c), y)
+        self.fb = {"x": 4 * (1 - 2 * x), "y": 1 - 2 * y, "z": 8 * (1 - 2 * self.zl), "c": 2 * (1 - 2 * c)}
+
+    def cube(self):
+        z, x, c, y = self.z, self.x, self.c, self.y
+        for k in range(1, 16):
+            zz = self.zf if k & 8 else z
+            xx = 1 - x if k & 4 else x
+            cc = 1 - c if k & 2 else c
+            yy = 1 - y if k & 1 else y
+            yield (sid(zz, xx, cc), yy)
+
+    def greet(self):
+        others = list(self.cube())
+        others += [(sid((self.z + 2) % 4, self.x, self.c), self.y), (sid((self.zf + 2) % 4, self.x, self.c), self.y)]
+        barrier = pltpu.get_barrier_semaphore()
+        for dev in others:
+            pl.semaphore_signal(barrier, inc=1, device_id=dev, device_id_type=MESH)
+        pl.semaphore_wait(barrier, len(others))
+
+
+class Mail:
+    def __init__(self, sems):
+        self.sems, self.used, self.sent = sems, 0, []
+
+    def send(self, src, dst, rsem, dev, cond=None):
+        k = self.used
+        self.used += 1
+
+        def make():
+            return pltpu.make_async_remote_copy(
+                src_ref=src, dst_ref=dst, send_sem=self.sems.at[k], recv_sem=rsem, device_id=dev, device_id_type=MESH
+            )
+
+        if cond is None:
+            make().start()
+        else:
+            pl.when(cond)(lambda: make().start())
+        self.sent.append((cond, make))
+
+    def got(self, dst, rsem, dev):
+        pltpu.make_async_remote_copy(
+            src_ref=dst, dst_ref=dst, send_sem=self.sems.at[0], recv_sem=rsem, device_id=dev, device_id_type=MESH
+        ).wait_recv()
+
+    def close(self):
+        for cond, make in self.sent:
+            if cond is None:
+                make().wait_send()
+            else:
+                pl.when(cond)(lambda make=make: make().wait_send())
+
+
+def both(*terms):
+    out = terms[0]
+    for term in terms[1:]:
+        out = jnp.logical_and(out, term)
+    return out
+
+
+def iota(shape, dim):
+    return lax.broadcasted_iota(jnp.int32, shape, dim)
+
+
+def norm_parts(v):
+    mean = jnp.mean(v, axis=-1, keepdims=True)
+    cen = v - mean
+    inv = lax.rsqrt(jnp.mean(cen * cen, axis=-1, keepdims=True) + EPS)
+    return cen * inv, inv
+
+
+def norm_grad(z, inv, e):
+    return (e - jnp.mean(e, axis=-1, keepdims=True) - z * jnp.mean(e * z, axis=-1, keepdims=True)) * inv
+
+
+def pick_type(pos, head, rows):
+    v = pos - head + 24.0
+    m = v - 12.0 * jnp.floor((v + 0.5) * (1.0 / 12.0))
+    out = jnp.where(m == 0.0, rows[4], rows[0])
+    out = jnp.where(m == 6.0, rows[3], out)
+    out = jnp.where(jnp.logical_or(m == 4.0, m == 8.0), rows[2], out)
+    return jnp.where(jnp.logical_or(m == 2.0, m == 10.0), rows[1], out)
+
+
+def halves(e, o):
+    low = iota(e.shape, 1) < 64
+    return jnp.where(low, e, pltpu.roll(o, 64, 1)), jnp.where(low, pltpu.roll(e, 64, 1), o)
+
+
+def tile_mask(st, c, seg, parity, tq, par, start):
+    rr = iota((512, 256), 0)
+    near = (c - 2) * 512 + seg * SEG + 2 * (rr & 255) + (rr >> 8)
+    far = c * 1024 + 2 * rr + parity
+    kpos = near + jnp.asarray(c < 2, jnp.int32) * (far - near)
+    qpos = seg * SEG + tq * 512 + 2 * iota((512, 256), 1) + par
+    return both(kpos <= qpos, kpos.astype(F32) >= start)
+
+
+def kernel_one(
+    x_ref, dy_ref, doc_ref, wq_ref, bq_ref, g1_ref, b1_ref, wo_own, bo_ref, g2_ref, b2_ref, wud_ref, bup_ref, bd_ref, tab_ref,
+    qa, ka, va, ns, lse, ot, strow, dpk, grads, dh_out, lout, sums, supg,
+    xs, docs, wb, wo, dyp, orecv, osend, kvs, kvf, attn, vt, hid, n2s, dys, acts, dpre, facc, dacc, ys, yr, fs, fr, fo,
+    ss, rsx, rsc, rsd, rsw, rso, rsf, rsy,
+):
+    p = Place()
+    mail = Mail(ss)
+    seg, y, b, hl = p.seg, p.y, p.b, p.hl
+    p.greet()
+
+    dims = ("x", "y", "z")
+    nbr = {"x": p.nx, "y": p.ny, "z": p.nz}
+    part = [pl.ds(k * 256, 256) for k in range(3)]
+    xs[b] = x_ref[...]
+    docs[b] = doc_ref[...]
+    order = [[dims[(k + j) % 3] for j in range(3)] for k in range(3)]
+
+    def pass_on(k, blk, dev):
+        ref = xs.at[blk, :, part[k]]
+        mail.send(ref, ref, rsx.at[k, blk], dev)
+
+    def to_core(k, blk):
+        ref = xs.at[blk, :, part[k]]
+        mail.send(ref, ref, rsc.at[k, blk], p.nc)
+
+    for j in range(3):
+        for k in range(3):
+            pass_on(k, b, nbr[order[k][j]])
+    for k in range(3):
+        to_core(k, b)
+    for src in (0, 14, 15):
+        for dev in p.cube():
+            mail.send(docs.at[src], docs.at[src], rsd.at[src], dev, cond=b == src)
+
+    head = p.head.astype(F32)
+    for t in range(4):
+        rr = iota((512, 128), 0)
+        pos = (seg * SEG + t * 512 + 2 * (rr & 255) + (rr >> 8)).astype(F32)
+        qa[t] = pick_type(pos, head, [tab_ref[i : i + 1] for i in range(5)]).astype(B16)
+        ka[t + 2] = pick_type(pos, head, [tab_ref[8 + i : 9 + i] for i in range(5)]).astype(B16)
+
+    def seen(k, blk):
+        mail.got(xs.at[blk, :, part[k]], rsx.at[k, blk], p.nx)
+        to_core(k, blk)
+
+    for k in range(3):
+        f = [p.fb[d] for d in order[k]]
+        seen(k, b + f[0])
+        pass_on(k, b + f[0], nbr[order[k][1]])
+        pass_on(k, b + f[0], nbr[order[k][2]])
+    for k in range(3):
+        f = [p.fb[d] for d in order[k]]
+        for blk in (b + f[1], b + f[1] + f[0]):
+            seen(k, blk)
+            pass_on(k, blk, nbr[order[k][2]])
+
+    def rows_of(s):
+        return wb.at[pl.ds(pl.multiple_of(s * 48, 16), 48), :]
+
+    wb[pl.ds(pl.multiple_of(p.s * 48, 16), 48), :] = wud_ref[...]
+
+    def give(s, dev, cond=None):
+        mail.send(rows_of(s), rows_of(s), rsw.at[s], dev, cond)
+
+    z, x, c = p.z, p.x, p.c
+    give(p.s, (sid((z + 1) % 4, x, c), y), z <= 2)
+    give(p.s, (sid((z + 3) % 4, x, c), y), z >= 1)
+    give(p.s, p.nx)
+    give(p.s, p.nc)
+    wo[y] = wo_own[...]
+    mail.send(wo.at[y], wo.at[y], rsy.at[0], p.ny)
+    dyp[y] = dy_ref[...]
+    mail.send(dyp.at[y], dyp.at[y], rsy.at[1], p.ny)
+
+    def chain(d):
+        up, dn = (z - d + 4) % 4, (z + d) % 4
+        has_up, has_dn = z >= d, z <= 3 - d
+        su, sd = sid(up, x, c), sid(dn, x, c)
+        pl.when(has_up)(lambda: mail.got(rows_of(su), rsw.at[su], p.nx))
+        if d < 3:
+            give(su, (sid((z + 1) % 4, x, c), y), both(has_up, z <= 2))
+        give(su, p.nx, has_up)
+        give(su, p.nc, has_up)
+        pl.when(has_dn)(lambda: mail.got(rows_of(sd), rsw.at[sd], p.nx))
+        if d < 3:
+            give(sd, (sid((z + 3) % 4, x, c), y), both(has_dn, z >= 1))
+        give(sd, p.nx, has_dn)
+        give(sd, p.nc, has_dn)
+
+    for k in range(3):
+        f = [p.fb[d] for d in order[k]]
+        for blk in (b + f[2], b + f[2] + f[0], b + f[2] + f[1], b + f[2] + f[1] + f[0]):
+            seen(k, blk)
+    for i in range(8):
+        blk = (i // 4) * 8 + ((i // 2) % 2) * 4 + (1 - c) * 2 + i % 2
+        for k in range(3):
+            mail.got(xs.at[blk, :, part[k]], rsc.at[k, blk], p.nc)
+    for src in (0, 14, 15):
+        pl.when(b != src)(lambda src=src: mail.got(docs.at[src], rsd.at[src], p.nx))
+
+    def qkv_step(i, _):
+        rows = xs[pl.ds(2 * i, 2)].reshape(256, 768).astype(F32)
+        zz, _inv = norm_parts(rows)
+        n1 = (zz * g1_ref[...] + b1_ref[...]).astype(B16)
+        mix = (dot(n1, wq_ref[...]) + bq_ref[...]).astype(B16)
+        t = i // 2
+        for yy in range(2):
+            for par in range(2):
+                at = yy * 128 + par * 64
+                to = pl.ds(pl.multiple_of(par * 256 + (i % 2) * 128 + yy * 64, 64), 64)
+                m = mix[at : at + 64]
+                qa[t, to] = m[:, :128] * B16(0.125) + qa[t, to]
+                ka[t + 2, to] = m[:, 128:256] + ka[t + 2, to]
+                va[t + 2, to] = m[:, 256:]
+                ns[t, to] = n1[at : at + 64]
+        return 0
+
+    @pl.when(p.unit)
+    def _():
+        lax.fori_loop(0, 8, qkv_step, 0)
+
+    lowlane = iota((256, 128), 1) < 64
+    first = both(p.unit, seg == 0)
+    second = both(p.unit, seg == 1)
+    farrows = pl.ds(pl.multiple_of(p.parity * 256, 256), 256)
+
+    @pl.when(first)
+    def _():
+        for t in range(4):
+            kk = ka[t + 2, farrows].astype(F32)
+            vv = va[t + 2, farrows].astype(F32)
+            kvs[t] = jnp.where(lowlane, kk, pltpu.roll(vv, 64, 1)).astype(B16)
+
+    mail.send(kvs, kvf, rsf.at[0], p.far, first)
+    mail.send(docs.at[0], docs.at[16], rsf.at[1], p.far, first)
+    chain(1)
+
+    lane = iota((1, 128), 1)
+    lane64 = lane < 64
+
+    def code(row):
+        return jnp.where(row < 0.0, 4.0, row)
+
+    def count(rows, level):
+        lim = iota((2, 128), 1) < 64
+        hit = jnp.where(both(lim, code(rows) < level), 1.0, 0.0)
+        return jnp.sum(jnp.sum(hit, axis=1, keepdims=True), axis=0, keepdims=True)
+
+    @pl.when(second)
+    def _():
+        mail.got(docs.at[16], rsf.at[1], p.far)
+
+    pl.when(jnp.logical_not(second))(lambda: docs.__setitem__(16, docs[0]))
+    d0, da, db = docs[16][0:2], docs[14][0:2], docs[15][0:2]
+    n1c, n2c = count(d0, 1.0), count(d0, 2.0)
+    tail = float(TOKENS - 256)
+    t3 = count(da, 3.0) + count(db, 3.0) + tail
+    t4 = count(da, 4.0) + count(db, 4.0) + tail
+
+    def start_of(row):
+        k = code(row)
+        out = jnp.where(k == 1.0, n1c, 0.0)
+        out = jnp.where(k == 2.0, n2c, out)
+        out = jnp.where(k == 3.0, t3, out)
+        return jnp.where(k == 4.0, t4, out)
+
+    two = jnp.full((1, 128), 2.0, F32)
+    segf = seg.astype(F32)
+    for j in range(8):
+        t, par = j // 2, j % 2
+        ra, rb = two, two
+        if t == 0:
+            ra = jnp.where(lane64, 2.0 + (1.0 - segf) * (d0[par : par + 1] - 2.0), 2.0)
+        if t == 3:
+            last = jnp.where(lane64, da[par : par + 1], db[par : par + 1])
+            rb = 2.0 + segf * (last - 2.0)
+        strow[j] = jnp.concatenate([start_of(ra), start_of(rb)], axis=1)
+
+    @pl.when(p.unit)
+    def _():
+        for t in range(4):
+            vt[t + 2] = va[t + 2].astype(F32).T.astype(B16)
+
+    def far_ready():
+        mail.got(kvf, rsf.at[0], p.far)
+        for t in range(4):
+            rows = pl.ds((t % 2) * 256, 256)
+            fpos = ((t * 256 + iota((256, 128), 0)) * 2 + p.parity).astype(F32)
+            feat = pick_type(fpos, head, [tab_ref[16 + i : 17 + i] for i in range(5)])
+            kv = kvf[t].astype(F32)
+            ka[t // 2, rows] = jnp.where(lowlane, kv, feat).astype(B16)
+            one = jnp.where(iota((256, 128), 1) == 64, 1.0, 0.0)
+            vv = jnp.where(lowlane, pltpu.roll(kv, 64, 1), one)
+            va[t // 2, rows] = vv.astype(B16)
+        for h in range(2):
+            vt[h] = va[h].astype(F32).T.astype(B16)
+
+    pl.when(second)(far_ready)
+
+    def attend(t):
+        for par in range(2):
+            q = qa[t, par * 256 : par * 256 + 256]
+            begin = jnp.where(both(seg == 1, p.parity == par), 0, 2)
+
+            def step(cc, carry):
+                m, acc = carry
+                st = dot_nt(ka[cc], q)
+                st = jnp.where(tile_mask(st, cc, seg, p.parity, t, par, strow[2 * t + par]), st, NEGATIVE)
+                m_new = jnp.maximum(m, jnp.max(st, axis=0, keepdims=True))
+                pr = jnp.exp(st - m_new).astype(B16)
+                return m_new, acc * jnp.exp(m - m_new) + dot(vt[cc], pr)
+
+            m, acc = lax.fori_loop(begin, t + 3, step, (jnp.full((1, 256), NEGATIVE, F32), jnp.zeros((128, 256), F32)))
+            total = acc[64:65]
+            ot[t, par * 64 : par * 64 + 64] = acc[:64] / total
+            lse[2 * t + par] = m + jnp.log(total)
+        osend[t] = ot[t].T.astype(B16)
+
+    for t in range(4):
+        pl.when(p.unit)(functools.partial(attend, t))
+        zz, xx = seg * 2 + t // 2, t % 2
+        for cc in range(2):
+            for yy in range(2):
+                own = both(p.u == t * 2 + cc, y == yy)
+                src = osend.at[t, cc * 128 : cc * 128 + 128]
+                mail.send(src, orecv.at[p.head], rso.at[p.head], (sid(zz, xx, cc), yy), both(p.unit, jnp.logical_not(own)))
+
+                @pl.when(both(p.unit, own))
+                def _(t=t, cc=cc):
+                    orecv[p.head] = osend[t, cc * 128 : cc * 128 + 128]
+
+        if t == 1:
+            chain(2)
+    chain(3)
+    for zq in range(4):
+        s = sid(zq, 1 - x, c)
+        mail.got(rows_of(s), rsw.at[s], p.nx)
+        give(s, p.nc)
+
+    for hh in range(12):
+        mine = both(p.unit, p.head == hh)
+        pl.when(jnp.logical_not(mine))(lambda hh=hh: mail.got(orecv.at[hh], rso.at[hh], p.nx))
+    for a in range(6):
+        e, o = halves(orecv[2 * a].astype(F32), orecv[2 * a + 1].astype(F32))
+        attn[0:128, a * 128 : a * 128 + 128] = e.astype(B16)
+        attn[128:256, a * 128 : a * 128 + 128] = o.astype(B16)
+    mail.got(wo.at[1 - y], rsy.at[0], p.ny)
+    mail.got(dyp.at[1 - y], rsy.at[1], p.ny)
+    pair = pl.multiple_of(p.u * 2, 2)
+    for par in range(2):
+        for yy in range(2):
+            at = pl.ds(par * 128 + yy * 64, 64)
+            hid[at] = xs[pair + yy, par * 64 : par * 64 + 64].astype(F32)
+            dys[at] = dyp[yy, par * 64 : par * 64 + 64]
+    hid[...] = hid[...] + dot(attn[...], wo[...].reshape(768, 768)) + bo_ref[...]
+    z2, _inv = norm_parts(hid[...])
+    n2s[...] = (z2 * g2_ref[...] + b2_ref[...]).astype(B16)
+    for i in range(8):
+        s = sid(i // 2, i % 2, 1 - c)
+        mail.got(rows_of(s), rsw.at[s], p.nc)
+
+    facc[...] = jnp.zeros_like(facc)
+    dacc[...] = jnp.zeros_like(dacc)
+    k0 = 0.7978845608028654
+
+    def ffn_step(i, _):
+        cols = pl.ds(pl.multiple_of(i * 256, 256), 256)
+        dcols = pl.ds(pl.multiple_of(1536 + i * 256, 256), 256)
+        up, dn = wb[:, cols], wb[:, dcols]
+        pre = dot(n2s[...], up) + bup_ref[:, cols]
+        sq = pre * pre
+        th = jnp.tanh(k0 * pre * (1.0 + 0.044715 * sq))
+        half = 0.5 * (1.0 + th)
+        act = (pre * half).astype(B16)
+        slope = half + 0.5 * pre * (1.0 - th * th) * (k0 * (1.0 + 3.0 * 0.044715 * sq))
+        dp = dot(dys[...], dn) * slope
+        supg[:, cols] = jnp.broadcast_to(jnp.sum(dp, axis=0, keepdims=True), (8, 256))
+        dpl = dp.astype(B16)
+        acts[:, cols] = act
+        dpre[:, cols] = dpl
+        facc[...] += dot_nt(act, dn)
+        dacc[...] += dot_nt(dpl, up)
+        return 0
+
+    lax.fori_loop(0, 6, ffn_step, 0)
+    ys[...] = dacc[...].astype(B16)
+    mail.send(ys, yr, rsy.at[2], p.ny)
+    for par in range(2):
+        fo[par * 64 : par * 64 + 64] = facc[pl.ds(pl.multiple_of(par * 128 + y * 64, 64), 64)]
+        fs[par * 64 : par * 64 + 64] = facc[pl.ds(pl.multiple_of(par * 128 + (1 - y) * 64, 64), 64)].astype(B16)
+    mail.send(fs, fr, rsy.at[3], p.ny)
+
+    n2t = n2s[...].astype(F32).T.astype(B16)
+    dyt = dys[...].astype(F32).T.astype(B16)
+
+    def grad_step(i, _):
+        cols = pl.ds(pl.multiple_of(i * 256, 256), 256)
+        dcols = pl.ds(pl.multiple_of(1536 + i * 256, 256), 256)
+        grads[:, cols] = dot(n2t, dpre[:, cols]).astype(B16)
+        grads[:, dcols] = dot(dyt, acts[:, cols]).astype(B16)
+        return 0
+
+    lax.fori_loop(0, 6, grad_step, 0)
+    mail.got(yr, rsy.at[2], p.ny)
+    dn2 = ys[...].astype(F32) + yr[...].astype(F32)
+    z2, inv2 = norm_parts(hid[...])
+    dyf = dys[...].astype(F32)
+    dh = dyf + norm_grad(z2, inv2, dn2 * g2_ref[...])
+    facc[...] = dh
+    dacc[...] = dn2 * z2
+    dhl = dh.astype(B16)
+    da_ = dot_nt(dhl, wo[y])
+    for a in range(3):
+        e, o = halves(da_[0:128, a * 128 : a * 128 + 128], da_[128:256, a * 128 : a * 128 + 128])
+        dpk[2 * a] = e.astype(B16)
+        dpk[2 * a + 1] = o.astype(B16)
+    grads[:, 3072:3456] = dot(dh.T.astype(B16), attn[:, pl.ds(pl.multiple_of(y * 384, 128), 384)]).astype(B16)
+    mail.got(fr, rsy.at[3], p.ny)
+    total = [jnp.zeros((1, 768), F32)] * 4
+    for par in range(2):
+        at = pl.ds(pl.multiple_of(par * 128 + y * 64, 64), 64)
+        to = slice(par * 64, par * 64 + 64)
+        dh_out[to] = facc[at]
+        own = (ys[at].astype(F32) + yr[at].astype(F32), dys[at].astype(F32))
+        total[0] = total[0] + jnp.sum(dacc[at], axis=0, keepdims=True)
+        total[1] = total[1] + jnp.sum(own[0], axis=0, keepdims=True)
+        total[2] = total[2] + jnp.sum(facc[at], axis=0, keepdims=True)
+        total[3] = total[3] + jnp.sum(own[1], axis=0, keepdims=True)
+        lout[to] = (hid[at] + fo[to] + fr[to].astype(F32) + bd_ref[...]).astype(B16)
+    for i in range(4):
+        sums[i : i + 1] = total[i]
+    mail.close()
+
+
+UNITS = (0, 1, 2, 4, 6, 7)
+
+
+class Spread:
+    def __init__(self, p, mail, ref, sems, some):
+        self.p, self.mail, self.ref, self.sems, self.some = p, mail, ref, sems, some
+
+    def has(self, zz, xx, cc):
+        return jnp.logical_or(cc == 0, zz % 2 == xx) if self.some else None
+
+    def go(self, s, dev, cond):
+        self.mail.send(self.ref.at[s], self.ref.at[s], self.sems.at[s], dev, cond)
+
+    def take(self, s, cond):
+        def wait():
+            self.mail.got(self.ref.at[s], self.sems.at[s], self.p.nx)
+
+        if cond is None:
+            wait()
+        else:
+            pl.when(cond)(wait)
+
+    def first(self):
+        p = self.p
+        has = self.has(p.z, p.x, p.c)
+        for k in range(1, 4):
+            self.go(p.s, (sid((p.z + k) % 4, p.x, p.c), p.y), has)
+        self.go(p.s, p.nx, has)
+        self.go(p.s, p.nc, has)
+
+    def second(self):
+        p = self.p
+        for k in range(1, 4):
+            zz = (p.z + k) % 4
+            s, has = sid(zz, p.x, p.c), self.has(zz, p.x, p.c)
+            self.take(s, has)
+            self.go(s, p.nx, has)
+            self.go(s, p.nc, has)
+
+    def third(self):
+        p = self.p
+        for zz in range(4):
+            s, has = sid(zz, 1 - p.x, p.c), self.has(zz, 1 - p.x, p.c)
+            self.take(s, has)
+            self.go(s, p.nc, has)
+
+    def last(self):
+        p = self.p
+        for zz in range(4):
+            for xx in range(2):
+                self.take(sid(zz, xx, 1 - p.c), self.has(zz, xx, 1 - p.c))
+
+
+def kernel_two(
+    qa, ka, va, ns, lse, ot, strow, dpk, grads, dh, sums, supg, xp, g1_ref, wq_ref,
+    gin, wud, wag, woag, vec,
+    dor, doa, delta, kt, dka, dva, dqt, dtt, dfs, dfr, packs, dqr, wms, wmr, gc, gxs, gxr, gzs, gzr, dall, dn, dns, dnr, vbuf, vrec,
+    ss, rdo, rgc, rgx, rgz, rdf, rdq, rwm, rag, rwo, rdn, rvec,
+):
+    p = Place()
+    mail = Mail(ss)
+    seg, y, x, z, c = p.seg, p.y, p.x, p.z, p.c
+    first, second = both(p.unit, seg == 0), both(p.unit, seg == 1)
+    p.greet()
+    mine_t = p.zl * 2 + x
+    crow = pl.ds(pl.multiple_of(c * 128, 128), 128)
+
+    for h, u in enumerate(UNITS):
+        spot = dor.at[mine_t, crow]
+        mail.send(dpk.at[h], spot, rdo.at[p.u], (seg * 8 + u, y), p.u != u)
+
+        @pl.when(p.u == u)
+        def _(h=h):
+            dor[mine_t, crow] = dpk[h]
+
+    def block(s):
+        return pl.ds(pl.multiple_of(s * 48, 16), 48)
+
+    for xq in range(2):
+        xx = 1 - x if xq == 0 else x
+        for zz in range(4):
+            mail.send(grads.at[block(sid(zz, xx, 1 - c))], gc.at[xq, zz], rgc.at[xq, zz], p.nc)
+
+    def prepare():
+        for i in range(8):
+            pl.when(p.u != i)(lambda i=i: mail.got(dor.at[i // 2, (i % 2) * 128 : (i % 2) * 128 + 128], rdo.at[i], p.nx))
+        low = iota((256, 128), 1) < 64
+        for t in range(4):
+            d = dor[t].astype(F32)
+            doa[2 * t] = jnp.where(low, d, 0.0).astype(B16)
+            doa[2 * t + 1] = jnp.where(low, pltpu.roll(d, 64, 1), 0.0).astype(B16)
+            prod = d.T * ot[t]
+            delta[2 * t] = jnp.sum(prod[:64], axis=0, keepdims=True)
+            delta[2 * t + 1] = jnp.sum(prod[64:], axis=0, keepdims=True)
+            kt[t + 2] = ka[t + 2].astype(F32).T.astype(B16)
+        dqt[...] = jnp.zeros_like(dqt)
+
+    pl.when(p.unit)(prepare)
+
+    def pair(cc, j):
+        t, par = j // 2, j % 2
+        q = qa[t, pl.ds(pl.multiple_of(par * 256, 256), 256)]
+        st = dot_nt(ka[cc], q)
+        st = jnp.where(tile_mask(st, cc, seg, p.parity, t, par, strow[j]), st, NEGATIVE)
+        pr = jnp.exp(st - lse[j])
+        do = doa[j]
+        ds = (pr * (dot_nt(va[cc], do) - delta[j])).astype(B16)
+        dva[...] += dot(pr.astype(B16), do)
+        dka[...] += dot(ds, q)
+        dqt[j] += dot(kt[cc], ds)
+
+    def clear():
+        dka[...] = jnp.zeros_like(dka)
+        dva[...] = jnp.zeros_like(dva)
+
+    @pl.when(second)
+    def _():
+        for h in range(2):
+            kt[h] = ka[h].astype(F32).T.astype(B16)
+
+        def chunk(cc, _):
+            clear()
+
+            def step(t, _):
+                pair(cc, 2 * t + p.parity)
+                return 0
+
+            lax.fori_loop(0, 4, step, 0)
+            low = iota((512, 128), 1) < 64
+            both_ = jnp.where(low, dka[...], pltpu.roll(dva[...], 64, 1)).astype(B16)
+            dfs[2 * cc] = both_[:256]
+            dfs[2 * cc + 1] = both_[256:]
+            return 0
+
+        lax.fori_loop(0, 2, chunk, 0)
+
+    mail.send(dfs, dfr, rdf.at[0], p.far, second)
+
+    def near(t):
+        clear()
+
+        def step(j, _):
+            pair(t + 2, j)
+            return 0
+
+        lax.fori_loop(2 * t, 8, step, 0)
+        dtt[64:128, t * 512 : t * 512 + 512] = dka[...].T[:64].astype(B16)
+        dtt[128:192, t * 512 : t * 512 + 512] = dva[...].T[:64].astype(B16)
+
+    def add_far(t):
+        rows = dfr[t].astype(F32).T.astype(F32)
+        at = pl.ds(pl.multiple_of(t * 512 + p.parity * 256, 256), 256)
+        dtt[64:128, at] = (dtt[64:128, at].astype(F32) + rows[:64]).astype(B16)
+        dtt[128:192, at] = (dtt[128:192, at].astype(F32) + rows[64:]).astype(B16)
+
+    for xq in range(2):
+        for zz in range(4):
+            mail.got(gc.at[xq, zz], rgc.at[xq, zz], p.nc)
+    for zz in range(4):
+        rows = block(sid(zz, 1 - x, c))
+        gxs[zz] = (grads[rows].astype(F32) + gc[0, zz].astype(F32)).astype(B16)
+        mail.send(gxs.at[zz], gxr.at[zz], rgx.at[zz], p.nx)
+    pl.when(p.unit)(lambda: near(0))
+
+    def column(zz):
+        mail.got(gxr.at[zz], rgx.at[zz], p.nx)
+        return grads[block(sid(zz, x, c))].astype(F32) + gc[1, zz].astype(F32) + gxr[zz].astype(F32)
+
+    for k in range(1, 4):
+        zz = (z + k) % 4
+        gzs[k] = column(zz).astype(B16)
+        mail.send(gzs.at[k], gzr.at[z], rgz.at[z], (sid(zz, x, c), y))
+    pl.when(p.unit)(lambda: near(1))
+    pl.when(p.unit)(lambda: near(2))
+    pl.when(p.unit)(lambda: near(3))
+
+    @pl.when(first)
+    def _():
+        mail.got(dfr, rdf.at[0], p.far)
+        for t in range(4):
+            add_far(t)
+
+    @pl.when(p.unit)
+    def _():
+        for j in range(8):
+            dtt[0:64, j * 256 : j * 256 + 256] = (dqt[j][:64] * 0.125).astype(B16)
+        for t in range(4):
+            for k in range(3):
+                e = dtt[k * 64 : k * 64 + 64, t * 512 : t * 512 + 256].astype(F32)
+                o = dtt[k * 64 : k * 64 + 64, t * 512 + 256 : t * 512 + 512].astype(F32)
+                packs[t, k] = jnp.concatenate([e, o], axis=0).T.astype(B16)
+
+    for t in range(4):
+        for cc in range(2):
+            src = packs.at[t, :, cc * 128 : cc * 128 + 128]
+            u = t * 2 + cc
+            mail.send(src, dqr.at[p.hl], rdq.at[p.hl], (seg * 8 + u, y), both(p.unit, p.u != u))
+
+            @pl.when(both(p.unit, p.u == u))
+            def _(t=t, cc=cc):
+                dqr[p.hl] = packs[t, :, cc * 128 : cc * 128 + 128]
+
+    spread = Spread(p, mail, wag, rag, True)
+
+    @pl.when(p.unit)
+    def _():
+        dw = dot(dtt[...], ns[...].reshape(2048, 768))
+        bias = dot_nt(jnp.ones((16, 2048), B16), dtt[...])
+        for h in range(2):
+            wms[h, 0:96] = dw[h * 96 : h * 96 + 96].astype(B16)
+            wms[h, 96:112, 0:192] = bias.astype(B16)
+            wms[h, 96:112, 192:768] = jnp.zeros((16, 576), B16)
+
+    mail.send(wms.at[1 - seg], wmr, rwm.at[0], p.far, p.unit)
+
+    total = column(z)
+    for k in range(1, 4):
+        zz = (z + k) % 4
+        mail.got(gzr.at[zz], rgz.at[zz], p.nx)
+        total = total + gzr[zz].astype(F32)
+    wud[...] = total[:, :3072]
+    woag[p.s] = total[:, 3072:].astype(B16)
+    spread_out = Spread(p, mail, woag, rwo, False)
+    spread_out.first()
+
+    @pl.when(p.unit)
+    def _():
+        mail.got(wmr, rwm.at[0], p.far)
+        wag[p.s] = (wms[seg].astype(F32) + wmr[...].astype(F32)).astype(B16)
+
+    spread.first()
+
+    for h, u in enumerate(UNITS):
+        pl.when(p.u != u)(lambda h=h: mail.got(dqr.at[h], rdq.at[h], p.nx))
+    for k in range(3):
+        for a in range(3):
+            e, o = halves(dqr[2 * a, k].astype(F32), dqr[2 * a + 1, k].astype(F32))
+            col = k * 384 + a * 128
+            dall[0:128, col : col + 128] = e.astype(B16)
+            dall[128:256, col : col + 128] = o.astype(B16)
+    dn[...] = dot_nt(dall[...], wq_ref[...])
+    for par in range(2):
+        dns[par * 64 : par * 64 + 64] = dn[pl.ds(pl.multiple_of(par * 128 + (1 - y) * 64, 64), 64)].astype(B16)
+    mail.send(dns, dnr, rdn.at[0], p.ny)
+    spread_out.second()
+    spread.second()
+    z1, inv1 = norm_parts(xp[...].astype(F32))
+    mail.got(dnr, rdn.at[0], p.ny)
+    own = [dn[pl.ds(pl.multiple_of(par * 128 + y * 64, 64), 64)] for par in range(2)]
+    dn1 = jnp.concatenate(own, axis=0) + dnr[...].astype(F32)
+    gin[...] = dh[...] + norm_grad(z1, inv1, dn1 * g1_ref[...])
+
+    vbuf[0] = jnp.zeros((16, 768), F32)
+    vbuf[0, 0:1] = jnp.sum(dn1 * z1, axis=0, keepdims=True)
+    vbuf[0, 1:2] = jnp.sum(dn1, axis=0, keepdims=True)
+    vbuf[0, 2:6] = sums[0:4]
+    vbuf[0, 6:7] = supg[0:1, 0:768] * (1.0 - y.astype(F32))
+    vbuf[0, 7:8] = supg[0:1, 768:1536] * (1.0 - y.astype(F32))
+    vbuf[0, 8:9] = supg[0:1, 0:768] * y.astype(F32)
+    vbuf[0, 9:10] = supg[0:1, 768:1536] * y.astype(F32)
+    peers = (p.nc, p.nx, p.nz, p.far, p.ny)
+    for i, dev in enumerate(peers):
+        mail.send(vbuf.at[i], vrec.at[i], rvec.at[i], dev)
+        if i == 1:
+            spread_out.third()
+        if i == 2:
+            spread.third()
+        mail.got(vrec.at[i], rvec.at[i], dev)
+        new = vbuf[i] + vrec[i]
+        if i < 4:
+            vbuf[i + 1] = new
+        else:
+            vec[...] = new
+    spread_out.last()
+    spread.last()
+    mail.close()
+
+
+def count_table():
+    kinds = np.array([[0, 0, 0, 0], [1, 0, 0, 0], [1, 1, 0, 0], [1, 0, 1, 0], [1, 1, 1, 1]], np.float64)
+    shared = kinds @ kinds.T
+    table = np.zeros((24, 128), np.float64)
+    low = lambda v: float(np.asarray(v, dtype=ml_dtypes.bfloat16).astype(np.float64))
+    for i in range(5):
+        for k in range(5):
+            for base, count in ((64, 1.0 + shared[i, k]), (80, shared[i, k])):
+                rest = float(np.log(count)) if count > 0 else 0.0
+                for e in range(3):
+                    table[i, base + 3 * k + e] = low(rest)
+                    rest -= low(rest)
+        table[8 + i, 64 + 3 * i : 67 + 3 * i] = 1.0
+        table[16 + i, 80 + 3 * i : 83 + 3 * i] = 1.0
+    return table.astype(np.float32)
+
+
+def split_rows(v):
+    return v.reshape(64, 2, -1).transpose(1, 0, 2).reshape(128, -1)
+
+
+def join_rows(v):
+    return v.reshape(2, 64, -1).transpose(1, 0, 2).reshape(128, -1)
+
+
+def vm(shape, dtype=B16):
+    return pltpu.VMEM(shape, dtype)
+
+
+def dma(*shape):
+    return pltpu.SemaphoreType.DMA(shape)
+
+
+def out(shape, dtype=F32):
+    return jax.ShapeDtypeStruct(shape, dtype)
+
+
+def in_vmem(count):
+    return [pl.BlockSpec(memory_space=pltpu.VMEM)] * count
+
+
+def call_one(*args):
+    shapes = (
+        out((4, 512, 128), B16), out((6, 512, 128), B16), out((6, 512, 128), B16), out((4, 512, 768), B16),
+        out((8, 1, 256)), out((4, 128, 256)), out((8, 1, 256)), out((6, 128, 128), B16), out((768, 3456), B16),
+        out((128, 768)), out((128, 768), B16), out((8, 768)), out((8, 1536)),
+    )
+    scratch = [
+        vm((16, 128, 768)), vm((17, 8, 128), F32), vm((768, 3072)), vm((2, 384, 768)), vm((2, 128, 768)),
+        vm((12, 128, 128)), vm((4, 256, 128)), vm((4, 256, 128)), vm((4, 256, 128)), vm((256, 768)), vm((6, 128, 512)),
+        vm((256, 768), F32), vm((256, 768)), vm((256, 768)), vm((256, 1536)), vm((256, 1536)), vm((256, 768), F32),
+        vm((256, 768), F32), vm((256, 768)), vm((256, 768)), vm((128, 768)), vm((128, 768)), vm((128, 768), F32),
+        dma(160), dma(3, 16), dma(3, 16), dma(16), dma(16), dma(12), dma(2), dma(4),
+    ]
+    return pl.pallas_call(
+        kernel_one, out_shape=shapes, in_specs=in_vmem(len(args)), out_specs=tuple(in_vmem(len(shapes))), scratch_shapes=scratch,
+        compiler_params=pltpu.CompilerParams(collective_id=0, has_side_effects=True, vmem_limit_bytes=LIMIT),
+    )(*args)
+
+
+def front(layer_input, doc_ids, cotangent, ln1_gain, ln1_bias, w_qkv, bias_qv, w_out, b_out, ln2_gain, ln2_bias, w_up, b_up, w_down, b_down):
+    s, y = lax.axis_index("seq"), lax.axis_index("head")
+    u = s % 8
+    hl = u - u // 4 - u // 6
+    row = lambda v: v.reshape(1, -1)
+    xp = split_rows(layer_input)
+    dyp = split_rows(jnp.where((doc_ids >= 0)[:, None], cotangent, jnp.zeros_like(cotangent)))
+    doc = doc_ids.astype(F32).reshape(64, 2).T
+    doc = jnp.pad(jnp.concatenate([doc, doc], axis=1), ((0, 6), (0, 0)))
+    wide = ((0, 0), (0, 0), (0, 64))
+    wq = jnp.pad(lax.dynamic_slice(w_qkv, (0, 0, hl * 64), (768, 3, 64)), wide).reshape(768, 384)
+    bq = lax.dynamic_slice(bias_qv, (0, hl * 64), (2, 64))
+    zero, one = jnp.zeros((64,), F32), jnp.ones((1,), F32)
+    bq = row(jnp.concatenate([bq[0], zero, zero, zero, bq[1], one, zero[:63]]))
+    wud = jnp.concatenate([w_up, w_down.T], axis=1)
+    bup = row(lax.dynamic_slice(b_up, (y * 1536,), (1536,)))
+    return call_one(
+        xp, dyp, doc, wq, bq, row(ln1_gain), row(ln1_bias), w_out, row(b_out), row(ln2_gain), row(ln2_bias), wud, bup, row(b_down),
+        jnp.asarray(count_table()),
+    ), (xp,)
+
+
+def call_two(*args):
+    shapes = (out((128, 768)), out((48, 3072)), out((16, 112, 768), B16), out((16, 48, 384), B16), out((16, 768)))
+    scratch = [
+        vm((4, 256, 128)), vm((8, 256, 128)), vm((8, 1, 256), F32), vm((6, 128, 512)), vm((512, 128), F32), vm((512, 128), F32),
+        vm((8, 128, 256), F32), vm((192, 2048)), vm((4, 256, 128)), vm((4, 256, 128)), vm((4, 3, 256, 128)), vm((6, 3, 128, 128)),
+        vm((2, 112, 768)), vm((112, 768)), vm((2, 4, 48, 3456)), vm((4, 48, 3456)), vm((4, 48, 3456)), vm((4, 48, 3456)),
+        vm((4, 48, 3456)), vm((256, 1152)), vm((256, 768), F32), vm((128, 768)), vm((128, 768)), vm((5, 16, 768), F32),
+        vm((5, 16, 768), F32),
+        dma(100), dma(8), dma(2, 4), dma(4), dma(4), dma(1), dma(6), dma(1), dma(16), dma(16), dma(1), dma(5),
+    ]
+    return pl.pallas_call(
+        kernel_two, out_shape=shapes, in_specs=in_vmem(len(args)), out_specs=tuple(in_vmem(len(shapes))), scratch_shapes=scratch,
+        compiler_params=pltpu.CompilerParams(collective_id=1, has_side_effects=True, vmem_limit_bytes=LIMIT),
+    )(*args)
+
+
+def fast(*args):
+    (qa, ka, va, ns, lse, ot, strow, dpk, grads, dh, lout, sums, supg), (xp,) = front(*args)
+    gain, w_qkv = args[3].reshape(1, -1), args[5].reshape(768, 1152)
+    gin, wud, wag, woag, vec = call_two(qa, ka, va, ns, lse, ot, strow, dpk, grads, dh, sums, supg, xp, gain, w_qkv)
+    heads = jnp.stack([wag[u + 8 * g] for u in UNITS for g in range(2)]).reshape(6, 2, 112, 768)
+    w_qkv_grad = heads[:, :, :96].reshape(6, 3, 64, 768).transpose(3, 1, 0, 2).reshape(768, 3, 384).astype(F32)
+    bias = heads[:, 0, 96, :192].reshape(6, 3, 64).transpose(1, 0, 2).reshape(3, 384).astype(F32)
+    w_out_grad = woag.reshape(768, 384).T.astype(F32)
+    return (
+        join_rows(lout), join_rows(gin), vec[0], vec[1], w_qkv_grad, jnp.stack([bias[0], bias[2]]), w_out_grad, vec[4], vec[2], vec[3],
+        wud[:, :1536], vec[6:10].reshape(3072), wud[:, 1536:].T, vec[5],
+    )
 
 
 def from_behind(value, axis, by):
@@ -465,6 +1330,7 @@
         P("head", "seq"),
         P(),
     )
+    small = mesh.shape["seq"] == 16 and mesh.shape["head"] == 2
     return jax.shard_map(
-        per_device, mesh=mesh, in_specs=in_specs, out_specs=out_specs, check_vma=False
-    )
+        fast if small else per_device, mesh=mesh, in_specs=in_specs, out_specs=out_specs, check_vma=False
+    )

time: 994 us -> 249 us (0.25)
  waiting for transfers between devices: 381 us -> 0 us
  Pallas kernels: 0 us -> 201 us
  matrix products: 175 us -> 0 us
  blocking collectives: 163 us -> 0 us
  other arithmetic: 114 us -> 5.02 us
  local copies, waits for them, and re-layouts: 93.1 us -> 41 us
  starting transfers between devices: 41.4 us -> 0 us
  between operations: 16.5 us -> 0.92 us
    pallas_call x0 -> x2, Pallas kernels: none -> 201 us  [the longest x1 116 us: call_two(): pl.pallas_call(kernel_two, out_shape=shapes, in_specs=in_vmem(len(args)),...]
    dot_general x25 -> x0, matrix products: 175 us -> none  [the longest x4 63.7 us: block_terms(): jnp.einsum('qhe,khe->hqk', query_blk, key_blk, preferred_element_type=jnp...]
    reduce_scatter x5 -> x0, waiting for transfers between devices: 123 us -> none  [the longest x1 79.7 us: per_device(): lax.psum_scatter(up_grad, 'seq', scatter_dimension=0, tiled=True)]
    all_gather x8 -> x0, waiting for transfers between devices: 123 us -> none  [the longest x1 61.4 us: per_device(): lax.all_gather(up_rows, 'head', axis=1, tiled=True)]
    all_gather x5 -> x0, blocking collectives: 89.1 us -> none  [the longest x1 37.6 us: per_device(): lax.all_gather(row_doc, 'seq', axis=0, tiled=True)]
    unnamed x16 -> x0, waiting for transfers between devices: 81.4 us -> none
    psum x2 -> x0, blocking collectives: 73.6 us -> none  [the longest x1 38.5 us: per_device(): lax.psum((gain_one_grad, bias_one_grad, gain_two_grad, bias_two_grad, bia...]
    psum x1 -> x0, waiting for transfers between devices: 48.7 us -> none  [per_device(): lax.psum((w_qkv_part, bias_qv_part, w_out_part), 'seq')]
  transfers between devices with their start and end apart: 29 -> 0, of which waited for: 8 -> 0; matrix products, arithmetic and copies ran while one was open for 34% -> 0% of each run, Pallas kernels for 0% -> 0%
where the time goes in v1:
time: 249 us; the launch traced here: 248 us
  Pallas kernels  201 us (81%)
  local copies, waits for them, and re-layouts  41 us (16%)
  other arithmetic  5.02 us (2%)
    pallas_call x1, Pallas kernels, call_two(): pl.pallas_call(kernel_two, out_shape=shapes, in_specs=in_vmem(len(args)),...  116 us
    pallas_call x1, Pallas kernels, call_one(): pl.pallas_call(kernel_one, out_shape=shapes, in_specs=in_vmem(len(args)),...  84.9 us
    unnamed x25, local copies, waits for them, and re-layouts  14.2 us
    reshape x8, local copies, waits for them, and re-layouts, front(): row = lambda v: v.reshape(1, -1)  8.76 us

profile of v1, /device:TPU:0, one launch (start us, length us, event | category | flops | bytes accessed | tf_op | source)
XLA Modules:
  0.0 248.1 jit_solution(6876639093159927620)
XLA Ops:
  2.9 1.3 reshape.115.g1_ref
  4.2 1.3 reshape.116.b1_ref
  5.5 1.3 reshape.117.bo_ref
  6.7 1.3 reshape.118.g2_ref
  8.0 1.3 reshape.119.b2_ref
  9.3 1.3 reshape.121.bd_ref
  12.8 1.0 broadcast_select_fusion
  14.6 1.0 reshape.108
  17.1 0.9 copy.54
  18.1 1.1 copy.55.wq_ref
  19.2 2.2 copy.58.wq_ref
  21.4 84.9 %shard_map.263 = (bf16[4,512,128]{2,1,0:T(8,128)(2,1)}, bf16[6,512,128]{2,1,0:T(8,128)(2,1)}, bf16[6,512,128]{2,1,0:T(8,128)(2,1)}, bf16[4,512,768]{2,1,0:T(8,12...) custom-call(bf16[128,768]{1,0:T(8,128)(2,1)} %bitcast.39, ...), custom_call_target="tpu_custom_call" | custom-call | tf_op jit(solution)/shard_map/pallas_call | solution.py:824
  106.2 1.1 copy.56
  108.1 116.3 %shard_map.264 = (f32[128,768]{1,0:T(8,128)}, f32[48,3072]{1,0:T(8,128)}, bf16[16,112,768]{2,1,0:T(8,128)(2,1)}, bf16[16,48,384]{2,1,0:T(8,128)(2,1)}, f32[16,768]{1,0:T(8,128)}) custom-call(bf16[4,512,128]{2,1,0:T(8,128)(2,1)} %get-tuple-element.33.qa, bf16[6,512,128]{2,1,0:T(8,128)(2,1)} %get-tuple-element.34.ka, ...), custom_call_target="tpu_custom_call" | custom-call | tf_op jit(solution)/shard_map/pallas_call | solution.py:862
  224.5 1.4 copy.59
  225.9 1.0 reshape.126
  227.7 1.6 slice_reduce_fusion.2
  229.9 0.8 slice_bitcast_fusion
  230.9 1.4 copy.61
  232.3 0.9 slice_dynamic-update-slice_fusion.11
  233.2 0.9 slice_dynamic-update-slice_fusion.10
  234.1 0.9 slice_dynamic-update-slice_fusion.9
  235.1 0.9 slice_dynamic-update-slice_fusion.8
  236.0 0.9 slice_dynamic-update-slice_fusion.7
  237.0 0.9 slice_dynamic-update-slice_fusion.6
  237.9 0.9 slice_dynamic-update-slice_fusion.5
  238.8 0.9 slice_dynamic-update-slice_fusion.4
  239.8 0.9 slice_dynamic-update-slice_fusion.3
  240.7 0.9 slice_dynamic-update-slice_fusion.2
  241.6 0.9 slice_dynamic-update-slice_fusion.1
  242.6 0.9 slice_dynamic-update-slice_fusion
  245.2 2.9 %copy.62 = f32[768,3,384]{2,0,1:T(8,128)} copy(f32[768,3,384]{0,2,1:T(8,128)S(1)} %bitcast.33) | data formatting | bytes 7077888
  (44 shorter events, 10.7 us)
Async XLA Ops:
  0.6 1.6 copy-start
  0.7 15.7 %copy-start.4 = (bf16[1536,48]{0,1:T(8,128)(2,1)S(1)}, bf16[1536,48]{0,1:T(8,128)(2,1)}, u32[]{:S(2)}) copy-start(bf16[1536,48]{0,1:T(8,128)(2,1)} %param.29) | copy-start | bytes 442372
  0.7 15.7 %copy-start.5 = (bf16[48,1536]{1,0:T(8,128)(2,1)S(1)}, bf16[48,1536]{1,0:T(8,128)(2,1)}, u32[]{:S(2)}) copy-start(bf16[48,1536]{1,0:T(8,128)(2,1)} %param.27) | copy-start | bytes 442372
  0.7 16.4 %copy-start.1 = (bf16[768,3,384]{2,0,1:T(8,128)(2,1)S(1)}, bf16[768,3,384]{2,0,1:T(8,128)(2,1)}, u32[]{:S(2)}) copy-start(bf16[768,3,384]{2,0,1:T(8,128)(2,1)} %param.21) | copy-start | bytes 5308420
  224.4 5.5 %copy-start.3 = (f32[48,3072]{1,0:T(8,128)S(1)}, f32[48,3072]{1,0:T(8,128)}, u32[]{:S(2)}) copy-start(f32[48,3072]{1,0:T(8,128)} %get-tuple-element.49) | copy-start | bytes 1769476
  224.4 6.3 %copy-start.2 = (bf16[16,48,384]{2,1,0:T(8,128)(2,1)S(1)}, bf16[16,48,384]{2,1,0:T(8,128)(2,1)}, u32[]{:S(2)}) copy-start(bf16[16,48,384]{2,1,0:T(8,128)(2,1)} %get-tuple-element.48) | copy-start | bytes 1769476

commit v2 on v0

--- a/solution.py
+++ b/solution.py
@@ -1,6 +1,12 @@
+import functools
+
 import jax
 import jax.numpy as jnp
+import ml_dtypes
+import numpy as np
 from jax import lax
+from jax.experimental import pallas as pl
+from jax.experimental.pallas import tpu as pltpu
 from jax.sharding import PartitionSpec as P
 
 HEADS = 12
@@ -12,6 +18,972 @@
 EPS = 1e-05
 NEGATIVE = -1e30
 block_limit = 2048
+
+
+MESH = pl.DeviceIdType.MESH
+VMEM = pltpu.VMEM
+LIMIT = 60 << 20
+F32 = jnp.float32
+B16 = jnp.bfloat16
+
+
+def dot(a, b):
+    return jnp.dot(a, b, preferred_element_type=F32)
+
+
+def dot_nt(a, b):
+    return lax.dot_general(a, b, (((1,), (1,)), ((), ())), preferred_element_type=F32)
+
+
+def sid(z, x, c):
+    return z * 4 + x * 2 + c
+
+
+class Place:
+    def __init__(self):
+        s = lax.axis_index("seq")
+        self.s, self.y = s, lax.axis_index("head")
+        self.z, self.x, self.c = s // 4, (s // 2) % 2, s % 2
+        self.seg, self.zl = self.z // 2, self.z % 2
+        self.u = s % 8
+        self.b = self.u * 2 + self.y
+        self.unit = jnp.logical_and(self.u != 3, self.u != 5)
+        self.hl = self.u - self.u // 4 - self.u // 6
+        self.head = self.y * 6 + self.hl
+        self.parity = self.head % 2
+        z, x, c, y = self.z, self.x, self.c, self.y
+        self.zf = z + 1 - 2 * self.zl
+        self.nx, self.ny = (sid(z, 1 - x, c), y), (s, 1 - y)
+        self.nz, self.nc = (sid(self.zf, x, c), y), (sid(z, x, 1 - c), y)
+        self.far = (sid((z + 2) % 4, x, c), y)
+        self.fb = {"x": 4 * (1 - 2 * x), "y": 1 - 2 * y, "z": 8 * (1 - 2 * self.zl), "c": 2 * (1 - 2 * c)}
+
+    def cube(self):
+        z, x, c, y = self.z, self.x, self.c, self.y
+        for k in range(1, 16):
+            zz = self.zf if k & 8 else z
+            xx = 1 - x if k & 4 else x
+            cc = 1 - c if k & 2 else c
+            yy = 1 - y if k & 1 else y
+            yield (sid(zz, xx, cc), yy)
+
+    def greet(self):
+        others = list(self.cube())
+        others += [(sid((self.z + 2) % 4, self.x, self.c), self.y), (sid((self.zf + 2) % 4, self.x, self.c), self.y)]
+        barrier = pltpu.get_barrier_semaphore()
+        for dev in others:
+            pl.semaphore_signal(barrier, inc=1, device_id=dev, device_id_type=MESH)
+        self.greeted = len(others)
+
+    def meet(self):
+        pl.semaphore_wait(pltpu.get_barrier_semaphore(), self.greeted)
+
+
+class Mail:
+    def __init__(self, sems):
+        self.sems, self.used, self.sent = sems, 0, []
+
+    def send(self, src, dst, rsem, dev, cond=None):
+        k = self.used
+        self.used += 1
+
+        def make():
+            return pltpu.make_async_remote_copy(
+                src_ref=src, dst_ref=dst, send_sem=self.sems.at[k], recv_sem=rsem, device_id=dev, device_id_type=MESH
+            )
+
+        if cond is None:
+            make().start()
+        else:
+            pl.when(cond)(lambda: make().start())
+        self.sent.append((cond, make))
+
+    def got(self, dst, rsem, dev):
+        pltpu.make_async_remote_copy(
+            src_ref=dst, dst_ref=dst, send_sem=self.sems.at[0], recv_sem=rsem, device_id=dev, device_id_type=MESH
+        ).wait_recv()
+
+    def close(self):
+        for cond, make in self.sent:
+            if cond is None:
+                make().wait_send()
+            else:
+                pl.when(cond)(lambda make=make: make().wait_send())
+        self.sent = []
+
+
+def both(*terms):
+    out = terms[0]
+    for term in terms[1:]:
+        out = jnp.logical_and(out, term)
+    return out
+
+
+def iota(shape, dim):
+    return lax.broadcasted_iota(jnp.int32, shape, dim)
+
+
+def norm_parts(v):
+    mean = jnp.mean(v, axis=-1, keepdims=True)
+    cen = v - mean
+    inv = lax.rsqrt(jnp.mean(cen * cen, axis=-1, keepdims=True) + EPS)
+    return cen * inv, inv
+
+
+def norm_grad(z, inv, e):
+    return (e - jnp.mean(e, axis=-1, keepdims=True) - z * jnp.mean(e * z, axis=-1, keepdims=True)) * inv
+
+
+def pick_type(pos, head, rows):
+    v = pos - head + 24.0
+    m = v - 12.0 * jnp.floor((v + 0.5) * (1.0 / 12.0))
+    out = jnp.where(m == 0.0, rows[4], rows[0])
+    out = jnp.where(m == 6.0, rows[3], out)
+    out = jnp.where(jnp.logical_or(m == 4.0, m == 8.0), rows[2], out)
+    return jnp.where(jnp.logical_or(m == 2.0, m == 10.0), rows[1], out)
+
+
+def halves(e, o):
+    low = iota(e.shape, 1) < 64
+    return jnp.where(low, e, pltpu.roll(o, 64, 1)), jnp.where(low, pltpu.roll(e, 64, 1), o)
+
+
+UNITS = (0, 1, 2, 4, 6, 7)
+
+
+class Spread:
+    def __init__(self, p, mail, ref, sems, some):
+        self.p, self.mail, self.ref, self.sems, self.some = p, mail, ref, sems, some
+
+    def has(self, zz, xx, cc):
+        return jnp.logical_or(cc == 0, zz % 2 == xx) if self.some else None
+
+    def go(self, s, dev, cond):
+        self.mail.send(self.ref.at[s], self.ref.at[s], self.sems.at[s], dev, cond)
+
+    def take(self, s, cond):
+        def wait():
+            self.mail.got(self.ref.at[s], self.sems.at[s], self.p.nx)
+
+        if cond is None:
+            wait()
+        else:
+            pl.when(cond)(wait)
+
+    def first(self):
+        p = self.p
+        has = self.has(p.z, p.x, p.c)
+        for k in range(1, 4):
+            self.go(p.s, (sid((p.z + k) % 4, p.x, p.c), p.y), has)
+        self.go(p.s, p.nx, has)
+        self.go(p.s, p.nc, has)
+
+    def second(self):
+        p = self.p
+        for k in range(1, 4):
+            zz = (p.z + k) % 4
+            s, has = sid(zz, p.x, p.c), self.has(zz, p.x, p.c)
+            self.take(s, has)
+            self.go(s, p.nx, has)
+            self.go(s, p.nc, has)
+
+    def third(self):
+        p = self.p
+        for zz in range(4):
+            s, has = sid(zz, 1 - p.x, p.c), self.has(zz, 1 - p.x, p.c)
+            self.take(s, has)
+            self.go(s, p.nc, has)
+
+    def last(self):
+        p = self.p
+        for zz in range(4):
+            for xx in range(2):
+                self.take(sid(zz, xx, 1 - p.c), self.has(zz, xx, 1 - p.c))
+
+
+class Reduce:
+    def __init__(self, p, mail, src, gc, gxs, gxr, gzs, gzr, rc, rx, rz):
+        self.__dict__.update(locals())
+
+    def rows(self, zz, xx, cc):
+        return pl.ds(pl.multiple_of(sid(zz, xx, cc) * 48, 16), 48)
+
+    def cores(self):
+        p = self.p
+        for xq in range(2):
+            xx = 1 - p.x if xq == 0 else p.x
+            for k in (1, 2, 3, 0):
+                zz = (p.z + k) % 4
+                self.mail.send(self.src.at[self.rows(zz, xx, 1 - p.c)], self.gc.at[xq, zz], self.rc.at[xq, zz], p.nc)
+
+    def over_x(self):
+        p = self.p
+        for k in (1, 2, 3, 0):
+            zz = (p.z + k) % 4
+            self.mail.got(self.gc.at[0, zz], self.rc.at[0, zz], p.nc)
+            own = self.src[self.rows(zz, 1 - p.x, p.c)].astype(F32)
+            self.gxs[zz] = (own + self.gc[0, zz].astype(F32)).astype(B16)
+            self.mail.send(self.gxs.at[zz], self.gxr.at[zz], self.rx.at[zz], p.nx)
+
+    def column(self, zz):
+        p = self.p
+        self.mail.got(self.gc.at[1, zz], self.rc.at[1, zz], p.nc)
+        self.mail.got(self.gxr.at[zz], self.rx.at[zz], p.nx)
+        return self.src[self.rows(zz, p.x, p.c)].astype(F32) + self.gc[1, zz].astype(F32) + self.gxr[zz].astype(F32)
+
+    def over_z(self, k):
+        p = self.p
+        zz = (p.z + k) % 4
+        self.gzs[k] = self.column(zz).astype(B16)
+        self.mail.send(self.gzs.at[k], self.gzr.at[p.z], self.rz.at[p.z], (sid(zz, p.x, p.c), p.y))
+
+    def result(self):
+        p = self.p
+        total = self.column(p.z)
+        for k in range(1, 4):
+            zz = (p.z + k) % 4
+            self.mail.got(self.gzr.at[zz], self.rz.at[zz], p.nx)
+            total = total + self.gzr[zz].astype(F32)
+        return total
+
+
+class Slots:
+    def __init__(self, ref, base):
+        self.ref, self.base = ref, base
+
+    def span(self, i):
+        return pl.ds(pl.multiple_of(self.base + i * 48, 16), 48)
+
+    @property
+    def at(self):
+        return self
+
+    def __getitem__(self, i):
+        return self.ref.at[self.span(i)]
+
+    def __setitem__(self, i, value):
+        self.ref[self.span(i)] = value
+
+
+class Total:
+    def __init__(self, p, mail, buf, rec, sems):
+        self.mail, self.buf, self.rec, self.sems = mail, buf, rec, sems
+        self.peers = (p.nc, p.nx, p.nz, p.far, p.ny)
+
+    def start(self, i):
+        self.mail.send(self.buf.at[i], self.rec.at[i], self.sems.at[i], self.peers[i])
+
+    def finish(self, i):
+        self.mail.got(self.rec.at[i], self.sems.at[i], self.peers[i])
+        new = self.buf[i] + self.rec[i]
+        if i < 4:
+            self.buf[i + 1] = new
+        return new
+
+
+def mixed(shape, dim_to, dim_from):
+    r, i = iota(shape, dim_to), iota(shape, dim_from)
+    return jnp.where(i == 2 * (r & 63) + (r >> 6), 1.0, 0.0).astype(B16)
+
+
+def kernel(
+    x_ref, doc_ref, cot_ref, g1_ref, b1_ref, wq_ref, bqv_ref, wo_own, bo_ref, g2_ref, b2_ref, wup_ref, bup_ref, wdn_ref, bd_ref, tab_ref,
+    lout, gin, o_g1, o_b1, o_wq, o_bqv, o_wo, o_bo, o_g2, o_b2, o_up, o_bup, o_dn, o_bd,
+    qa, ka, va, ns, lse, ot, dpk, grads, gwo, dh_s, wqh, bqh, buph, msc, asc,
+    xs, docs, wb, wo, dyp, orecv, osend, kvs, kvf, attn, vt, hid, n2s, dys, acts, dpre, facc, dacc, ys, yr, fs, fr, fo,
+    dor, doa, delta, kt, dka, dva, dqt, dtt, dfs, dfr, packs, dqr, wms, wmr, gc, gxr, gzr, hc, hxs, hxr, hzs, hzr, dall, dns, dnr,
+    vb1, vr1, vb2, vr2, wag, woag,
+    ss, rsx, rsc, rsd, rsw, rso, rsf, rsy, rdo, rgc, rgx, rgz, rhc, rhx, rhz, rdf, rdq, rwm, rag, rwo, rdn, rv1, rv2,
+):
+    p = Place()
+    mail = Mail(ss)
+    seg, x, y, z, c, b = p.seg, p.x, p.y, p.z, p.c, p.b
+    first, second = both(p.unit, seg == 0), both(p.unit, seg == 1)
+    row = lambda ref: ref[...].reshape(1, -1)
+    p.greet()
+
+    mix = mixed((128, 128), 0, 1)
+    xs[b] = dot(mix, x_ref[...]).astype(B16)
+    doc_row = doc_ref[...].astype(F32).reshape(1, 128)
+    turn = jnp.where(iota((128, 128), 0) == 2 * (iota((128, 128), 1) & 63), 1.0, 0.0).astype(B16)
+    turn_odd = jnp.where(iota((128, 128), 0) == 2 * (iota((128, 128), 1) & 63) + 1, 1.0, 0.0).astype(B16)
+    doc8 = jnp.broadcast_to(doc_row, (8, 128)).astype(B16)
+    docs[b] = jnp.where(iota((8, 128), 0) == 0, dot(doc8, turn), dot(doc8, turn_odd))
+    p.meet()
+
+    dims = ("x", "y", "z")
+    nbr = {"x": p.nx, "y": p.ny, "z": p.nz}
+    part = [pl.ds(k * 256, 256) for k in range(3)]
+    order = [[dims[(k + j) % 3] for j in range(3)] for k in range(3)]
+
+    def pass_on(k, blk, dev):
+        ref = xs.at[blk, :, part[k]]
+        mail.send(ref, ref, rsx.at[k, blk], dev)
+
+    def to_core(k, blk):
+        ref = xs.at[blk, :, part[k]]
+        mail.send(ref, ref, rsc.at[k, blk], p.nc)
+
+    for j in range(3):
+        for k in range(3):
+            pass_on(k, b, nbr[order[k][j]])
+    for k in range(3):
+        to_core(k, b)
+    for src in (0, 14, 15):
+        for dev in p.cube():
+            mail.send(docs.at[src], docs.at[src], rsd.at[src], dev, cond=b == src)
+
+    pair_cols = pl.ds(pl.multiple_of(p.hl // 2 * 128, 128), 128)
+    for odd in range(2):
+
+        @pl.when(p.hl % 2 == odd)
+        def _(odd=odd):
+            for k in range(3):
+                w = wq_ref[k, :, pair_cols].astype(F32)
+                w = pltpu.roll(w, 64, 1) if odd else w
+                wqh[:, k * 128 : k * 128 + 128] = jnp.where(iota((768, 128), 1) < 64, w, 0.0).astype(B16)
+            v = jnp.concatenate([bqv_ref[:, pair_cols], jnp.zeros((6, 128), F32)], axis=0)
+            v = pltpu.roll(v, 64, 1) if odd else v
+            lane = iota((1, 128), 1)
+            bqh[:, 0:128] = jnp.where(lane < 64, v[0:1], 0.0)
+            bqh[:, 128:256] = jnp.zeros((1, 128), F32)
+            bqh[:, 256:384] = jnp.where(lane < 64, v[1:2], jnp.where(lane == 64, 1.0, 0.0))
+
+    head = p.head.astype(F32)
+    for t in range(4):
+        rr = iota((512, 128), 0)
+        pos = (seg * SEG + t * 512 + 2 * (rr & 255) + (rr >> 8)).astype(F32)
+        qa[t] = pick_type(pos, head, [tab_ref[i : i + 1] for i in range(5)]).astype(B16)
+        ka[t + 2] = pick_type(pos, head, [tab_ref[8 + i : 9 + i] for i in range(5)]).astype(B16)
+
+    real = jnp.broadcast_to(doc_row, (128, 128)).T >= 0.0
+    for k in range(6):
+        cols = slice(k * 128, k * 128 + 128)
+        kept = jnp.where(real, cot_ref[:, cols].astype(F32), 0.0).astype(B16)
+        dyp[y, :, cols] = dot(mix, kept).astype(B16)
+    for half in range(2):
+
+        @pl.when(y == half)
+        def _(half=half):
+            buph[...] = bup_ref[half * 1536 : half * 1536 + 1536].reshape(1, 1536)
+
+    wrow = pl.ds(pl.multiple_of(p.s * 48, 16), 48)
+    wb[wrow, 0:1536] = wup_ref[...]
+    wb[wrow, 1536:3072] = wdn_ref[...]
+    wo[y] = wo_own[...]
+
+    def qkv(i):
+        rows = xs[pl.ds(2 * i, 2)].reshape(256, 768).astype(F32)
+        zz, _inv = norm_parts(rows)
+        n1 = (zz * row(g1_ref) + row(b1_ref)).astype(B16)
+        m = (dot(n1, wqh[...]) + bqh[...]).astype(B16)
+        t = i // 2
+        for yy in range(2):
+            for par in range(2):
+                at = slice(yy * 128 + par * 64, yy * 128 + par * 64 + 64)
+                to = pl.ds(pl.multiple_of(par * 256 + (i % 2) * 128 + yy * 64, 64), 64)
+                qa[t, to] = m[at, :128] * B16(0.125) + qa[t, to]
+                ka[t + 2, to] = m[at, 128:256] + ka[t + 2, to]
+                va[t + 2, to] = m[at, 256:]
+                ns[t, to] = n1[at]
+
+    def seen(k, blk):
+        mail.got(xs.at[blk, :, part[k]], rsx.at[k, blk], p.nx)
+        to_core(k, blk)
+
+    def from_core(blk):
+        for k in range(3):
+            mail.got(xs.at[blk, :, part[k]], rsc.at[k, blk], p.nc)
+
+    fx, fy, fz, fc = p.fb["x"], p.fb["y"], p.fb["z"], p.fb["c"]
+
+    def qkv_of(*flips):
+        at = (b + sum(flips)) // 2
+        pl.when(p.unit)(lambda: qkv(at))
+
+    for k in range(3):
+        f = [p.fb[d] for d in order[k]]
+        seen(k, b + f[0])
+        pass_on(k, b + f[0], nbr[order[k][1]])
+        pass_on(k, b + f[0], nbr[order[k][2]])
+    for k in range(3):
+        f = [p.fb[d] for d in order[k]]
+        for blk in (b + f[1], b + f[1] + f[0]):
+            seen(k, blk)
+            pass_on(k, blk, nbr[order[k][2]])
+
+    def rows_of(s):
+        return wb.at[pl.ds(pl.multiple_of(s * 48, 16), 48), :]
+
+    def give(s, dev, cond=None):
+        mail.send(rows_of(s), rows_of(s), rsw.at[s], dev, cond)
+
+    give(p.s, (sid((z + 1) % 4, x, c), y), z <= 2)
+    give(p.s, (sid((z + 3) % 4, x, c), y), z >= 1)
+    give(p.s, p.nx)
+    give(p.s, p.nc)
+    mail.send(wo.at[y], wo.at[y], rsy.at[0], p.ny)
+    mail.send(dyp.at[y], dyp.at[y], rsy.at[1], p.ny)
+
+    def chain(d):
+        up, dn = (z - d + 4) % 4, (z + d) % 4
+        has_up, has_dn = z >= d, z <= 3 - d
+        su, sd = sid(up, x, c), sid(dn, x, c)
+        pl.when(has_up)(lambda: mail.got(rows_of(su), rsw.at[su], p.nx))
+        if d < 3:
+            give(su, (sid((z + 1) % 4, x, c), y), both(has_up, z <= 2))
+        give(su, p.nx, has_up)
+        give(su, p.nc, has_up)
+        pl.when(has_dn)(lambda: mail.got(rows_of(sd), rsw.at[sd], p.nx))
+        if d < 3:
+            give(sd, (sid((z + 3) % 4, x, c), y), both(has_dn, z >= 1))
+        give(sd, p.nx, has_dn)
+        give(sd, p.nc, has_dn)
+
+    for k in range(3):
+        f = [p.fb[d] for d in order[k]]
+        for blk in (b + f[2], b + f[2] + f[0], b + f[2] + f[1], b + f[2] + f[1] + f[0]):
+            seen(k, blk)
+    for flips in ((), (fx,), (fz,), (fx, fz)):
+        qkv_of(*flips)
+    for flips in ((), (fx,), (fz,), (fx, fz)):
+        from_core(b + fc + sum(flips))
+        from_core(b + fc + sum(flips) + fy)
+        qkv_of(fc, *flips)
+    for src in (0, 14, 15):
+        pl.when(b != src)(lambda src=src: mail.got(docs.at[src], rsd.at[src], p.nx))
+
+    lowlane = iota((256, 128), 1) < 64
+    farrows = pl.ds(pl.multiple_of(p.parity * 256, 256), 256)
+
+    @pl.when(first)
+    def _():
+        for t in range(4):
+            kk = ka[t + 2, farrows].astype(F32)
+            vv = va[t + 2, farrows].astype(F32)
+            kvs[t] = jnp.where(lowlane, kk, pltpu.roll(vv, 64, 1)).astype(B16)
+
+    mail.send(kvs, kvf, rsf.at[0], p.far, first)
+    mail.send(docs.at[0], docs.at[16], rsf.at[1], p.far, first)
+
+    def codes(src, par):
+        r = docs[src, par : par + 1]
+        return jnp.broadcast_to(jnp.where(r < 0.0, 4.0, r), (128, 128)).T[0:64]
+
+    def mark(ref, at, code, query):
+        lane = iota((64, 128), 1)
+        hit = (lane - 96).astype(F32) == code
+        if query:
+            feat = jnp.where(hit, 0.0, jnp.where(lane < 101, NEGATIVE, 0.0))
+        else:
+            feat = jnp.where(hit, 1.0, 0.0)
+        ref[at] = jnp.where(lane >= 96, feat, ref[at].astype(F32)).astype(B16)
+
+    @pl.when(first)
+    def _():
+        for par in range(2):
+            code = codes(0, par)
+            at = slice(par * 256, par * 256 + 64)
+            mark(qa.at[0], at, code, True)
+            mark(ka.at[2], at, code, False)
+
+    @pl.when(second)
+    def _():
+        for par in range(2):
+            for yy in range(2):
+                code = codes(14 + yy, par)
+                at = slice(par * 256 + 128 + yy * 64, par * 256 + 192 + yy * 64)
+                mark(qa.at[3], at, code, True)
+                mark(ka.at[5], at, code, False)
+
+    @pl.when(p.unit)
+    def _():
+        for t in range(4):
+            vt[t + 2] = va[t + 2].astype(F32).T.astype(B16)
+
+    rr, ll = iota((512, 512), 0), iota((512, 512), 1)
+    causal = lambda st: jnp.where(2 * (rr & 255) + (rr >> 8) <= 2 * (ll & 255) + (ll >> 8), st, NEGATIVE)
+
+    def near_attention(t):
+        q = qa[t]
+
+        def update(cc, carry, st):
+            m, acc = carry
+            m_new = jnp.maximum(m, jnp.max(st, axis=0, keepdims=True))
+            pr = jnp.exp(st - m_new).astype(B16)
+            return m_new, acc * jnp.exp(m - m_new) + dot(vt[cc], pr)
+
+        state = (jnp.full((1, 512), NEGATIVE, F32), jnp.zeros((128, 512), F32))
+        if t:
+            state = lax.fori_loop(2, t + 2, lambda cc, s: update(cc, s, dot_nt(ka[cc], q)), state)
+        msc[t], asc[t] = update(t + 2, state, causal(dot_nt(ka[t + 2], q)))
+
+    def far_ready():
+        mail.got(kvf, rsf.at[0], p.far)
+        mail.got(docs.at[16], rsf.at[1], p.far)
+        for t in range(4):
+            rows = pl.ds((t % 2) * 256, 256)
+            fpos = ((t * 256 + iota((256, 128), 0)) * 2 + p.parity).astype(F32)
+            feat = pick_type(fpos, head, [tab_ref[16 + i : 17 + i] for i in range(5)])
+            kv = kvf[t].astype(F32)
+            ka[t // 2, rows] = jnp.where(lowlane, kv, feat).astype(B16)
+            one = jnp.where(iota((256, 128), 1) == 64, 1.0, 0.0)
+            va[t // 2, rows] = jnp.where(lowlane, pltpu.roll(kv, 64, 1), one).astype(B16)
+        even, odd = codes(16, 0), codes(16, 1)
+        mark(ka.at[0], slice(0, 64), even + p.parity.astype(F32) * (odd - even), False)
+        for h in range(2):
+            vt[h] = va[h].astype(F32).T.astype(B16)
+
+    farcols = pl.ds(pl.multiple_of(p.parity * 256, 256), 256)
+
+    def far_attention(t):
+        q = qa[t, farcols]
+        m = msc[t, :, farcols]
+        s0, s1 = dot_nt(ka[0], q), dot_nt(ka[1], q)
+        m_new = jnp.maximum(m, jnp.maximum(jnp.max(s0, axis=0, keepdims=True), jnp.max(s1, axis=0, keepdims=True)))
+        acc = asc[t, :, farcols] * jnp.exp(m - m_new)
+        acc = acc + dot(vt[0], jnp.exp(s0 - m_new).astype(B16))
+        acc = acc + dot(vt[1], jnp.exp(s1 - m_new).astype(B16))
+        msc[t, :, farcols] = m_new
+        asc[t, :, farcols] = acc
+
+    def conclude(t):
+        acc = asc[t]
+        total = acc[64:65]
+        o = acc[:64] / total
+        lse[t] = msc[t] + jnp.log(total)
+        ot[t] = jnp.concatenate([o[:, :256], o[:, 256:]], axis=0)
+        osend[t] = ot[t].T.astype(B16)
+
+    def deliver(t, who):
+        for cc in range(2):
+            for yy in range(2):
+                own = both(p.u == t * 2 + cc, y == yy)
+                src = osend.at[t, cc * 128 : cc * 128 + 128]
+                dev = (sid(seg * 2 + t // 2, t % 2, cc), yy)
+                mail.send(src, orecv.at[p.head], rso.at[p.head], dev, both(who, jnp.logical_not(own)))
+
+                @pl.when(both(who, own))
+                def _(cc=cc):
+                    orecv[p.head] = osend[t, cc * 128 : cc * 128 + 128]
+
+    for t in range(4):
+        pl.when(p.unit)(functools.partial(near_attention, t))
+        pl.when(first)(functools.partial(conclude, t))
+        deliver(t, first)
+        if t == 1:
+            chain(1)
+        if t == 3:
+            chain(2)
+    pl.when(second)(far_ready)
+    for t in range(4):
+        pl.when(second)(functools.partial(far_attention, t))
+        pl.when(second)(functools.partial(conclude, t))
+        deliver(t, second)
+    chain(3)
+    for zq in range(4):
+        s = sid(zq, 1 - x, c)
+        mail.got(rows_of(s), rsw.at[s], p.nx)
+        give(s, p.nc)
+
+    for hh in range(12):
+        mine = both(p.unit, p.head == hh)
+        pl.when(jnp.logical_not(mine))(lambda hh=hh: mail.got(orecv.at[hh], rso.at[hh], p.nx))
+    for a in range(6):
+        e, o = halves(orecv[2 * a].astype(F32), orecv[2 * a + 1].astype(F32))
+        attn[0:128, a * 128 : a * 128 + 128] = e.astype(B16)
+        attn[128:256, a * 128 : a * 128 + 128] = o.astype(B16)
+    mail.got(wo.at[1 - y], rsy.at[0], p.ny)
+    mail.got(dyp.at[1 - y], rsy.at[1], p.ny)
+    pair = pl.multiple_of(p.u * 2, 2)
+    for par in range(2):
+        for yy in range(2):
+            at = pl.ds(par * 128 + yy * 64, 64)
+            hid[at] = xs[pair + yy, par * 64 : par * 64 + 64].astype(F32)
+            dys[at] = dyp[yy, par * 64 : par * 64 + 64]
+    hid[...] = hid[...] + dot(attn[...], wo[...].reshape(768, 768)) + row(bo_ref)
+    z2, _inv = norm_parts(hid[...])
+    n2s[...] = (z2 * row(g2_ref) + row(b2_ref)).astype(B16)
+    for i in range(8):
+        s = sid(i // 2, i % 2, 1 - c)
+        mail.got(rows_of(s), rsw.at[s], p.nc)
+
+    facc[...] = jnp.zeros_like(facc)
+    dacc[...] = jnp.zeros_like(dacc)
+    k0 = 0.7978845608028654
+    vb1[0] = jnp.zeros((8, 768), F32)
+
+    def ffn_step(i, _):
+        cols = pl.ds(pl.multiple_of(i * 256, 256), 256)
+        dcols = pl.ds(pl.multiple_of(1536 + i * 256, 256), 256)
+        up, dn = wb[:, cols], wb[:, dcols]
+        pre = dot(n2s[...], up) + buph[:, cols]
+        sq = pre * pre
+        th = jnp.tanh(k0 * pre * (1.0 + 0.044715 * sq))
+        half = 0.5 * (1.0 + th)
+        act = (pre * half).astype(B16)
+        slope = half + 0.5 * pre * (1.0 - th * th) * (k0 * (1.0 + 3.0 * 0.044715 * sq))
+        dp = dot(dys[...], dn) * slope
+        buph[:, cols] = jnp.sum(dp, axis=0, keepdims=True)
+        dpl = dp.astype(B16)
+        acts[:, cols] = act
+        dpre[:, cols] = dpl
+        facc[...] += dot_nt(act, dn)
+        dacc[...] += dot_nt(dpl, up)
+        return 0
+
+    lax.fori_loop(0, 6, ffn_step, 0)
+    ys[...] = dacc[...].astype(B16)
+    mail.send(ys, yr, rsy.at[2], p.ny)
+    for par in range(2):
+        fo[par * 64 : par * 64 + 64] = facc[pl.ds(pl.multiple_of(par * 128 + y * 64, 64), 64)]
+        fs[par * 64 : par * 64 + 64] = facc[pl.ds(pl.multiple_of(par * 128 + (1 - y) * 64, 64), 64)].astype(B16)
+    mail.send(fs, fr, rsy.at[3], p.ny)
+
+    n2t = n2s[...].astype(F32).T.astype(B16)
+    dyt = dys[...].astype(F32).T.astype(B16)
+
+    def grad_step(i, _):
+        cols = pl.ds(pl.multiple_of(i * 256, 256), 256)
+        dcols = pl.ds(pl.multiple_of(1536 + i * 256, 256), 256)
+        grads[:, cols] = dot(n2t, dpre[:, cols]).astype(B16)
+        grads[:, dcols] = dot(dyt, acts[:, cols]).astype(B16)
+        return 0
+
+    lax.fori_loop(0, 6, grad_step, 0)
+    mail.close()
+    ffn_sum = Reduce(p, mail, grads, gc, Slots(wb, 0), gxr, Slots(wb, 192), gzr, rgc, rgx, rgz)
+    out_sum = Reduce(p, mail, gwo, hc, hxs, hxr, hzs, hzr, rhc, rhx, rhz)
+    ffn_sum.cores()
+    mail.got(yr, rsy.at[2], p.ny)
+    dn2 = ys[...].astype(F32) + yr[...].astype(F32)
+    z2, inv2 = norm_parts(hid[...])
+    dh = dys[...].astype(F32) + norm_grad(z2, inv2, dn2 * row(g2_ref))
+    facc[...] = dh
+    dacc[...] = dn2 * z2
+    da_ = dot_nt(dh.astype(B16), wo[y])
+    for a in range(3):
+        e, o = halves(da_[0:128, a * 128 : a * 128 + 128], da_[128:256, a * 128 : a * 128 + 128])
+        dpk[2 * a] = e.astype(B16)
+        dpk[2 * a + 1] = o.astype(B16)
+
+    mine_t = p.zl * 2 + x
+    crow = pl.ds(pl.multiple_of(c * 128, 128), 128)
+    for h, u in enumerate(UNITS):
+        mail.send(dpk.at[h], dor.at[mine_t, crow], rdo.at[p.u], (seg * 8 + u, y), p.u != u)
+
+        @pl.when(p.u == u)
+        def _(h=h):
+            dor[mine_t, crow] = dpk[h]
+
+    ffn_sum.over_x()
+    gwo[...] = dot(dh.T.astype(B16), attn[:, pl.ds(pl.multiple_of(y * 384, 128), 384)]).astype(B16)
+    out_sum.cores()
+    mail.got(fr, rsy.at[3], p.ny)
+    sums = [jnp.zeros((1, 768), F32)] * 4
+    for par in range(2):
+        at = pl.ds(pl.multiple_of(par * 128 + y * 64, 64), 64)
+        to = slice(par * 64, par * 64 + 64)
+        dh_s[to] = facc[at]
+        own = (dacc[at], ys[at].astype(F32) + yr[at].astype(F32), facc[at], dys[at].astype(F32))
+        sums = [total + jnp.sum(v, axis=0, keepdims=True) for total, v in zip(sums, own)]
+        fo[to] = hid[at] + fo[to] + fr[to].astype(F32) + row(bd_ref)
+    back = mixed((128, 128), 1, 0)
+    lout[...] = dot(back, fo[...].astype(B16)).astype(B16)
+    for i in range(4):
+        vb1[0, i : i + 1] = sums[i]
+    for half in range(2):
+
+        @pl.when(y == half)
+        def _(half=half):
+            for k in range(2):
+                vb1[0, 4 + 2 * half + k : 5 + 2 * half + k] = buph[:, k * 768 : k * 768 + 768]
+
+    early = Total(p, mail, vb1, vr1, rv1)
+    late = Total(p, mail, vb2, vr2, rv2)
+    early.start(0)
+
+    def prepare():
+        for i in range(8):
+            pl.when(p.u != i)(lambda i=i: mail.got(dor.at[i // 2, (i % 2) * 128 : (i % 2) * 128 + 128], rdo.at[i], p.nx))
+        low = iota((256, 128), 1) < 64
+        for t in range(4):
+            d = dor[t].astype(F32)
+            doa[t, 0:256] = jnp.where(low, d, 0.0).astype(B16)
+            doa[t, 256:512] = jnp.where(low, pltpu.roll(d, 64, 1), 0.0).astype(B16)
+            prod = d.T * ot[t]
+            delta[t, :, 0:256] = jnp.sum(prod[:64], axis=0, keepdims=True)
+            delta[t, :, 256:512] = jnp.sum(prod[64:], axis=0, keepdims=True)
+            kt[t + 2] = ka[t + 2].astype(F32).T.astype(B16)
+        dqt[...] = jnp.zeros_like(dqt)
+
+    pl.when(p.unit)(prepare)
+
+    def score_grads(cc, q, do, st, lse_row, delta_row):
+        pr = jnp.exp(st - lse_row)
+        ds = (pr * (dot_nt(va[cc], do) - delta_row)).astype(B16)
+        dva[...] += dot(pr.astype(B16), do)
+        dka[...] += dot(ds, q)
+        return dot(kt[cc], ds)
+
+    def clear():
+        dka[...] = jnp.zeros_like(dka)
+        dva[...] = jnp.zeros_like(dva)
+
+    @pl.when(second)
+    def _():
+        for h in range(2):
+            kt[h] = ka[h].astype(F32).T.astype(B16)
+
+        def chunk(cc, _):
+            clear()
+
+            def step(t, _):
+                q, do = qa[t, farcols], doa[t, farcols]
+                dqt[t, :, farcols] += score_grads(cc, q, do, dot_nt(ka[cc], q), lse[t, :, farcols], delta[t, :, farcols])
+                return 0
+
+            lax.fori_loop(0, 4, step, 0)
+            low = iota((512, 128), 1) < 64
+            pack = jnp.where(low, dka[...], pltpu.roll(dva[...], 64, 1)).astype(B16)
+            dfs[2 * cc] = pack[:256]
+            dfs[2 * cc + 1] = pack[256:]
+            return 0
+
+        lax.fori_loop(0, 2, chunk, 0)
+
+    mail.send(dfs, dfr, rdf.at[0], p.far, second)
+
+    def near(t):
+        clear()
+        q, do = qa[t], doa[t]
+        dqt[t] += score_grads(t + 2, q, do, causal(dot_nt(ka[t + 2], q)), lse[t], delta[t])
+        if t < 3:
+
+            def step(tq, _):
+                q, do = qa[tq], doa[tq]
+                dqt[tq] += score_grads(t + 2, q, do, dot_nt(ka[t + 2], q), lse[tq], delta[tq])
+                return 0
+
+            lax.fori_loop(t + 1, 4, step, 0)
+        dtt[64:128, t * 512 : t * 512 + 512] = dka[...].T[:64].astype(B16)
+        dtt[128:192, t * 512 : t * 512 + 512] = dva[...].T[:64].astype(B16)
+
+    def add_far(t):
+        rows = dfr[t].astype(F32).T
+        at = pl.ds(pl.multiple_of(t * 512 + p.parity * 256, 256), 256)
+        dtt[64:128, at] = (dtt[64:128, at].astype(F32) + rows[:64]).astype(B16)
+        dtt[128:192, at] = (dtt[128:192, at].astype(F32) + rows[64:]).astype(B16)
+
+    out_sum.over_x()
+    early.finish(0)
+    early.start(1)
+    pl.when(p.unit)(lambda: near(0))
+    ffn_sum.over_z(1)
+    early.finish(1)
+    early.start(2)
+    pl.when(p.unit)(lambda: near(1))
+    ffn_sum.over_z(2)
+    early.finish(2)
+    early.start(3)
+    pl.when(p.unit)(lambda: near(2))
+    pl.when(p.unit)(lambda: near(3))
+    early.finish(3)
+    early.start(4)
+
+    @pl.when(first)
+    def _():
+        mail.got(dfr, rdf.at[0], p.far)
+        for t in range(4):
+            add_far(t)
+
+    @pl.when(p.unit)
+    def _():
+        for t in range(4):
+            dtt[0:64, t * 512 : t * 512 + 512] = (dqt[t, 0:64] * 0.125).astype(B16)
+            for k in range(3):
+                e = dtt[k * 64 : k * 64 + 64, t * 512 : t * 512 + 256].astype(F32)
+                o = dtt[k * 64 : k * 64 + 64, t * 512 + 256 : t * 512 + 512].astype(F32)
+                packs[t, k] = jnp.concatenate([e, o], axis=0).T.astype(B16)
+
+    for t in range(4):
+        for cc in range(2):
+            u = t * 2 + cc
+            mail.send(packs.at[t, :, cc * 128 : cc * 128 + 128], dqr.at[p.hl], rdq.at[p.hl], (seg * 8 + u, y), both(p.unit, p.u != u))
+
+            @pl.when(both(p.unit, p.u == u))
+            def _(t=t, cc=cc):
+                dqr[p.hl] = packs[t, :, cc * 128 : cc * 128 + 128]
+
+    spread = Spread(p, mail, wag, rag, True)
+
+    @pl.when(p.unit)
+    def _():
+        dw = dot(dtt[...], ns[...].reshape(2048, 768))
+        bias = dot_nt(jnp.ones((16, 2048), B16), dtt[...])
+        for h in range(2):
+            wms[h, 0:96] = dw[h * 96 : h * 96 + 96].astype(B16)
+            wms[h, 96:112, 0:192] = bias.astype(B16)
+            wms[h, 96:112, 192:768] = jnp.zeros((16, 576), B16)
+
+    mail.send(wms.at[1 - seg], wmr, rwm.at[0], p.far, p.unit)
+    ffn_sum.over_z(3)
+    for k in range(1, 4):
+        out_sum.over_z(k)
+
+    for h, u in enumerate(UNITS):
+        pl.when(p.u != u)(lambda h=h: mail.got(dqr.at[h], rdq.at[h], p.nx))
+    for k in range(3):
+        for a in range(3):
+            e, o = halves(dqr[2 * a, k].astype(F32), dqr[2 * a + 1, k].astype(F32))
+            col = slice(a * 128, a * 128 + 128)
+            dall[k, 0:128, col] = e.astype(B16)
+            dall[k, 128:256, col] = o.astype(B16)
+    facc[...] = dot_nt(dall[0], wq_ref[0]) + dot_nt(dall[1], wq_ref[1]) + dot_nt(dall[2], wq_ref[2])
+    for par in range(2):
+        dns[par * 64 : par * 64 + 64] = facc[pl.ds(pl.multiple_of(par * 128 + (1 - y) * 64, 64), 64)].astype(B16)
+    mail.send(dns, dnr, rdn.at[0], p.ny)
+
+    @pl.when(p.unit)
+    def _():
+        mail.got(wmr, rwm.at[0], p.far)
+        wag[p.s] = (wms[seg].astype(F32) + wmr[...].astype(F32)).astype(B16)
+
+    spread.first()
+    o_total = out_sum.result()
+    woag[p.s] = o_total.astype(B16)
+    spread_out = Spread(p, mail, woag, rwo, False)
+    spread_out.first()
+    z1, inv1 = norm_parts(xs[b].astype(F32))
+    mail.got(dnr, rdn.at[0], p.ny)
+    own = [facc[pl.ds(pl.multiple_of(par * 128 + y * 64, 64), 64)] for par in range(2)]
+    dn1 = jnp.concatenate(own, axis=0) + dnr[...].astype(F32)
+    vb2[0] = jnp.zeros((8, 768), F32)
+    vb2[0, 0:1] = jnp.sum(dn1 * z1, axis=0, keepdims=True)
+    vb2[0, 1:2] = jnp.sum(dn1, axis=0, keepdims=True)
+    late.start(0)
+    rest = dh_s[...] + norm_grad(z1, inv1, dn1 * row(g1_ref))
+    result = jnp.zeros((128, 768), F32)
+    for _k in range(3):
+        piece = rest.astype(B16)
+        result = result + dot(back, piece)
+        rest = rest - piece.astype(F32)
+    gin[...] = result
+    late.finish(0)
+    late.start(1)
+    total = ffn_sum.result()
+    o_up[...] = total[:, :1536]
+    o_dn[...] = total[:, 1536:]
+    late.finish(1)
+    late.start(2)
+    spread.second()
+    spread_out.second()
+    late.finish(2)
+    late.start(3)
+    e = early.finish(4)
+    for i, ref in enumerate((o_g2, o_b2, o_bo, o_bd)):
+        ref[...] = e[i : i + 1].reshape(768)
+    for i in range(4):
+        o_bup[i * 768 : i * 768 + 768] = e[4 + i : 5 + i].reshape(768)
+    spread.third()
+    spread_out.third()
+    late.finish(3)
+    late.start(4)
+    spread_out.last()
+    o_wo[...] = woag[...].reshape(768, 384).astype(F32).T
+    e = late.finish(4)
+    o_g1[...] = e[0:1].reshape(768)
+    o_b1[...] = e[1:2].reshape(768)
+    spread.last()
+    for a in range(3):
+        u0, u1 = UNITS[2 * a], UNITS[2 * a + 1]
+        col = slice(a * 128, a * 128 + 128)
+        w0 = jnp.concatenate([wag[u0, 0:96], wag[u0 + 8, 0:96]], axis=0).astype(F32)
+        w1 = jnp.concatenate([wag[u1, 0:96], wag[u1 + 8, 0:96]], axis=0).astype(F32)
+        for k in range(3):
+            at = slice(k * 64, k * 64 + 64)
+            o_wq[k, :, col] = jnp.concatenate([w0[at], w1[at]], axis=0).T
+        r0, r1 = wag[u0, 96:112].astype(F32), wag[u1, 96:112].astype(F32)
+        low = iota((16, 128), 1) < 64
+        for k in range(2):
+            at = slice(k * 128, k * 128 + 128)
+            o_bqv[k : k + 1, col] = jnp.where(low, r0[:, at], pltpu.roll(r1[:, at], 64, 1))[0:1]
+    mail.close()
+    assert mail.used <= SENDS, mail.used
+
+
+SENDS = 400
+
+
+def count_table():
+    kinds = np.array([[0, 0, 0, 0], [1, 0, 0, 0], [1, 1, 0, 0], [1, 0, 1, 0], [1, 1, 1, 1]], np.float64)
+    shared = kinds @ kinds.T
+    table = np.zeros((24, 128), np.float64)
+    low = lambda v: float(np.asarray(v, dtype=ml_dtypes.bfloat16).astype(np.float64))
+    for i in range(5):
+        for k in range(5):
+            for base, count in ((64, 1.0 + shared[i, k]), (80, shared[i, k])):
+                rest = float(np.log(count)) if count > 0 else 0.0
+                for e in range(3):
+                    table[i, base + 3 * k + e] = low(rest)
+                    rest -= low(rest)
+        table[i, 96:101] = [NEGATIVE, NEGATIVE, 0.0, NEGATIVE, NEGATIVE]
+        table[8 + i, 64 + 3 * i : 67 + 3 * i] = 1.0
+        table[16 + i, 80 + 3 * i : 83 + 3 * i] = 1.0
+        table[8 + i, 98] = table[16 + i, 98] = 1.0
+    return table.astype(np.float32)
+
+
+def vm(*shape):
+    return pltpu.VMEM(shape, B16)
+
+
+def vf(*shape):
+    return pltpu.VMEM(shape, F32)
+
+
+def dma(*shape):
+    return pltpu.SemaphoreType.DMA(shape)
+
+
+def in_vmem(count):
+    return [pl.BlockSpec(memory_space=pltpu.VMEM)] * count
+
+
+def fast(
+    layer_input, doc_ids, cotangent, ln1_gain, ln1_bias, w_qkv, bias_qv, w_out, b_out, ln2_gain, ln2_bias, w_up, b_up, w_down, b_down
+):
+    out = lambda shape, dtype=F32: jax.ShapeDtypeStruct(shape, dtype)
+    shapes = (
+        out((128, 768), B16), out((128, 768)), out((768,)), out((768,)), out((3, 768, 384)), out((2, 384)), out((384, 768)), out((768,)),
+        out((768,)), out((768,)), out((48, 1536)), out((3072,)), out((48, 1536)), out((768,)),
+    )
+    scratch = [
+        vm(4, 512, 128), vm(6, 512, 128), vm(6, 512, 128), vm(4, 512, 768), vf(4, 1, 512), vf(4, 128, 256), vm(6, 128, 128),
+        vm(768, 3072), vm(768, 384), vf(128, 768), vm(768, 384), vf(1, 384), vf(1, 1536), vf(4, 1, 512), vf(4, 128, 512),
+        vm(16, 128, 768), vf(17, 8, 128), vm(768, 3072), vm(2, 384, 768), vm(2, 128, 768), vm(12, 128, 128), vm(4, 256, 128),
+        vm(4, 256, 128), vm(4, 256, 128), vm(256, 768), vm(6, 128, 512), vf(256, 768), vm(256, 768), vm(256, 768), vm(256, 1536),
+        vm(256, 1536), vf(256, 768), vf(256, 768), vm(256, 768), vm(256, 768), vm(128, 768), vm(128, 768), vf(128, 768),
+        vm(4, 256, 128), vm(4, 512, 128), vf(4, 1, 512), vm(6, 128, 512), vf(512, 128), vf(512, 128), vf(4, 128, 512), vm(192, 2048),
+        vm(4, 256, 128), vm(4, 256, 128), vm(4, 3, 256, 128), vm(6, 3, 128, 128), vm(2, 112, 768), vm(112, 768),
+        vm(2, 4, 48, 3072), vm(4, 48, 3072), vm(4, 48, 3072), vm(2, 4, 48, 384), vm(4, 48, 384), vm(4, 48, 384), vm(4, 48, 384),
+        vm(4, 48, 384), vm(3, 256, 384), vm(128, 768), vm(128, 768),
+        vf(5, 8, 768), vf(5, 8, 768), vf(5, 8, 768), vf(5, 8, 768), vm(16, 112, 768), vm(16, 48, 384),
+        dma(SENDS), dma(3, 16), dma(3, 16), dma(16), dma(16), dma(12), dma(2), dma(4), dma(8), dma(2, 4), dma(4), dma(4), dma(2, 4), dma(4),
+        dma(4), dma(1), dma(6), dma(1), dma(16), dma(16), dma(1), dma(5), dma(5),
+    ]
+    args = (
+        layer_input, doc_ids, cotangent, ln1_gain, ln1_bias, w_qkv.transpose(1, 0, 2), bias_qv, w_out, b_out, ln2_gain, ln2_bias, w_up,
+        b_up, w_down.T, b_down, jnp.asarray(count_table()),
+    )
+    outs = pl.pallas_call(
+        kernel, out_shape=shapes, in_specs=in_vmem(len(args)), out_specs=tuple(in_vmem(len(shapes))), scratch_shapes=scratch,
+        compiler_params=pltpu.CompilerParams(collective_id=0, has_side_effects=True, vmem_limit_bytes=LIMIT),
+    )(*args)
+    outs = list(outs)
+    outs[4] = outs[4].transpose(1, 0, 2)
+    outs[12] = outs[12].T
+    return tuple(outs)
 
 
 def from_behind(value, axis, by):
@@ -465,6 +1437,7 @@
         P("head", "seq"),
         P(),
     )
+    small = mesh.shape["seq"] == 16 and mesh.shape["head"] == 2
     return jax.shard_map(
-        per_device, mesh=mesh, in_specs=in_specs, out_specs=out_specs, check_vma=False
-    )
+        fast if small else per_device, mesh=mesh, in_specs=in_specs, out_specs=out_specs, check_vma=False
+    )

time: 994 us -> 207 us (0.21)
  the two profiles are of different devices: /device:TPU:0 before, /device:TPU:16 now
where the time goes in v2:
time: 207 us
  Pallas kernels  190 us (92%)
  local copies, waits for them, and re-layouts  16.1 us (8%)
    pallas_call x1, Pallas kernels, fast(): pl.pallas_call(kernel, out_shape=shapes, in_specs=in_vmem(len(args)), out...  190 us
    unnamed x32, local copies, waits for them, and re-layouts  16.1 us

profile of v2, /device:TPU:16, one launch (start us, length us, event | category | flops | bytes accessed | tf_op | source)
XLA Modules:
  0.0 206.9 jit_solution(2557647113321426762)
XLA Ops:
  0.7 190.1 %shard_map.263 = (bf16[128,768]{1,0:T(8,128)(2,1)}, f32[128,768]{1,0:T(8,128)}, f32[768]{0:T(1024)}, f32[768]{0:T(1024)}, f32[3,768,384]{2,1,0:T(8,128)}, /*inde...) custom-call(bf16[128,768]{1,0:T(8,128)(2,1)} %x_ref.1, ...), custom_call_target="tpu_custom_call" | custom-call | tf_op jit(solution)/shard_map/pallas_call | solution.py:979
  190.8 1.6 copy.44
  192.4 1.8 copy.45
  194.2 1.3 copy.46
  195.4 1.3 copy.47
  196.7 0.0 copy-start.8
  196.7 4.1 %copy.48 = f32[768,3,384]{2,0,1:T(8,128)} copy(f32[768,3,384]{2,0,1:T(8,128)} %bitcast.4) | data formatting | bytes 7077888
  200.8 0.0 copy-done.8
  200.8 0.0 copy-start.7
  200.8 0.0 copy-start.6
  200.8 0.0 copy-start.5
  200.8 0.0 copy-start.2
  200.9 0.0 copy-start.3
  200.9 0.0 copy-start.1
  200.9 0.6 copy.49
  201.5 0.0 copy-done
  201.5 0.0 copy-start.4
  201.5 1.0 copy.50
  202.5 0.0 copy-done.7
  202.5 0.6 copy.51
  203.1 0.0 copy-done.6
  203.1 0.6 copy.52
  203.7 0.0 copy-done.5
  203.7 0.6 copy.53
  204.3 0.0 copy-done.2
  204.3 0.7 copy.54
  205.0 0.0 copy-done.3
  205.0 0.6 copy.55
  205.6 0.0 copy-done.1
  205.6 0.7 copy.56
  206.3 0.0 copy-done.4
  206.3 0.6 copy.57
  (1 shorter events, 0.0 us)
Async XLA Ops:
  196.7 4.1 %copy-start.8 = (f32[2,384]{1,0:T(2,128)S(1)}, f32[2,384]{1,0:T(2,128)}, u32[]{:S(2)}) copy-start(f32[2,384]{1,0:T(2,128)} %get-tuple-element.61) | copy-start | bytes 9220
  196.7 4.7 %copy-start = (f32[384,768]{1,0:T(8,128)S(1)}, f32[384,768]{1,0:T(8,128)}, u32[]{:S(2)}) copy-start(f32[384,768]{1,0:T(8,128)} %get-tuple-element.62) | copy-start | bytes 3538948
  200.8 1.6 copy-start.7
  200.8 2.2 %copy-start.6 = (f32[768]{0:T(1024)S(1)}, f32[768]{0:T(1024)}, u32[]{:S(2)}) copy-start(f32[768]{0:T(1024)} %get-tuple-element.64) | copy-start | bytes 9220
  200.8 2.8 %copy-start.5 = (f32[768]{0:T(1024)S(1)}, f32[768]{0:T(1024)}, u32[]{:S(2)}) copy-start(f32[768]{0:T(1024)} %get-tuple-element.65) | copy-start | bytes 9220
  200.8 3.4 %copy-start.2 = (f32[48,1536]{1,0:T(8,128)S(1)}, f32[48,1536]{1,0:T(8,128)}, u32[]{:S(2)}) copy-start(f32[48,1536]{1,0:T(8,128)} %get-tuple-element.66) | copy-start | bytes 884740
  200.9 4.1 %copy-start.3 = (f32[3072]{0:T(1024)S(1)}, f32[3072]{0:T(1024)}, u32[]{:S(2)}) copy-start(f32[3072]{0:T(1024)} %get-tuple-element.67) | copy-start | bytes 36868
  200.9 4.7 %copy-start.1 = (f32[48,1536]{1,0:T(8,128)S(1)}, f32[48,1536]{1,0:T(8,128)}, u32[]{:S(2)}) copy-start(f32[48,1536]{1,0:T(8,128)} %get-tuple-element.40) | copy-start | bytes 884740
  201.5 4.8 %copy-start.4 = (f32[768]{0:T(1024)S(1)}, f32[768]{0:T(1024)}, u32[]{:S(2)}) copy-start(f32[768]{0:T(1024)} %get-tuple-element.69) | copy-start | bytes 9220

commit v3 on v2

--- a/solution.py
+++ b/solution.py
@@ -247,38 +247,36 @@
         return total
 
 
-class Slots:
-    def __init__(self, ref, base):
-        self.ref, self.base = ref, base
-
-    def span(self, i):
-        return pl.ds(pl.multiple_of(self.base + i * 48, 16), 48)
-
-    @property
-    def at(self):
-        return self
-
-    def __getitem__(self, i):
-        return self.ref.at[self.span(i)]
-
-    def __setitem__(self, i, value):
-        self.ref[self.span(i)] = value
-
-
 class Total:
-    def __init__(self, p, mail, buf, rec, sems):
-        self.mail, self.buf, self.rec, self.sems = mail, buf, rec, sems
-        self.peers = (p.nc, p.nx, p.nz, p.far, p.ny)
-
-    def start(self, i):
-        self.mail.send(self.buf.at[i], self.rec.at[i], self.sems.at[i], self.peers[i])
-
-    def finish(self, i):
-        self.mail.got(self.rec.at[i], self.sems.at[i], self.peers[i])
-        new = self.buf[i] + self.rec[i]
-        if i < 4:
-            self.buf[i + 1] = new
-        return new
+    def __init__(self, p, mail, one, two, sem_one, sem_two):
+        self.p, self.mail, self.one, self.two, self.sem_one, self.sem_two = p, mail, one, two, sem_one, sem_two
+        self.k = (p.x * 2 + p.c) * 2 + p.y
+
+    def start(self):
+        p = self.p
+        for i in range(1, 4):
+            dev = (sid((p.z + i) % 4, p.x, p.c), p.y)
+            self.mail.send(self.one.at[p.z], self.one.at[p.z], self.sem_one.at[p.z], dev)
+
+    def middle(self):
+        p = self.p
+        for i in range(1, 4):
+            zz = (p.z + i) % 4
+            self.mail.got(self.one.at[zz], self.sem_one.at[zz], p.nx)
+        self.two[self.k] = self.one[0] + self.one[1] + self.one[2] + self.one[3]
+        for i in range(1, 8):
+            xx = 1 - p.x if i & 4 else p.x
+            cc = 1 - p.c if i & 2 else p.c
+            yy = 1 - p.y if i & 1 else p.y
+            self.mail.send(self.two.at[self.k], self.two.at[self.k], self.sem_two.at[self.k], (sid(p.z, xx, cc), yy))
+
+    def finish(self):
+        for i in range(8):
+            pl.when(self.k != i)(lambda i=i: self.mail.got(self.two.at[i], self.sem_two.at[i], self.p.nx))
+        out = self.two[0]
+        for i in range(1, 8):
+            out = out + self.two[i]
+        return out
 
 
 def mixed(shape, dim_to, dim_from):
@@ -288,12 +286,12 @@
 
 def kernel(
     x_ref, doc_ref, cot_ref, g1_ref, b1_ref, wq_ref, bqv_ref, wo_own, bo_ref, g2_ref, b2_ref, wup_ref, bup_ref, wdn_ref, bd_ref, tab_ref,
-    lout, gin, o_g1, o_b1, o_wq, o_bqv, o_wo, o_bo, o_g2, o_b2, o_up, o_bup, o_dn, o_bd,
-    qa, ka, va, ns, lse, ot, dpk, grads, gwo, dh_s, wqh, bqh, buph, msc, asc,
+    lout, gin, wag, woag, o_ud, o_tot,
+    qa, ka, va, ns, lse, ot, dpk, gwo, dh_s, wqh, bqh, buph, msc, asc,
     xs, docs, wb, wo, dyp, orecv, osend, kvs, kvf, attn, vt, hid, n2s, dys, acts, dpre, facc, dacc, ys, yr, fs, fr, fo,
-    dor, doa, delta, kt, dka, dva, dqt, dtt, dfs, dfr, packs, dqr, wms, wmr, gc, gxr, gzr, hc, hxs, hxr, hzs, hzr, dall, dns, dnr,
-    vb1, vr1, vb2, vr2, wag, woag,
-    ss, rsx, rsc, rsd, rsw, rso, rsf, rsy, rdo, rgc, rgx, rgz, rhc, rhx, rhz, rdf, rdq, rwm, rag, rwo, rdn, rv1, rv2,
+    dor, doa, delta, kt, dka, dva, dqt, dtt, dfs, dfr, packs, dqr, wms, wmr, n2t, dyt, ga, gb, gd, ge, ra, rb, gxr, gzr,
+    hc, hxs, hxr, hzs, hzr, dall, dns, dnr, vb1, vr1, vb2, vr2,
+    ss, rsx, rsc, rsd, rsw, rso, rsf, rsy, rdo, rga, rgx, rgz, rhc, rhx, rhz, rdf, rdq, rwm, rag, rwo, rdn, rv1, rv2, rv3, rv4,
 ):
     p = Place()
     mail = Mail(ss)
@@ -309,6 +307,9 @@
     turn_odd = jnp.where(iota((128, 128), 0) == 2 * (iota((128, 128), 1) & 63) + 1, 1.0, 0.0).astype(B16)
     doc8 = jnp.broadcast_to(doc_row, (8, 128)).astype(B16)
     docs[b] = jnp.where(iota((8, 128), 0) == 0, dot(doc8, turn), dot(doc8, turn_odd))
+    wrow = pl.ds(pl.multiple_of(p.s * 48, 16), 48)
+    wb[wrow, 0:1536] = wup_ref[...]
+    wb[wrow, 1536:3072] = wdn_ref[...]
     p.meet()
 
     dims = ("x", "y", "z")
@@ -332,6 +333,17 @@
     for src in (0, 14, 15):
         for dev in p.cube():
             mail.send(docs.at[src], docs.at[src], rsd.at[src], dev, cond=b == src)
+
+    def rows_of(s):
+        return wb.at[pl.ds(pl.multiple_of(s * 48, 16), 48), :]
+
+    def give(s, dev, cond=None):
+        mail.send(rows_of(s), rows_of(s), rsw.at[s], dev, cond)
+
+    give(p.s, (sid((z + 1) % 4, x, c), y), z <= 2)
+    give(p.s, (sid((z + 3) % 4, x, c), y), z >= 1)
+    give(p.s, p.nx)
+    give(p.s, p.nc)
 
     pair_cols = pl.ds(pl.multiple_of(p.hl // 2 * 128, 128), 128)
     for odd in range(2):
@@ -367,9 +379,6 @@
         def _(half=half):
             buph[...] = bup_ref[half * 1536 : half * 1536 + 1536].reshape(1, 1536)
 
-    wrow = pl.ds(pl.multiple_of(p.s * 48, 16), 48)
-    wb[wrow, 0:1536] = wup_ref[...]
-    wb[wrow, 1536:3072] = wdn_ref[...]
     wo[y] = wo_own[...]
 
     def qkv(i):
@@ -401,30 +410,6 @@
         at = (b + sum(flips)) // 2
         pl.when(p.unit)(lambda: qkv(at))
 
-    for k in range(3):
-        f = [p.fb[d] for d in order[k]]
-        seen(k, b + f[0])
-        pass_on(k, b + f[0], nbr[order[k][1]])
-        pass_on(k, b + f[0], nbr[order[k][2]])
-    for k in range(3):
-        f = [p.fb[d] for d in order[k]]
-        for blk in (b + f[1], b + f[1] + f[0]):
-            seen(k, blk)
-            pass_on(k, blk, nbr[order[k][2]])
-
-    def rows_of(s):
-        return wb.at[pl.ds(pl.multiple_of(s * 48, 16), 48), :]
-
-    def give(s, dev, cond=None):
-        mail.send(rows_of(s), rows_of(s), rsw.at[s], dev, cond)
-
-    give(p.s, (sid((z + 1) % 4, x, c), y), z <= 2)
-    give(p.s, (sid((z + 3) % 4, x, c), y), z >= 1)
-    give(p.s, p.nx)
-    give(p.s, p.nc)
-    mail.send(wo.at[y], wo.at[y], rsy.at[0], p.ny)
-    mail.send(dyp.at[y], dyp.at[y], rsy.at[1], p.ny)
-
     def chain(d):
         up, dn = (z - d + 4) % 4, (z + d) % 4
         has_up, has_dn = z >= d, z <= 3 - d
@@ -440,16 +425,39 @@
         give(sd, p.nx, has_dn)
         give(sd, p.nc, has_dn)
 
+    flips = [[p.fb[d] for d in order[k]] for k in range(3)]
     for k in range(3):
-        f = [p.fb[d] for d in order[k]]
-        for blk in (b + f[2], b + f[2] + f[0], b + f[2] + f[1], b + f[2] + f[1] + f[0]):
-            seen(k, blk)
-    for flips in ((), (fx,), (fz,), (fx, fz)):
-        qkv_of(*flips)
-    for flips in ((), (fx,), (fz,), (fx, fz)):
-        from_core(b + fc + sum(flips))
-        from_core(b + fc + sum(flips) + fy)
-        qkv_of(fc, *flips)
+        f = flips[k]
+        seen(k, b + f[0])
+        pass_on(k, b + f[0], nbr[order[k][1]])
+        pass_on(k, b + f[0], nbr[order[k][2]])
+        seen(k, b + f[1])
+        pass_on(k, b + f[1], nbr[order[k][2]])
+        seen(k, b + f[2])
+    mail.send(wo.at[y], wo.at[y], rsy.at[0], p.ny)
+    mail.send(dyp.at[y], dyp.at[y], rsy.at[1], p.ny)
+    qkv_of()
+    for k in range(3):
+        f = flips[k]
+        seen(k, b + f[1] + f[0])
+        pass_on(k, b + f[1] + f[0], nbr[order[k][2]])
+    for k in range(3):
+        f = flips[k]
+        seen(k, b + f[2] + f[0])
+        seen(k, b + f[2] + f[1])
+    qkv_of(fx)
+    qkv_of(fz)
+    from_core(b + fc)
+    from_core(b + fc + fy)
+    qkv_of(fc)
+    for k in range(3):
+        seen(k, b + fx + fy + fz)
+    chain(1)
+    qkv_of(fx, fz)
+    for more in ((fx,), (fz,), (fx, fz)):
+        from_core(b + fc + sum(more))
+        from_core(b + fc + sum(more) + fy)
+        qkv_of(fc, *more)
     for src in (0, 14, 15):
         pl.when(b != src)(lambda src=src: mail.got(docs.at[src], rsd.at[src], p.nx))
 
@@ -572,15 +580,13 @@
         pl.when(first)(functools.partial(conclude, t))
         deliver(t, first)
         if t == 1:
-            chain(1)
-        if t == 3:
             chain(2)
+    chain(3)
     pl.when(second)(far_ready)
     for t in range(4):
         pl.when(second)(functools.partial(far_attention, t))
         pl.when(second)(functools.partial(conclude, t))
         deliver(t, second)
-    chain(3)
     for zq in range(4):
         s = sid(zq, 1 - x, c)
         mail.got(rows_of(s), rsw.at[s], p.nx)
@@ -611,7 +617,7 @@
     facc[...] = jnp.zeros_like(facc)
     dacc[...] = jnp.zeros_like(dacc)
     k0 = 0.7978845608028654
-    vb1[0] = jnp.zeros((8, 768), F32)
+    vb1[z] = jnp.zeros((8, 768), F32)
 
     def ffn_step(i, _):
         cols = pl.ds(pl.multiple_of(i * 256, 256), 256)
@@ -640,21 +646,50 @@
         fs[par * 64 : par * 64 + 64] = facc[pl.ds(pl.multiple_of(par * 128 + (1 - y) * 64, 64), 64)].astype(B16)
     mail.send(fs, fr, rsy.at[3], p.ny)
 
-    n2t = n2s[...].astype(F32).T.astype(B16)
-    dyt = dys[...].astype(F32).T.astype(B16)
-
-    def grad_step(i, _):
-        cols = pl.ds(pl.multiple_of(i * 256, 256), 256)
-        dcols = pl.ds(pl.multiple_of(1536 + i * 256, 256), 256)
-        grads[:, cols] = dot(n2t, dpre[:, cols]).astype(B16)
-        grads[:, dcols] = dot(dyt, acts[:, cols]).astype(B16)
-        return 0
-
-    lax.fori_loop(0, 6, grad_step, 0)
-    mail.close()
-    ffn_sum = Reduce(p, mail, grads, gc, Slots(wb, 0), gxr, Slots(wb, 192), gzr, rgc, rgx, rgz)
+    n2t[...] = n2s[...].astype(F32).T.astype(B16)
+    dyt[...] = dys[...].astype(F32).T.astype(B16)
+
+    def owners(ref, xx, cc):
+        at = [pl.ds(pl.multiple_of(sid(zz, xx, cc) * 48, 16), 48) for zz in range(4)]
+        up = jnp.concatenate([n2t[i] for i in at], axis=0)
+        dn = jnp.concatenate([dyt[i] for i in at], axis=0)
+
+        def step(i, _):
+            cols = pl.ds(pl.multiple_of(i * 256, 256), 256)
+            dcols = pl.ds(pl.multiple_of(1536 + i * 256, 256), 256)
+            u = dot(up, dpre[:, cols]).astype(B16)
+            d = dot(dn, acts[:, cols]).astype(B16)
+            for zz in range(4):
+                ref[zz, :, cols] = u[zz * 48 : zz * 48 + 48]
+                ref[zz, :, dcols] = d[zz * 48 : zz * 48 + 48]
+            return 0
+
+        lax.fori_loop(0, 6, step, 0)
+
     out_sum = Reduce(p, mail, gwo, hc, hxs, hxr, hzs, hzr, rhc, rhx, rhz)
-    ffn_sum.cores()
+
+    def ffn_over_x(k):
+        zz = (z + k) % 4
+        gb[zz] = (gb[zz].astype(F32) + ra[zz].astype(F32)).astype(B16)
+        mail.send(gb.at[zz], gxr.at[zz], rgx.at[zz], p.nx)
+
+    def ffn_column(zz):
+        mail.got(gxr.at[zz], rgx.at[zz], p.nx)
+        return ge[zz].astype(F32) + rb[zz].astype(F32) + gxr[zz].astype(F32)
+
+    def ffn_over_z(k):
+        zz = (z + k) % 4
+        ge[zz] = ffn_column(zz).astype(B16)
+        mail.send(ge.at[zz], gzr.at[z], rgz.at[z], (sid(zz, x, c), y))
+
+    owners(ga, 1 - x, 1 - c)
+    mail.send(ga, ra, rga.at[0], p.nc)
+    owners(gb, 1 - x, c)
+    mail.got(ra, rga.at[0], p.nc)
+    ffn_over_x(2)
+    owners(gd, x, 1 - c)
+    mail.send(gd, rb, rga.at[1], p.nc)
+    owners(ge, x, c)
     mail.got(yr, rsy.at[2], p.ny)
     dn2 = ys[...].astype(F32) + yr[...].astype(F32)
     z2, inv2 = norm_parts(hid[...])
@@ -676,7 +711,9 @@
         def _(h=h):
             dor[mine_t, crow] = dpk[h]
 
-    ffn_sum.over_x()
+    for k in (1, 3, 0):
+        ffn_over_x(k)
+    mail.got(rb, rga.at[1], p.nc)
     gwo[...] = dot(dh.T.astype(B16), attn[:, pl.ds(pl.multiple_of(y * 384, 128), 384)]).astype(B16)
     out_sum.cores()
     mail.got(fr, rsy.at[3], p.ny)
@@ -691,17 +728,17 @@
     back = mixed((128, 128), 1, 0)
     lout[...] = dot(back, fo[...].astype(B16)).astype(B16)
     for i in range(4):
-        vb1[0, i : i + 1] = sums[i]
+        vb1[z, i : i + 1] = sums[i]
     for half in range(2):
 
         @pl.when(y == half)
         def _(half=half):
             for k in range(2):
-                vb1[0, 4 + 2 * half + k : 5 + 2 * half + k] = buph[:, k * 768 : k * 768 + 768]
-
-    early = Total(p, mail, vb1, vr1, rv1)
-    late = Total(p, mail, vb2, vr2, rv2)
-    early.start(0)
+                vb1[z, 4 + 2 * half + k : 5 + 2 * half + k] = buph[:, k * 768 : k * 768 + 768]
+
+    early = Total(p, mail, vb1, vr1, rv1, rv2)
+    late = Total(p, mail, vb2, vr2, rv3, rv4)
+    early.start()
 
     def prepare():
         for i in range(8):
@@ -776,20 +813,14 @@
         dtt[128:192, at] = (dtt[128:192, at].astype(F32) + rows[64:]).astype(B16)
 
     out_sum.over_x()
-    early.finish(0)
-    early.start(1)
+    ffn_over_z(2)
     pl.when(p.unit)(lambda: near(0))
-    ffn_sum.over_z(1)
-    early.finish(1)
-    early.start(2)
+    ffn_over_z(1)
+    early.middle()
     pl.when(p.unit)(lambda: near(1))
-    ffn_sum.over_z(2)
-    early.finish(2)
-    early.start(3)
+    ffn_over_z(3)
     pl.when(p.unit)(lambda: near(2))
     pl.when(p.unit)(lambda: near(3))
-    early.finish(3)
-    early.start(4)
 
     @pl.when(first)
     def _():
@@ -827,7 +858,6 @@
             wms[h, 96:112, 192:768] = jnp.zeros((16, 576), B16)
 
     mail.send(wms.at[1 - seg], wmr, rwm.at[0], p.far, p.unit)
-    ffn_sum.over_z(3)
     for k in range(1, 4):
         out_sum.over_z(k)
 
@@ -858,10 +888,10 @@
     mail.got(dnr, rdn.at[0], p.ny)
     own = [facc[pl.ds(pl.multiple_of(par * 128 + y * 64, 64), 64)] for par in range(2)]
     dn1 = jnp.concatenate(own, axis=0) + dnr[...].astype(F32)
-    vb2[0] = jnp.zeros((8, 768), F32)
-    vb2[0, 0:1] = jnp.sum(dn1 * z1, axis=0, keepdims=True)
-    vb2[0, 1:2] = jnp.sum(dn1, axis=0, keepdims=True)
-    late.start(0)
+    vb2[z] = jnp.zeros((8, 768), F32)
+    vb2[z, 0:1] = jnp.sum(dn1 * z1, axis=0, keepdims=True)
+    vb2[z, 1:2] = jnp.sum(dn1, axis=0, keepdims=True)
+    late.start()
     rest = dh_s[...] + norm_grad(z1, inv1, dn1 * row(g1_ref))
     result = jnp.zeros((128, 768), F32)
     for _k in range(3):
@@ -869,32 +899,37 @@
         result = result + dot(back, piece)
         rest = rest - piece.astype(F32)
     gin[...] = result
-    late.finish(0)
-    late.start(1)
-    total = ffn_sum.result()
-    o_up[...] = total[:, :1536]
-    o_dn[...] = total[:, 1536:]
-    late.finish(1)
-    late.start(2)
     spread.second()
     spread_out.second()
-    late.finish(2)
-    late.start(3)
-    e = early.finish(4)
-    for i, ref in enumerate((o_g2, o_b2, o_bo, o_bd)):
-        ref[...] = e[i : i + 1].reshape(768)
-    for i in range(4):
-        o_bup[i * 768 : i * 768 + 768] = e[4 + i : 5 + i].reshape(768)
+    late.middle()
+    total = ffn_column(z)
+    for k in range(1, 4):
+        zz = (z + k) % 4
+        mail.got(gzr.at[zz], rgz.at[zz], p.nx)
+        total = total + gzr[zz].astype(F32)
+    o_ud[...] = total
+    o_tot[0] = early.finish()
     spread.third()
     spread_out.third()
-    late.finish(3)
-    late.start(4)
+    o_tot[1] = late.finish()
     spread_out.last()
+    spread.last()
+    mail.close()
+    assert mail.used <= SENDS, mail.used
+
+
+def write_out(lout, gin, wag, woag, ud, tot, o_l, o_g, o_g1, o_b1, o_wq, o_bqv, o_wo, o_bo, o_g2, o_b2, o_up, o_bup, o_dn, o_bd):
+    o_l[...] = lout[...]
+    o_g[...] = gin[...]
+    o_up[...] = ud[:, :1536]
+    o_dn[...] = ud[:, 1536:]
+    for i, ref in enumerate((o_g2, o_b2, o_bo, o_bd)):
+        ref[...] = tot[0, i : i + 1].reshape(768)
+    for i in range(4):
+        o_bup[i * 768 : i * 768 + 768] = tot[0, 4 + i : 5 + i].reshape(768)
+    o_g1[...] = tot[1, 0:1].reshape(768)
+    o_b1[...] = tot[1, 1:2].reshape(768)
     o_wo[...] = woag[...].reshape(768, 384).astype(F32).T
-    e = late.finish(4)
-    o_g1[...] = e[0:1].reshape(768)
-    o_b1[...] = e[1:2].reshape(768)
-    spread.last()
     for a in range(3):
         u0, u1 = UNITS[2 * a], UNITS[2 * a + 1]
         col = slice(a * 128, a * 128 + 128)
@@ -908,8 +943,6 @@
         for k in range(2):
             at = slice(k * 128, k * 128 + 128)
             o_bqv[k : k + 1, col] = jnp.where(low, r0[:, at], pltpu.roll(r1[:, at], 64, 1))[0:1]
-    mail.close()
-    assert mail.used <= SENDS, mail.used
 
 
 SENDS = 400
@@ -958,28 +991,33 @@
         out((128, 768), B16), out((128, 768)), out((768,)), out((768,)), out((3, 768, 384)), out((2, 384)), out((384, 768)), out((768,)),
         out((768,)), out((768,)), out((48, 1536)), out((3072,)), out((48, 1536)), out((768,)),
     )
+    raw = (out((128, 768), B16), out((128, 768)), out((16, 112, 768), B16), out((16, 48, 384), B16), out((48, 3072)), out((2, 8, 768)))
     scratch = [
         vm(4, 512, 128), vm(6, 512, 128), vm(6, 512, 128), vm(4, 512, 768), vf(4, 1, 512), vf(4, 128, 256), vm(6, 128, 128),
-        vm(768, 3072), vm(768, 384), vf(128, 768), vm(768, 384), vf(1, 384), vf(1, 1536), vf(4, 1, 512), vf(4, 128, 512),
+        vm(768, 384), vf(128, 768), vm(768, 384), vf(1, 384), vf(1, 1536), vf(4, 1, 512), vf(4, 128, 512),
         vm(16, 128, 768), vf(17, 8, 128), vm(768, 3072), vm(2, 384, 768), vm(2, 128, 768), vm(12, 128, 128), vm(4, 256, 128),
         vm(4, 256, 128), vm(4, 256, 128), vm(256, 768), vm(6, 128, 512), vf(256, 768), vm(256, 768), vm(256, 768), vm(256, 1536),
         vm(256, 1536), vf(256, 768), vf(256, 768), vm(256, 768), vm(256, 768), vm(128, 768), vm(128, 768), vf(128, 768),
         vm(4, 256, 128), vm(4, 512, 128), vf(4, 1, 512), vm(6, 128, 512), vf(512, 128), vf(512, 128), vf(4, 128, 512), vm(192, 2048),
         vm(4, 256, 128), vm(4, 256, 128), vm(4, 3, 256, 128), vm(6, 3, 128, 128), vm(2, 112, 768), vm(112, 768),
-        vm(2, 4, 48, 3072), vm(4, 48, 3072), vm(4, 48, 3072), vm(2, 4, 48, 384), vm(4, 48, 384), vm(4, 48, 384), vm(4, 48, 384),
-        vm(4, 48, 384), vm(3, 256, 384), vm(128, 768), vm(128, 768),
-        vf(5, 8, 768), vf(5, 8, 768), vf(5, 8, 768), vf(5, 8, 768), vm(16, 112, 768), vm(16, 48, 384),
-        dma(SENDS), dma(3, 16), dma(3, 16), dma(16), dma(16), dma(12), dma(2), dma(4), dma(8), dma(2, 4), dma(4), dma(4), dma(2, 4), dma(4),
-        dma(4), dma(1), dma(6), dma(1), dma(16), dma(16), dma(1), dma(5), dma(5),
+        vm(768, 256), vm(768, 256), *[vm(4, 48, 3072)] * 8,
+        vm(2, 4, 48, 384), vm(4, 48, 384), vm(4, 48, 384), vm(4, 48, 384), vm(4, 48, 384), vm(3, 256, 384), vm(128, 768), vm(128, 768),
+        vf(4, 8, 768), vf(8, 8, 768), vf(4, 8, 768), vf(8, 8, 768),
+        dma(SENDS), dma(3, 16), dma(3, 16), dma(16), dma(16), dma(12), dma(2), dma(4), dma(8), dma(2), dma(4), dma(4), dma(2, 4), dma(4),
+        dma(4), dma(1), dma(6), dma(1), dma(16), dma(16), dma(1), dma(4), dma(8), dma(4), dma(8),
     ]
     args = (
         layer_input, doc_ids, cotangent, ln1_gain, ln1_bias, w_qkv.transpose(1, 0, 2), bias_qv, w_out, b_out, ln2_gain, ln2_bias, w_up,
         b_up, w_down.T, b_down, jnp.asarray(count_table()),
     )
-    outs = pl.pallas_call(
-        kernel, out_shape=shapes, in_specs=in_vmem(len(args)), out_specs=tuple(in_vmem(len(shapes))), scratch_shapes=scratch,
+    found = pl.pallas_call(
+        kernel, out_shape=raw, in_specs=in_vmem(len(args)), out_specs=tuple(in_vmem(len(raw))), scratch_shapes=scratch,
         compiler_params=pltpu.CompilerParams(collective_id=0, has_side_effects=True, vmem_limit_bytes=LIMIT),
     )(*args)
+    outs = pl.pallas_call(
+        write_out, out_shape=shapes, in_specs=in_vmem(len(raw)), out_specs=tuple(in_vmem(len(shapes))),
+        compiler_params=pltpu.CompilerParams(vmem_limit_bytes=LIMIT),
+    )(*found)
     outs = list(outs)
     outs[4] = outs[4].transpose(1, 0, 2)
     outs[12] = outs[12].T

time: 207 us -> 181 us (0.87)
  the two profiles are of different devices: /device:TPU:16 before, /device:TPU:27 now
where the time goes in v3:
time: 181 us
  Pallas kernels  180 us (99%)
    pallas_call x1, Pallas kernels, fast(): pl.pallas_call(kernel, out_shape=raw, in_specs=in_vmem(len(args)), out_sp...  174 us
    pallas_call x1, Pallas kernels, fast(): pl.pallas_call(write_out, out_shape=shapes, in_specs=in_vmem(len(raw)), o...  5.6 us

profile of v3, /device:TPU:27, one launch (start us, length us, event | category | flops | bytes accessed | tf_op | source)
XLA Modules:
  0.0 180.7 jit_solution(14222908756734107311)
XLA Ops:
  0.7 174.3 %shard_map.263 = (bf16[128,768]{1,0:T(8,128)(2,1)}, f32[128,768]{1,0:T(8,128)}, bf16[16,112,768]{2,1,0:T(8,128)(2,1)}, bf16[16,48,384]{2,1,0:T(8,128)(2,1)}, f32[48,3072]{1,0:T(8,128)}, /*index=5*/f32[2,8,768]{2,1,0:T(8,128)}) custom-call(bf16[128,768]{1,0:T(8,128)(2,1)} %x_ref.1, s32[128]{0:T(128)} %doc_ref.1, bf16[128,768]{1,0:T(8,128)(2,1)} %cot_ref.1, ...), custom_call_target="tpu_custom_call" | custom-call | tf_op jit(solution)/shard_map/pallas_call | solution.py:1013
  175.0 5.6 %shard_map.264 = (bf16[128,768]{1,0:T(8,128)(2,1)}, f32[128,768]{1,0:T(8,128)}, f32[768]{0:T(1024)}, f32[768]{0:T(1024)}, f32[3,768,384]{2,1,0:T(8,128)}, /*inde...) custom-call(bf16[128,768]{1,0:T(8,128)(2,1)} %get-tuple-element.34.l, ...), custom_call_target="tpu_custom_call" | custom-call | tf_op jit(solution)/shard_map/pallas_call | solution.py:1017

commit v4 on v3

--- a/solution.py
+++ b/solution.py
@@ -80,12 +80,13 @@
 
 
 class Mail:
-    def __init__(self, sems):
-        self.sems, self.used, self.sent = sems, 0, []
+    def __init__(self, sems, slots):
+        self.sems, self.slots, self.used, self.sent = sems, slots, 0, {}
 
     def send(self, src, dst, rsem, dev, cond=None):
-        k = self.used
+        k = self.used % self.slots
         self.used += 1
+        self.settle(k)
 
         def make():
             return pltpu.make_async_remote_copy(
@@ -96,7 +97,15 @@
             make().start()
         else:
             pl.when(cond)(lambda: make().start())
-        self.sent.append((cond, make))
+        self.sent[k] = (cond, make)
+
+    def settle(self, k):
+        if k in self.sent:
+            cond, make = self.sent.pop(k)
+            if cond is None:
+                make().wait_send()
+            else:
+                pl.when(cond)(lambda: make().wait_send())
 
     def got(self, dst, rsem, dev):
         pltpu.make_async_remote_copy(
@@ -104,12 +113,8 @@
         ).wait_recv()
 
     def close(self):
-        for cond, make in self.sent:
-            if cond is None:
-                make().wait_send()
-            else:
-                pl.when(cond)(lambda make=make: make().wait_send())
-        self.sent = []
+        for k in range(self.slots):
+            self.settle(k)
 
 
 def both(*terms):
@@ -173,21 +178,25 @@
     def first(self):
         p = self.p
         has = self.has(p.z, p.x, p.c)
-        for k in range(1, 4):
-            self.go(p.s, (sid((p.z + k) % 4, p.x, p.c), p.y), has)
-        self.go(p.s, p.nx, has)
-        self.go(p.s, p.nc, has)
+        for dev in (p.far, p.nz, p.nx, p.nc):
+            self.go(p.s, dev, has)
+
+    def onward(self, zz, devs):
+        s, has = sid(zz, self.p.x, self.p.c), self.has(zz, self.p.x, self.p.c)
+        self.take(s, has)
+        for dev in devs:
+            self.go(s, dev, has)
 
     def second(self):
         p = self.p
-        for k in range(1, 4):
-            zz = (p.z + k) % 4
-            s, has = sid(zz, p.x, p.c), self.has(zz, p.x, p.c)
-            self.take(s, has)
-            self.go(s, p.nx, has)
-            self.go(s, p.nc, has)
+        self.onward((p.z + 2) % 4, (p.nz, p.nx, p.nc))
+        self.onward(p.zf, (p.nx, p.nc))
 
     def third(self):
+        p = self.p
+        self.onward((p.zf + 2) % 4, (p.nx, p.nc))
+
+    def fourth(self):
         p = self.p
         for zz in range(4):
             s, has = sid(zz, 1 - p.x, p.c), self.has(zz, 1 - p.x, p.c)
@@ -216,10 +225,13 @@
                 zz = (p.z + k) % 4
                 self.mail.send(self.src.at[self.rows(zz, xx, 1 - p.c)], self.gc.at[xq, zz], self.rc.at[xq, zz], p.nc)
 
+    def order(self):
+        z, zf = self.p.z, self.p.zf
+        return zf, (zf + 2) % 4, (z + 2) % 4, z
+
     def over_x(self):
         p = self.p
-        for k in (1, 2, 3, 0):
-            zz = (p.z + k) % 4
+        for zz in self.order():
             self.mail.got(self.gc.at[0, zz], self.rc.at[0, zz], p.nc)
             own = self.src[self.rows(zz, 1 - p.x, p.c)].astype(F32)
             self.gxs[zz] = (own + self.gc[0, zz].astype(F32)).astype(B16)
@@ -231,19 +243,21 @@
         self.mail.got(self.gxr.at[zz], self.rx.at[zz], p.nx)
         return self.src[self.rows(zz, p.x, p.c)].astype(F32) + self.gc[1, zz].astype(F32) + self.gxr[zz].astype(F32)
 
-    def over_z(self, k):
-        p = self.p
-        zz = (p.z + k) % 4
-        self.gzs[k] = self.column(zz).astype(B16)
-        self.mail.send(self.gzs.at[k], self.gzr.at[p.z], self.rz.at[p.z], (sid(zz, p.x, p.c), p.y))
+    def over_z(self):
+        for i, zz in enumerate(self.order()[:2]):
+            self.gzs[i] = self.column(zz).astype(B16)
+            self.mail.send(self.gzs.at[i], self.gzr.at[i], self.rz.at[i], self.p.nz)
+
+    def over_far(self):
+        self.mail.got(self.gzr.at[1], self.rz.at[1], self.p.nz)
+        self.gzs[2] = (self.column((self.p.z + 2) % 4) + self.gzr[1].astype(F32)).astype(B16)
+        self.mail.send(self.gzs.at[2], self.gzr.at[2], self.rz.at[2], self.p.far)
 
     def result(self):
-        p = self.p
-        total = self.column(p.z)
-        for k in range(1, 4):
-            zz = (p.z + k) % 4
-            self.mail.got(self.gzr.at[zz], self.rz.at[zz], p.nx)
-            total = total + self.gzr[zz].astype(F32)
+        total = self.column(self.p.z)
+        for i in (0, 2):
+            self.mail.got(self.gzr.at[i], self.rz.at[i], self.p.nz)
+            total = total + self.gzr[i].astype(F32)
         return total
 
 
@@ -294,7 +308,7 @@
     ss, rsx, rsc, rsd, rsw, rso, rsf, rsy, rdo, rga, rgx, rgz, rhc, rhx, rhz, rdf, rdq, rwm, rag, rwo, rdn, rv1, rv2, rv3, rv4,
 ):
     p = Place()
-    mail = Mail(ss)
+    mail = Mail(ss, SLOTS)
     seg, x, y, z, c, b = p.seg, p.x, p.y, p.z, p.c, p.b
     first, second = both(p.unit, seg == 0), both(p.unit, seg == 1)
     row = lambda ref: ref[...].reshape(1, -1)
@@ -317,22 +331,28 @@
     part = [pl.ds(k * 256, 256) for k in range(3)]
     order = [[dims[(k + j) % 3] for j in range(3)] for k in range(3)]
 
-    def pass_on(k, blk, dev):
-        ref = xs.at[blk, :, part[k]]
-        mail.send(ref, ref, rsx.at[k, blk], dev)
-
-    def to_core(k, blk):
-        ref = xs.at[blk, :, part[k]]
-        mail.send(ref, ref, rsc.at[k, blk], p.nc)
+    bit = {"x": 1, "y": 2, "z": 4}
+
+    def place(rel):
+        return b + sum(p.fb[d] for d in dims if rel & bit[d])
+
+    def third(rel, k):
+        return xs.at[place(rel), :, part[k]]
+
+    def pass_on(k, rel, d):
+        mail.send(third(rel, k), third(rel, k), rsx.at[k, rel ^ bit[d]], nbr[d])
+
+    def to_core(k, rel):
+        mail.send(third(rel, k), third(rel, k), rsc.at[k, rel], p.nc)
 
     for j in range(3):
         for k in range(3):
-            pass_on(k, b, nbr[order[k][j]])
+            pass_on(k, 0, order[k][j])
     for k in range(3):
-        to_core(k, b)
-    for src in (0, 14, 15):
-        for dev in p.cube():
-            mail.send(docs.at[src], docs.at[src], rsd.at[src], dev, cond=b == src)
+        to_core(k, 0)
+    special = jnp.logical_or(b == 0, b >= 14)
+    for dev in p.cube():
+        mail.send(docs.at[b], docs.at[b], rsd.at[b // 14 + b // 15], dev, special)
 
     def rows_of(s):
         return wb.at[pl.ds(pl.multiple_of(s * 48, 16), 48), :]
@@ -396,18 +416,16 @@
                 va[t + 2, to] = m[at, 256:]
                 ns[t, to] = n1[at]
 
-    def seen(k, blk):
-        mail.got(xs.at[blk, :, part[k]], rsx.at[k, blk], p.nx)
-        to_core(k, blk)
-
-    def from_core(blk):
+    def seen(k, rel):
+        mail.got(third(rel, k), rsx.at[k, rel], p.nx)
+        to_core(k, rel)
+
+    def from_core(rel):
         for k in range(3):
-            mail.got(xs.at[blk, :, part[k]], rsc.at[k, blk], p.nc)
-
-    fx, fy, fz, fc = p.fb["x"], p.fb["y"], p.fb["z"], p.fb["c"]
-
-    def qkv_of(*flips):
-        at = (b + sum(flips)) // 2
+            mail.got(xs.at[place(rel) + p.fb["c"], :, part[k]], rsc.at[k, rel], p.nc)
+
+    def qkv_of(rel, core=0):
+        at = (place(rel) + core * p.fb["c"]) // 2
         pl.when(p.unit)(lambda: qkv(at))
 
     def chain(d):
@@ -425,41 +443,42 @@
         give(sd, p.nx, has_dn)
         give(sd, p.nc, has_dn)
 
-    flips = [[p.fb[d] for d in order[k]] for k in range(3)]
+    X, Y, Z = 1, 2, 4
     for k in range(3):
-        f = flips[k]
-        seen(k, b + f[0])
-        pass_on(k, b + f[0], nbr[order[k][1]])
-        pass_on(k, b + f[0], nbr[order[k][2]])
-        seen(k, b + f[1])
-        pass_on(k, b + f[1], nbr[order[k][2]])
-        seen(k, b + f[2])
-    mail.send(wo.at[y], wo.at[y], rsy.at[0], p.ny)
+        d0, d1, d2 = order[k]
+        seen(k, bit[d0])
+        pass_on(k, bit[d0], d1)
+        pass_on(k, bit[d0], d2)
+        seen(k, bit[d1])
+        pass_on(k, bit[d1], d2)
+        seen(k, bit[d2])
+    qkv_of(0)
+    for k in range(3):
+        d0, d1, d2 = order[k]
+        seen(k, bit[d0] | bit[d1])
+        pass_on(k, bit[d0] | bit[d1], d2)
     mail.send(dyp.at[y], dyp.at[y], rsy.at[1], p.ny)
-    qkv_of()
+    whalf = pl.ds(pl.multiple_of(c * 192, 64), 192)
+    mail.send(wo.at[y, whalf], wo.at[y, whalf], rsy.at[0], p.ny)
     for k in range(3):
-        f = flips[k]
-        seen(k, b + f[1] + f[0])
-        pass_on(k, b + f[1] + f[0], nbr[order[k][2]])
+        d0, d1, d2 = order[k]
+        seen(k, bit[d0] | bit[d2])
+        seen(k, bit[d1] | bit[d2])
+    qkv_of(X)
+    qkv_of(Z)
+    from_core(0)
+    from_core(Y)
+    qkv_of(0, 1)
     for k in range(3):
-        f = flips[k]
-        seen(k, b + f[2] + f[0])
-        seen(k, b + f[2] + f[1])
-    qkv_of(fx)
-    qkv_of(fz)
-    from_core(b + fc)
-    from_core(b + fc + fy)
-    qkv_of(fc)
-    for k in range(3):
-        seen(k, b + fx + fy + fz)
+        seen(k, X | Y | Z)
     chain(1)
-    qkv_of(fx, fz)
-    for more in ((fx,), (fz,), (fx, fz)):
-        from_core(b + fc + sum(more))
-        from_core(b + fc + sum(more) + fy)
-        qkv_of(fc, *more)
+    qkv_of(X | Z)
+    for rel in (X, Z, X | Z):
+        from_core(rel)
+        from_core(rel | Y)
+        qkv_of(rel, 1)
     for src in (0, 14, 15):
-        pl.when(b != src)(lambda src=src: mail.got(docs.at[src], rsd.at[src], p.nx))
+        pl.when(b != src)(lambda src=src: mail.got(docs.at[src], rsd.at[src // 14 + src // 15], p.nx))
 
     lowlane = iota((256, 128), 1) < 64
     farrows = pl.ds(pl.multiple_of(p.parity * 256, 256), 256)
@@ -581,6 +600,8 @@
         deliver(t, first)
         if t == 1:
             chain(2)
+            mail.got(wo.at[1 - y, whalf], rsy.at[0], p.ny)
+            mail.send(wo.at[1 - y, whalf], wo.at[1 - y, whalf], rsy.at[4], p.nc)
     chain(3)
     pl.when(second)(far_ready)
     for t in range(4):
@@ -599,7 +620,7 @@
         e, o = halves(orecv[2 * a].astype(F32), orecv[2 * a + 1].astype(F32))
         attn[0:128, a * 128 : a * 128 + 128] = e.astype(B16)
         attn[128:256, a * 128 : a * 128 + 128] = o.astype(B16)
-    mail.got(wo.at[1 - y], rsy.at[0], p.ny)
+    mail.got(wo.at[1 - y, pl.ds(pl.multiple_of((1 - c) * 192, 64), 192)], rsy.at[4], p.nc)
     mail.got(dyp.at[1 - y], rsy.at[1], p.ny)
     pair = pl.multiple_of(p.u * 2, 2)
     for par in range(2):
@@ -644,7 +665,6 @@
     for par in range(2):
         fo[par * 64 : par * 64 + 64] = facc[pl.ds(pl.multiple_of(par * 128 + y * 64, 64), 64)]
         fs[par * 64 : par * 64 + 64] = facc[pl.ds(pl.multiple_of(par * 128 + (1 - y) * 64, 64), 64)].astype(B16)
-    mail.send(fs, fr, rsy.at[3], p.ny)
 
     n2t[...] = n2s[...].astype(F32).T.astype(B16)
     dyt[...] = dys[...].astype(F32).T.astype(B16)
@@ -668,8 +688,8 @@
 
     out_sum = Reduce(p, mail, gwo, hc, hxs, hxr, hzs, hzr, rhc, rhx, rhz)
 
-    def ffn_over_x(k):
-        zz = (z + k) % 4
+    def ffn_over_x(i):
+        zz = ring[i]
         gb[zz] = (gb[zz].astype(F32) + ra[zz].astype(F32)).astype(B16)
         mail.send(gb.at[zz], gxr.at[zz], rgx.at[zz], p.nx)
 
@@ -677,20 +697,28 @@
         mail.got(gxr.at[zz], rgx.at[zz], p.nx)
         return ge[zz].astype(F32) + rb[zz].astype(F32) + gxr[zz].astype(F32)
 
-    def ffn_over_z(k):
-        zz = (z + k) % 4
+    def ffn_over_z(i):
+        zz = ring[i]
         ge[zz] = ffn_column(zz).astype(B16)
-        mail.send(ge.at[zz], gzr.at[z], rgz.at[z], (sid(zz, x, c), y))
-
+        mail.send(ge.at[zz], gzr.at[i], rgz.at[i], p.nz)
+
+    def ffn_over_far():
+        zz = ring[2]
+        mail.got(gzr.at[1], rgz.at[1], p.nz)
+        ge[zz] = (ffn_column(zz) + gzr[1].astype(F32)).astype(B16)
+        mail.send(ge.at[zz], gzr.at[2], rgz.at[2], p.far)
+
+    ring = out_sum.order()
     owners(ga, 1 - x, 1 - c)
     mail.send(ga, ra, rga.at[0], p.nc)
     owners(gb, 1 - x, c)
     mail.got(ra, rga.at[0], p.nc)
-    ffn_over_x(2)
+    ffn_over_x(0)
     owners(gd, x, 1 - c)
     mail.send(gd, rb, rga.at[1], p.nc)
     owners(ge, x, c)
     mail.got(yr, rsy.at[2], p.ny)
+    mail.send(fs, fr, rsy.at[3], p.ny)
     dn2 = ys[...].astype(F32) + yr[...].astype(F32)
     z2, inv2 = norm_parts(hid[...])
     dh = dys[...].astype(F32) + norm_grad(z2, inv2, dn2 * row(g2_ref))
@@ -711,9 +739,10 @@
         def _(h=h):
             dor[mine_t, crow] = dpk[h]
 
-    for k in (1, 3, 0):
-        ffn_over_x(k)
+    for i in (1, 2, 3):
+        ffn_over_x(i)
     mail.got(rb, rga.at[1], p.nc)
+    ffn_over_z(0)
     gwo[...] = dot(dh.T.astype(B16), attn[:, pl.ds(pl.multiple_of(y * 384, 128), 384)]).astype(B16)
     out_sum.cores()
     mail.got(fr, rsy.at[3], p.ny)
@@ -812,15 +841,19 @@
         dtt[64:128, at] = (dtt[64:128, at].astype(F32) + rows[:64]).astype(B16)
         dtt[128:192, at] = (dtt[128:192, at].astype(F32) + rows[64:]).astype(B16)
 
+    ffn_over_z(1)
     out_sum.over_x()
-    ffn_over_z(2)
     pl.when(p.unit)(lambda: near(0))
-    ffn_over_z(1)
+    out_sum.over_z()
     early.middle()
     pl.when(p.unit)(lambda: near(1))
-    ffn_over_z(3)
+    ffn_over_far()
+    out_sum.over_far()
     pl.when(p.unit)(lambda: near(2))
     pl.when(p.unit)(lambda: near(3))
+    woag[p.s] = out_sum.result().astype(B16)
+    spread_out = Spread(p, mail, woag, rwo, False)
+    spread_out.first()
 
     @pl.when(first)
     def _():
@@ -846,20 +879,26 @@
             def _(t=t, cc=cc):
                 dqr[p.hl] = packs[t, :, cc * 128 : cc * 128 + 128]
 
+    vb2[z] = jnp.zeros((8, 768), F32)
     spread = Spread(p, mail, wag, rag, True)
 
     @pl.when(p.unit)
     def _():
         dw = dot(dtt[...], ns[...].reshape(2048, 768))
-        bias = dot_nt(jnp.ones((16, 2048), B16), dtt[...])
         for h in range(2):
-            wms[h, 0:96] = dw[h * 96 : h * 96 + 96].astype(B16)
-            wms[h, 96:112, 0:192] = bias.astype(B16)
-            wms[h, 96:112, 192:768] = jnp.zeros((16, 576), B16)
+            wms[h] = dw[h * 96 : h * 96 + 96].astype(B16)
+        bias = dot_nt(jnp.ones((16, 2048), B16), dtt[...])[0:8]
+        at = pl.ds(pl.multiple_of(p.head // 2 * 128, 128), 128)
+        lane = iota((8, 128), 1) < 64
+        low_q, low_v = jnp.where(lane, bias[:, 0:128], 0.0), jnp.concatenate([bias[:, 128:192], jnp.zeros((8, 64), F32)], axis=1)
+        for odd in range(2):
+
+            @pl.when(p.head % 2 == odd)
+            def _(odd=odd):
+                for i, v in enumerate((low_q, low_v)):
+                    vb2[z, 2 + i : 3 + i, at] = (pltpu.roll(v, 64, 1) if odd else v)[0:1]
 
     mail.send(wms.at[1 - seg], wmr, rwm.at[0], p.far, p.unit)
-    for k in range(1, 4):
-        out_sum.over_z(k)
 
     for h, u in enumerate(UNITS):
         pl.when(p.u != u)(lambda h=h: mail.got(dqr.at[h], rdq.at[h], p.nx))
@@ -880,15 +919,11 @@
         wag[p.s] = (wms[seg].astype(F32) + wmr[...].astype(F32)).astype(B16)
 
     spread.first()
-    o_total = out_sum.result()
-    woag[p.s] = o_total.astype(B16)
-    spread_out = Spread(p, mail, woag, rwo, False)
-    spread_out.first()
+    spread_out.second()
     z1, inv1 = norm_parts(xs[b].astype(F32))
     mail.got(dnr, rdn.at[0], p.ny)
     own = [facc[pl.ds(pl.multiple_of(par * 128 + y * 64, 64), 64)] for par in range(2)]
     dn1 = jnp.concatenate(own, axis=0) + dnr[...].astype(F32)
-    vb2[z] = jnp.zeros((8, 768), F32)
     vb2[z, 0:1] = jnp.sum(dn1 * z1, axis=0, keepdims=True)
     vb2[z, 1:2] = jnp.sum(dn1, axis=0, keepdims=True)
     late.start()
@@ -900,22 +935,21 @@
         rest = rest - piece.astype(F32)
     gin[...] = result
     spread.second()
-    spread_out.second()
+    spread_out.third()
     late.middle()
     total = ffn_column(z)
-    for k in range(1, 4):
-        zz = (z + k) % 4
-        mail.got(gzr.at[zz], rgz.at[zz], p.nx)
-        total = total + gzr[zz].astype(F32)
+    for i in (0, 2):
+        mail.got(gzr.at[i], rgz.at[i], p.nz)
+        total = total + gzr[i].astype(F32)
     o_ud[...] = total
+    spread.third()
+    spread_out.fourth()
     o_tot[0] = early.finish()
-    spread.third()
-    spread_out.third()
+    spread.fourth()
     o_tot[1] = late.finish()
     spread_out.last()
     spread.last()
     mail.close()
-    assert mail.used <= SENDS, mail.used
 
 
 def write_out(lout, gin, wag, woag, ud, tot, o_l, o_g, o_g1, o_b1, o_wq, o_bqv, o_wo, o_bo, o_g2, o_b2, o_up, o_bup, o_dn, o_bd):
@@ -938,14 +972,11 @@
         for k in range(3):
             at = slice(k * 64, k * 64 + 64)
             o_wq[k, :, col] = jnp.concatenate([w0[at], w1[at]], axis=0).T
-        r0, r1 = wag[u0, 96:112].astype(F32), wag[u1, 96:112].astype(F32)
-        low = iota((16, 128), 1) < 64
-        for k in range(2):
-            at = slice(k * 128, k * 128 + 128)
-            o_bqv[k : k + 1, col] = jnp.where(low, r0[:, at], pltpu.roll(r1[:, at], 64, 1))[0:1]
-
-
-SENDS = 400
+    half = lax.axis_index("head")
+    o_bqv[...] = tot[1, 2:4, pl.ds(pl.multiple_of(half * 384, 128), 384)]
+
+
+SLOTS = 64
 
 
 def count_table():
@@ -991,7 +1022,7 @@
         out((128, 768), B16), out((128, 768)), out((768,)), out((768,)), out((3, 768, 384)), out((2, 384)), out((384, 768)), out((768,)),
         out((768,)), out((768,)), out((48, 1536)), out((3072,)), out((48, 1536)), out((768,)),
     )
-    raw = (out((128, 768), B16), out((128, 768)), out((16, 112, 768), B16), out((16, 48, 384), B16), out((48, 3072)), out((2, 8, 768)))
+    raw = (out((128, 768), B16), out((128, 768)), out((16, 96, 768), B16), out((16, 48, 384), B16), out((48, 3072)), out((2, 8, 768)))
     scratch = [
         vm(4, 512, 128), vm(6, 512, 128), vm(6, 512, 128), vm(4, 512, 768), vf(4, 1, 512), vf(4, 128, 256), vm(6, 128, 128),
         vm(768, 384), vf(128, 768), vm(768, 384), vf(1, 384), vf(1, 1536), vf(4, 1, 512), vf(4, 128, 512),
@@ -999,12 +1030,12 @@
         vm(4, 256, 128), vm(4, 256, 128), vm(256, 768), vm(6, 128, 512), vf(256, 768), vm(256, 768), vm(256, 768), vm(256, 1536),
         vm(256, 1536), vf(256, 768), vf(256, 768), vm(256, 768), vm(256, 768), vm(128, 768), vm(128, 768), vf(128, 768),
         vm(4, 256, 128), vm(4, 512, 128), vf(4, 1, 512), vm(6, 128, 512), vf(512, 128), vf(512, 128), vf(4, 128, 512), vm(192, 2048),
-        vm(4, 256, 128), vm(4, 256, 128), vm(4, 3, 256, 128), vm(6, 3, 128, 128), vm(2, 112, 768), vm(112, 768),
+        vm(4, 256, 128), vm(4, 256, 128), vm(4, 3, 256, 128), vm(6, 3, 128, 128), vm(2, 96, 768), vm(96, 768),
         vm(768, 256), vm(768, 256), *[vm(4, 48, 3072)] * 8,
         vm(2, 4, 48, 384), vm(4, 48, 384), vm(4, 48, 384), vm(4, 48, 384), vm(4, 48, 384), vm(3, 256, 384), vm(128, 768), vm(128, 768),
         vf(4, 8, 768), vf(8, 8, 768), vf(4, 8, 768), vf(8, 8, 768),
-        dma(SENDS), dma(3, 16), dma(3, 16), dma(16), dma(16), dma(12), dma(2), dma(4), dma(8), dma(2), dma(4), dma(4), dma(2, 4), dma(4),
-        dma(4), dma(1), dma(6), dma(1), dma(16), dma(16), dma(1), dma(4), dma(8), dma(4), dma(8),
+        dma(SLOTS), dma(3, 8), dma(3, 8), dma(3), dma(16), dma(12), dma(2), dma(5), dma(8), dma(2), dma(4), dma(3), dma(2, 4), dma(4),
+        dma(3), dma(1), dma(6), dma(1), dma(16), dma(16), dma(1), dma(4), dma(8), dma(4), dma(8),
     ]
     args = (
         layer_input, doc_ids, cotangent, ln1_gain, ln1_bias, w_qkv.transpose(1, 0, 2), bias_qv, w_out, b_out, ln2_gain, ln2_bias, w_up,

time: 181 us -> 159 us (0.88)
  the two profiles are of different devices: /device:TPU:27 before, /device:TPU:0 now
where the time goes in v4:
time: 159 us
  Pallas kernels  158 us (99%)
    pallas_call x1, Pallas kernels, fast(): pl.pallas_call(kernel, out_shape=raw, in_specs=in_vmem(len(args)), out_sp...  153 us
    pallas_call x1, Pallas kernels, fast(): pl.pallas_call(write_out, out_shape=shapes, in_specs=in_vmem(len(raw)), o...  5.46 us

profile of v4, /device:TPU:0, one launch (start us, length us, event | category | flops | bytes accessed | tf_op | source)
XLA Modules:
  0.0 159.2 jit_solution(9245949231562122888)
XLA Ops:
  0.7 152.9 %shard_map.263 = (bf16[128,768]{1,0:T(8,128)(2,1)}, f32[128,768]{1,0:T(8,128)}, bf16[16,96,768]{2,1,0:T(8,128)(2,1)}, bf16[16,48,384]{2,1,0:T(8,128)(2,1)}, f32[48,3072]{1,0:T(8,128)}, /*index=5*/f32[2,8,768]{2,1,0:T(8,128)}) custom-call(bf16[128,768]{1,0:T(8,128)(2,1)} %x_ref.1, s32[128]{0:T(128)} %doc_ref.1, bf16[128,768]{1,0:T(8,128)(2,1)} %cot_ref.1, ...), custom_call_target="tpu_custom_call" | custom-call | tf_op jit(solution)/shard_map/pallas_call | solution.py:1044
  153.5 5.5 %shard_map.264 = (bf16[128,768]{1,0:T(8,128)(2,1)}, f32[128,768]{1,0:T(8,128)}, f32[768]{0:T(1024)}, f32[768]{0:T(1024)}, f32[3,768,384]{2,1,0:T(8,128)}, /*inde...) custom-call(bf16[128,768]{1,0:T(8,128)(2,1)} %get-tuple-element.34.l, ...), custom_call_target="tpu_custom_call" | custom-call | tf_op jit(solution)/shard_map/pallas_call | solution.py:1048

commit v5 on v4

--- a/solution.py
+++ b/solution.py
@@ -227,7 +227,7 @@
 
     def order(self):
         z, zf = self.p.z, self.p.zf
-        return zf, (zf + 2) % 4, (z + 2) % 4, z
+        return (zf + 2) % 4, (z + 2) % 4, zf, z
 
     def over_x(self):
         p = self.p
@@ -243,19 +243,18 @@
         self.mail.got(self.gxr.at[zz], self.rx.at[zz], p.nx)
         return self.src[self.rows(zz, p.x, p.c)].astype(F32) + self.gc[1, zz].astype(F32) + self.gxr[zz].astype(F32)
 
-    def over_z(self):
-        for i, zz in enumerate(self.order()[:2]):
-            self.gzs[i] = self.column(zz).astype(B16)
-            self.mail.send(self.gzs.at[i], self.gzr.at[i], self.rz.at[i], self.p.nz)
+    def over_z(self, i):
+        self.gzs[i] = self.column(self.order()[i]).astype(B16)
+        self.mail.send(self.gzs.at[i], self.gzr.at[i], self.rz.at[i], self.p.nz)
 
     def over_far(self):
-        self.mail.got(self.gzr.at[1], self.rz.at[1], self.p.nz)
-        self.gzs[2] = (self.column((self.p.z + 2) % 4) + self.gzr[1].astype(F32)).astype(B16)
-        self.mail.send(self.gzs.at[2], self.gzr.at[2], self.rz.at[2], self.p.far)
+        self.mail.got(self.gzr.at[0], self.rz.at[0], self.p.nz)
+        self.gzs[1] = (self.column(self.order()[1]) + self.gzr[0].astype(F32)).astype(B16)
+        self.mail.send(self.gzs.at[1], self.gzr.at[1], self.rz.at[1], self.p.far)
 
     def result(self):
         total = self.column(self.p.z)
-        for i in (0, 2):
+        for i in (1, 2):
             self.mail.got(self.gzr.at[i], self.rz.at[i], self.p.nz)
             total = total + self.gzr[i].astype(F32)
         return total
@@ -360,10 +359,6 @@
     def give(s, dev, cond=None):
         mail.send(rows_of(s), rows_of(s), rsw.at[s], dev, cond)
 
-    give(p.s, (sid((z + 1) % 4, x, c), y), z <= 2)
-    give(p.s, (sid((z + 3) % 4, x, c), y), z >= 1)
-    give(p.s, p.nx)
-    give(p.s, p.nc)
 
     pair_cols = pl.ds(pl.multiple_of(p.hl // 2 * 128, 128), 128)
     for odd in range(2):
@@ -457,6 +452,10 @@
         d0, d1, d2 = order[k]
         seen(k, bit[d0] | bit[d1])
         pass_on(k, bit[d0] | bit[d1], d2)
+    give(p.s, (sid((z + 1) % 4, x, c), y), z <= 2)
+    give(p.s, (sid((z + 3) % 4, x, c), y), z >= 1)
+    give(p.s, p.nx)
+    give(p.s, p.nc)
     mail.send(dyp.at[y], dyp.at[y], rsy.at[1], p.ny)
     whalf = pl.ds(pl.multiple_of(c * 192, 64), 192)
     mail.send(wo.at[y, whalf], wo.at[y, whalf], rsy.at[0], p.ny)
@@ -471,12 +470,13 @@
     qkv_of(0, 1)
     for k in range(3):
         seen(k, X | Y | Z)
-    chain(1)
     qkv_of(X | Z)
     for rel in (X, Z, X | Z):
         from_core(rel)
         from_core(rel | Y)
         qkv_of(rel, 1)
+        if rel == Z:
+            chain(1)
     for src in (0, 14, 15):
         pl.when(b != src)(lambda src=src: mail.got(docs.at[src], rsd.at[src // 14 + src // 15], p.nx))
 
@@ -598,16 +598,17 @@
         pl.when(p.unit)(functools.partial(near_attention, t))
         pl.when(first)(functools.partial(conclude, t))
         deliver(t, first)
-        if t == 1:
+        if t == 2:
             chain(2)
+        if t == 0:
             mail.got(wo.at[1 - y, whalf], rsy.at[0], p.ny)
             mail.send(wo.at[1 - y, whalf], wo.at[1 - y, whalf], rsy.at[4], p.nc)
-    chain(3)
     pl.when(second)(far_ready)
     for t in range(4):
         pl.when(second)(functools.partial(far_attention, t))
         pl.when(second)(functools.partial(conclude, t))
         deliver(t, second)
+    chain(3)
     for zq in range(4):
         s = sid(zq, 1 - x, c)
         mail.got(rows_of(s), rsw.at[s], p.nx)
@@ -635,8 +636,6 @@
         s = sid(i // 2, i % 2, 1 - c)
         mail.got(rows_of(s), rsw.at[s], p.nc)
 
-    facc[...] = jnp.zeros_like(facc)
-    dacc[...] = jnp.zeros_like(dacc)
     k0 = 0.7978845608028654
     vb1[z] = jnp.zeros((8, 768), F32)
 
@@ -655,13 +654,13 @@
         dpl = dp.astype(B16)
         acts[:, cols] = act
         dpre[:, cols] = dpl
-        facc[...] += dot_nt(act, dn)
-        dacc[...] += dot_nt(dpl, up)
         return 0
 
     lax.fori_loop(0, 6, ffn_step, 0)
-    ys[...] = dacc[...].astype(B16)
-    mail.send(ys, yr, rsy.at[2], p.ny)
+    for k in range(3):
+        ys[k] = dot_nt(dpre[...], wb[k * 256 : k * 256 + 256, 0:1536]).astype(B16)
+        mail.send(ys.at[k], yr.at[k], rsy.at[5 + k], p.ny)
+    facc[...] = dot_nt(acts[:, 0:768], wb[:, 1536:2304]) + dot_nt(acts[:, 768:1536], wb[:, 2304:3072])
     for par in range(2):
         fo[par * 64 : par * 64 + 64] = facc[pl.ds(pl.multiple_of(par * 128 + y * 64, 64), 64)]
         fs[par * 64 : par * 64 + 64] = facc[pl.ds(pl.multiple_of(par * 128 + (1 - y) * 64, 64), 64)].astype(B16)
@@ -703,10 +702,10 @@
         mail.send(ge.at[zz], gzr.at[i], rgz.at[i], p.nz)
 
     def ffn_over_far():
-        zz = ring[2]
-        mail.got(gzr.at[1], rgz.at[1], p.nz)
-        ge[zz] = (ffn_column(zz) + gzr[1].astype(F32)).astype(B16)
-        mail.send(ge.at[zz], gzr.at[2], rgz.at[2], p.far)
+        zz = ring[1]
+        mail.got(gzr.at[0], rgz.at[0], p.nz)
+        ge[zz] = (ffn_column(zz) + gzr[0].astype(F32)).astype(B16)
+        mail.send(ge.at[zz], gzr.at[1], rgz.at[1], p.far)
 
     ring = out_sum.order()
     owners(ga, 1 - x, 1 - c)
@@ -717,9 +716,21 @@
     owners(gd, x, 1 - c)
     mail.send(gd, rb, rga.at[1], p.nc)
     owners(ge, x, c)
-    mail.got(yr, rsy.at[2], p.ny)
+    @pl.when(p.unit)
+    def _():
+        for t in range(4):
+            kt[t + 2] = ka[t + 2].astype(F32).T.astype(B16)
+        dqt[...] = jnp.zeros_like(dqt)
+
+    @pl.when(second)
+    def _():
+        for h in range(2):
+            kt[h] = ka[h].astype(F32).T.astype(B16)
+
+    for k in range(3):
+        mail.got(yr.at[k], rsy.at[5 + k], p.ny)
     mail.send(fs, fr, rsy.at[3], p.ny)
-    dn2 = ys[...].astype(F32) + yr[...].astype(F32)
+    dn2 = jnp.concatenate([ys[k].astype(F32) + yr[k].astype(F32) for k in range(3)], axis=1)
     z2, inv2 = norm_parts(hid[...])
     dh = dys[...].astype(F32) + norm_grad(z2, inv2, dn2 * row(g2_ref))
     facc[...] = dh
@@ -739,19 +750,20 @@
         def _(h=h):
             dor[mine_t, crow] = dpk[h]
 
-    for i in (1, 2, 3):
-        ffn_over_x(i)
+    gwo[...] = dot(dh.T.astype(B16), attn[:, pl.ds(pl.multiple_of(y * 384, 128), 384)]).astype(B16)
+    out_sum.cores()
+    ffn_over_x(1)
     mail.got(rb, rga.at[1], p.nc)
     ffn_over_z(0)
-    gwo[...] = dot(dh.T.astype(B16), attn[:, pl.ds(pl.multiple_of(y * 384, 128), 384)]).astype(B16)
-    out_sum.cores()
+    out_sum.over_x()
     mail.got(fr, rsy.at[3], p.ny)
     sums = [jnp.zeros((1, 768), F32)] * 4
     for par in range(2):
         at = pl.ds(pl.multiple_of(par * 128 + y * 64, 64), 64)
         to = slice(par * 64, par * 64 + 64)
         dh_s[to] = facc[at]
-        own = (dacc[at], ys[at].astype(F32) + yr[at].astype(F32), facc[at], dys[at].astype(F32))
+        dn2_own = jnp.concatenate([ys[k, at].astype(F32) + yr[k, at].astype(F32) for k in range(3)], axis=1)
+        own = (dacc[at], dn2_own, facc[at], dys[at].astype(F32))
         sums = [total + jnp.sum(v, axis=0, keepdims=True) for total, v in zip(sums, own)]
         fo[to] = hid[at] + fo[to] + fr[to].astype(F32) + row(bd_ref)
     back = mixed((128, 128), 1, 0)
@@ -768,6 +780,7 @@
     early = Total(p, mail, vb1, vr1, rv1, rv2)
     late = Total(p, mail, vb2, vr2, rv3, rv4)
     early.start()
+    ffn_over_x(2)
 
     def prepare():
         for i in range(8):
@@ -780,10 +793,9 @@
             prod = d.T * ot[t]
             delta[t, :, 0:256] = jnp.sum(prod[:64], axis=0, keepdims=True)
             delta[t, :, 256:512] = jnp.sum(prod[64:], axis=0, keepdims=True)
-            kt[t + 2] = ka[t + 2].astype(F32).T.astype(B16)
-        dqt[...] = jnp.zeros_like(dqt)
 
     pl.when(p.unit)(prepare)
+    ffn_over_x(3)
 
     def score_grads(cc, q, do, st, lse_row, delta_row):
         pr = jnp.exp(st - lse_row)
@@ -796,42 +808,32 @@
         dka[...] = jnp.zeros_like(dka)
         dva[...] = jnp.zeros_like(dva)
 
-    @pl.when(second)
-    def _():
-        for h in range(2):
-            kt[h] = ka[h].astype(F32).T.astype(B16)
-
-        def chunk(cc, _):
-            clear()
-
-            def step(t, _):
-                q, do = qa[t, farcols], doa[t, farcols]
-                dqt[t, :, farcols] += score_grads(cc, q, do, dot_nt(ka[cc], q), lse[t, :, farcols], delta[t, :, farcols])
-                return 0
-
-            lax.fori_loop(0, 4, step, 0)
-            low = iota((512, 128), 1) < 64
-            pack = jnp.where(low, dka[...], pltpu.roll(dva[...], 64, 1)).astype(B16)
-            dfs[2 * cc] = pack[:256]
-            dfs[2 * cc + 1] = pack[256:]
+    def far_grads(cc):
+        clear()
+
+        def step(t, _):
+            q, do = qa[t, farcols], doa[t, farcols]
+            dqt[t, :, farcols] += score_grads(cc, q, do, dot_nt(ka[cc], q), lse[t, :, farcols], delta[t, :, farcols])
             return 0
 
-        lax.fori_loop(0, 2, chunk, 0)
-
-    mail.send(dfs, dfr, rdf.at[0], p.far, second)
+        lax.fori_loop(0, 4, step, 0)
+        low = iota((512, 128), 1) < 64
+        pack = jnp.where(low, dka[...], pltpu.roll(dva[...], 64, 1)).astype(B16)
+        dfs[2 * cc] = pack[:256]
+        dfs[2 * cc + 1] = pack[256:]
+
+    for cc in range(2):
+        pl.when(second)(functools.partial(far_grads, cc))
+        mail.send(dfs.at[2 * cc : 2 * cc + 2], dfr.at[2 * cc : 2 * cc + 2], rdf.at[cc], p.far, second)
+    ffn_over_far()
 
     def near(t):
         clear()
         q, do = qa[t], doa[t]
         dqt[t] += score_grads(t + 2, q, do, causal(dot_nt(ka[t + 2], q)), lse[t], delta[t])
-        if t < 3:
-
-            def step(tq, _):
-                q, do = qa[tq], doa[tq]
-                dqt[tq] += score_grads(t + 2, q, do, dot_nt(ka[t + 2], q), lse[tq], delta[tq])
-                return 0
-
-            lax.fori_loop(t + 1, 4, step, 0)
+        for tq in range(t + 1, 4):
+            q, do = qa[tq], doa[tq]
+            dqt[tq] += score_grads(t + 2, q, do, dot_nt(ka[t + 2], q), lse[tq], delta[tq])
         dtt[64:128, t * 512 : t * 512 + 512] = dka[...].T[:64].astype(B16)
         dtt[128:192, t * 512 : t * 512 + 512] = dva[...].T[:64].astype(B16)
 
@@ -841,14 +843,13 @@
         dtt[64:128, at] = (dtt[64:128, at].astype(F32) + rows[:64]).astype(B16)
         dtt[128:192, at] = (dtt[128:192, at].astype(F32) + rows[64:]).astype(B16)
 
-    ffn_over_z(1)
-    out_sum.over_x()
+    out_sum.over_z(0)
     pl.when(p.unit)(lambda: near(0))
-    out_sum.over_z()
+    out_sum.over_far()
+    ffn_over_z(2)
+    out_sum.over_z(2)
     early.middle()
     pl.when(p.unit)(lambda: near(1))
-    ffn_over_far()
-    out_sum.over_far()
     pl.when(p.unit)(lambda: near(2))
     pl.when(p.unit)(lambda: near(3))
     woag[p.s] = out_sum.result().astype(B16)
@@ -857,7 +858,8 @@
 
     @pl.when(first)
     def _():
-        mail.got(dfr, rdf.at[0], p.far)
+        for cc in range(2):
+            mail.got(dfr.at[2 * cc : 2 * cc + 2], rdf.at[cc], p.far)
         for t in range(4):
             add_far(t)
 
@@ -937,16 +939,17 @@
     spread.second()
     spread_out.third()
     late.middle()
-    total = ffn_column(z)
-    for i in (0, 2):
-        mail.got(gzr.at[i], rgz.at[i], p.nz)
-        total = total + gzr[i].astype(F32)
-    o_ud[...] = total
     spread.third()
     spread_out.fourth()
     o_tot[0] = early.finish()
     spread.fourth()
     o_tot[1] = late.finish()
+    total = ffn_column(z)
+    for i in (1, 2):
+        mail.got(gzr.at[i], rgz.at[i], p.nz)
+        total = total + gzr[i].astype(F32)
+    o_ud[0] = total[:, :1536]
+    o_ud[1] = total[:, 1536:]
     spread_out.last()
     spread.last()
     mail.close()
@@ -955,8 +958,8 @@
 def write_out(lout, gin, wag, woag, ud, tot, o_l, o_g, o_g1, o_b1, o_wq, o_bqv, o_wo, o_bo, o_g2, o_b2, o_up, o_bup, o_dn, o_bd):
     o_l[...] = lout[...]
     o_g[...] = gin[...]
-    o_up[...] = ud[:, :1536]
-    o_dn[...] = ud[:, 1536:]
+    o_up[...] = ud[0]
+    o_dn[...] = ud[1]
     for i, ref in enumerate((o_g2, o_b2, o_bo, o_bd)):
         ref[...] = tot[0, i : i + 1].reshape(768)
     for i in range(4):
@@ -976,7 +979,7 @@
     o_bqv[...] = tot[1, 2:4, pl.ds(pl.multiple_of(half * 384, 128), 384)]
 
 
-SLOTS = 64
+SLOTS = 40
 
 
 def count_table():
@@ -1022,20 +1025,20 @@
         out((128, 768), B16), out((128, 768)), out((768,)), out((768,)), out((3, 768, 384)), out((2, 384)), out((384, 768)), out((768,)),
         out((768,)), out((768,)), out((48, 1536)), out((3072,)), out((48, 1536)), out((768,)),
     )
-    raw = (out((128, 768), B16), out((128, 768)), out((16, 96, 768), B16), out((16, 48, 384), B16), out((48, 3072)), out((2, 8, 768)))
+    raw = (out((128, 768), B16), out((128, 768)), out((16, 96, 768), B16), out((16, 48, 384), B16), out((2, 48, 1536)), out((2, 8, 768)))
     scratch = [
         vm(4, 512, 128), vm(6, 512, 128), vm(6, 512, 128), vm(4, 512, 768), vf(4, 1, 512), vf(4, 128, 256), vm(6, 128, 128),
         vm(768, 384), vf(128, 768), vm(768, 384), vf(1, 384), vf(1, 1536), vf(4, 1, 512), vf(4, 128, 512),
         vm(16, 128, 768), vf(17, 8, 128), vm(768, 3072), vm(2, 384, 768), vm(2, 128, 768), vm(12, 128, 128), vm(4, 256, 128),
         vm(4, 256, 128), vm(4, 256, 128), vm(256, 768), vm(6, 128, 512), vf(256, 768), vm(256, 768), vm(256, 768), vm(256, 1536),
-        vm(256, 1536), vf(256, 768), vf(256, 768), vm(256, 768), vm(256, 768), vm(128, 768), vm(128, 768), vf(128, 768),
+        vm(256, 1536), vf(256, 768), vf(256, 768), vm(3, 256, 256), vm(3, 256, 256), vm(128, 768), vm(128, 768), vf(128, 768),
         vm(4, 256, 128), vm(4, 512, 128), vf(4, 1, 512), vm(6, 128, 512), vf(512, 128), vf(512, 128), vf(4, 128, 512), vm(192, 2048),
         vm(4, 256, 128), vm(4, 256, 128), vm(4, 3, 256, 128), vm(6, 3, 128, 128), vm(2, 96, 768), vm(96, 768),
         vm(768, 256), vm(768, 256), *[vm(4, 48, 3072)] * 8,
         vm(2, 4, 48, 384), vm(4, 48, 384), vm(4, 48, 384), vm(4, 48, 384), vm(4, 48, 384), vm(3, 256, 384), vm(128, 768), vm(128, 768),
         vf(4, 8, 768), vf(8, 8, 768), vf(4, 8, 768), vf(8, 8, 768),
-        dma(SLOTS), dma(3, 8), dma(3, 8), dma(3), dma(16), dma(12), dma(2), dma(5), dma(8), dma(2), dma(4), dma(3), dma(2, 4), dma(4),
-        dma(3), dma(1), dma(6), dma(1), dma(16), dma(16), dma(1), dma(4), dma(8), dma(4), dma(8),
+        dma(SLOTS), dma(3, 8), dma(3, 8), dma(3), dma(16), dma(12), dma(2), dma(8), dma(8), dma(2), dma(4), dma(3), dma(2, 4), dma(4),
+        dma(3), dma(2), dma(6), dma(1), dma(16), dma(16), dma(1), dma(4), dma(8), dma(4), dma(8),
     ]
     args = (
         layer_input, doc_ids, cotangent, ln1_gain, ln1_bias, w_qkv.transpose(1, 0, 2), bias_qv, w_out, b_out, ln2_gain, ln2_bias, w_up,

time: 159 us -> 156 us (0.981)
  Pallas kernels: 158 us -> 155 us
    pallas_call x1, Pallas kernels: 153 us -> 149 us  [fast(): pl.pallas_call(kernel, out_shape=raw, in_specs=in_vmem(len(args)), out_sp...]
where the time goes in v5:
time: 156 us
  Pallas kernels  155 us (99%)
    pallas_call x1, Pallas kernels, fast(): pl.pallas_call(kernel, out_shape=raw, in_specs=in_vmem(len(args)), out_sp...  149 us
    pallas_call x1, Pallas kernels, fast(): pl.pallas_call(write_out, out_shape=shapes, in_specs=in_vmem(len(raw)), o...  5.46 us

profile of v5, /device:TPU:0, one launch (start us, length us, event | category | flops | bytes accessed | tf_op | source)
XLA Modules:
  0.0 155.7 jit_solution(13406161483944150879)
XLA Ops:
  0.7 149.4 %shard_map.263 = (bf16[128,768]{1,0:T(8,128)(2,1)}, f32[128,768]{1,0:T(8,128)}, bf16[16,96,768]{2,1,0:T(8,128)(2,1)}, bf16[16,48,384]{2,1,0:T(8,128)(2,1)}, f32[...) custom-call(bf16[128,768]{1,0:T(8,128)(2,1)} %x_ref.1, s32[128]{0:T(128)} %doc_ref.1, bf16[128,768]{1,0:T(8,128)(2,1)} %cot_ref.1, ...), custom_call_target="tpu_custom_call" | custom-call | tf_op jit(solution)/shard_map/pallas_call | solution.py:1047
  150.1 5.5 %shard_map.264 = (bf16[128,768]{1,0:T(8,128)(2,1)}, f32[128,768]{1,0:T(8,128)}, f32[768]{0:T(1024)}, f32[768]{0:T(1024)}, f32[3,768,384]{2,1,0:T(8,128)}, /*inde...) custom-call(bf16[128,768]{1,0:T(8,128)(2,1)} %get-tuple-element.34.l, ...), custom_call_target="tpu_custom_call" | custom-call | tf_op jit(solution)/shard_map/pallas_call | solution.py:1051

commit v6 on v5

--- a/solution.py
+++ b/solution.py
@@ -598,17 +598,17 @@
         pl.when(p.unit)(functools.partial(near_attention, t))
         pl.when(first)(functools.partial(conclude, t))
         deliver(t, first)
+        if t == 1:
+            chain(2)
         if t == 2:
-            chain(2)
-        if t == 0:
             mail.got(wo.at[1 - y, whalf], rsy.at[0], p.ny)
             mail.send(wo.at[1 - y, whalf], wo.at[1 - y, whalf], rsy.at[4], p.nc)
     pl.when(second)(far_ready)
+    chain(3)
     for t in range(4):
         pl.when(second)(functools.partial(far_attention, t))
         pl.when(second)(functools.partial(conclude, t))
         deliver(t, second)
-    chain(3)
     for zq in range(4):
         s = sid(zq, 1 - x, c)
         mail.got(rows_of(s), rsw.at[s], p.nx)

time: 156 us -> 156 us (level)
  no operation moved by 1% of the time
where the time goes in v6:
time: 156 us; the launch traced here: 155 us
  Pallas kernels  155 us (99%)
    pallas_call x1, Pallas kernels, fast(): pl.pallas_call(kernel, out_shape=raw, in_specs=in_vmem(len(args)), out_sp...  149 us
    pallas_call x1, Pallas kernels, fast(): pl.pallas_call(write_out, out_shape=shapes, in_specs=in_vmem(len(raw)), o...  5.46 us

profile of v6, /device:TPU:0, one launch (start us, length us, event | category | flops | bytes accessed | tf_op | source)
XLA Modules:
  0.0 155.4 jit_solution(12679287722327199941)
XLA Ops:
  0.7 149.1 %shard_map.263 = (bf16[128,768]{1,0:T(8,128)(2,1)}, f32[128,768]{1,0:T(8,128)}, bf16[16,96,768]{2,1,0:T(8,128)(2,1)}, bf16[16,48,384]{2,1,0:T(8,128)(2,1)}, f32[...) custom-call(bf16[128,768]{1,0:T(8,128)(2,1)} %x_ref.1, s32[128]{0:T(128)} %doc_ref.1, bf16[128,768]{1,0:T(8,128)(2,1)} %cot_ref.1, ...), custom_call_target="tpu_custom_call" | custom-call | tf_op jit(solution)/shard_map/pallas_call | solution.py:1047
  149.8 5.5 %shard_map.264 = (bf16[128,768]{1,0:T(8,128)(2,1)}, f32[128,768]{1,0:T(8,128)}, f32[768]{0:T(1024)}, f32[768]{0:T(1024)}, f32[3,768,384]{2,1,0:T(8,128)}, /*inde...) custom-call(bf16[128,768]{1,0:T(8,128)(2,1)} %get-tuple-element.34.l, ...), custom_call_target="tpu_custom_call" | custom-call | tf_op jit(solution)/shard_map/pallas_call | solution.py:1051

commit v7 on v6

--- a/solution.py
+++ b/solution.py
@@ -298,13 +298,13 @@
 
 
 def kernel(
-    x_ref, doc_ref, cot_ref, g1_ref, b1_ref, wq_ref, bqv_ref, wo_own, bo_ref, g2_ref, b2_ref, wup_ref, bup_ref, wdn_ref, bd_ref, tab_ref,
+    x_ref, doc_ref, cot_ref, g1_ref, b1_ref, wq_far, bqv_ref, wo_own, bo_ref, g2_ref, b2_ref, wup_ref, bup_ref, wdn_ref, bd_ref, tab_ref,
     lout, gin, wag, woag, o_ud, o_tot,
     qa, ka, va, ns, lse, ot, dpk, gwo, dh_s, wqh, bqh, buph, msc, asc,
     xs, docs, wb, wo, dyp, orecv, osend, kvs, kvf, attn, vt, hid, n2s, dys, acts, dpre, facc, dacc, ys, yr, fs, fr, fo,
-    dor, doa, delta, kt, dka, dva, dqt, dtt, dfs, dfr, packs, dqr, wms, wmr, n2t, dyt, ga, gb, gd, ge, ra, rb, gxr, gzr,
+    wq_ref, dor, doa, delta, kt, dka, dva, dqt, dtt, dfs, dfr, packs, dqr, wms, wmr, n2t, dyt, ga, gb, gd, ge, ra, rb, gxr, gzr,
     hc, hxs, hxr, hzs, hzr, dall, dns, dnr, vb1, vr1, vb2, vr2,
-    ss, rsx, rsc, rsd, rsw, rso, rsf, rsy, rdo, rga, rgx, rgz, rhc, rhx, rhz, rdf, rdq, rwm, rag, rwo, rdn, rv1, rv2, rv3, rv4,
+    ss, rsx, rsc, rsd, rsw, rso, rsf, rsy, rdo, rga, rgx, rgz, rhc, rhx, rhz, rdf, rdq, rwm, rag, rwo, rdn, rv1, rv2, rv3, rv4, lds,
 ):
     p = Place()
     mail = Mail(ss, SLOTS)
@@ -312,6 +312,15 @@
     first, second = both(p.unit, seg == 0), both(p.unit, seg == 1)
     row = lambda ref: ref[...].reshape(1, -1)
     p.greet()
+    wrow = pl.ds(pl.multiple_of(p.s * 48, 16), 48)
+    loads = [
+        pltpu.make_async_copy(wq_far, wq_ref, lds.at[0]),
+        pltpu.make_async_copy(wup_ref, wb.at[wrow, 0:1536], lds.at[1]),
+        pltpu.make_async_copy(wdn_ref, wb.at[wrow, 1536:3072], lds.at[2]),
+        pltpu.make_async_copy(wo_own, wo.at[y], lds.at[3]),
+    ]
+    for load in loads:
+        load.start()
 
     mix = mixed((128, 128), 0, 1)
     xs[b] = dot(mix, x_ref[...]).astype(B16)
@@ -320,9 +329,6 @@
     turn_odd = jnp.where(iota((128, 128), 0) == 2 * (iota((128, 128), 1) & 63) + 1, 1.0, 0.0).astype(B16)
     doc8 = jnp.broadcast_to(doc_row, (8, 128)).astype(B16)
     docs[b] = jnp.where(iota((8, 128), 0) == 0, dot(doc8, turn), dot(doc8, turn_odd))
-    wrow = pl.ds(pl.multiple_of(p.s * 48, 16), 48)
-    wb[wrow, 0:1536] = wup_ref[...]
-    wb[wrow, 1536:3072] = wdn_ref[...]
     p.meet()
 
     dims = ("x", "y", "z")
@@ -360,6 +366,7 @@
         mail.send(rows_of(s), rows_of(s), rsw.at[s], dev, cond)
 
 
+    loads[0].wait()
     pair_cols = pl.ds(pl.multiple_of(p.hl // 2 * 128, 128), 128)
     for odd in range(2):
 
@@ -394,7 +401,8 @@
         def _(half=half):
             buph[...] = bup_ref[half * 1536 : half * 1536 + 1536].reshape(1, 1536)
 
-    wo[y] = wo_own[...]
+    for load in loads[1:]:
+        load.wait()
 
     def qkv(i):
         rows = xs[pl.ds(2 * i, 2)].reshape(256, 768).astype(F32)
@@ -1032,20 +1040,22 @@
         vm(16, 128, 768), vf(17, 8, 128), vm(768, 3072), vm(2, 384, 768), vm(2, 128, 768), vm(12, 128, 128), vm(4, 256, 128),
         vm(4, 256, 128), vm(4, 256, 128), vm(256, 768), vm(6, 128, 512), vf(256, 768), vm(256, 768), vm(256, 768), vm(256, 1536),
         vm(256, 1536), vf(256, 768), vf(256, 768), vm(3, 256, 256), vm(3, 256, 256), vm(128, 768), vm(128, 768), vf(128, 768),
-        vm(4, 256, 128), vm(4, 512, 128), vf(4, 1, 512), vm(6, 128, 512), vf(512, 128), vf(512, 128), vf(4, 128, 512), vm(192, 2048),
+        vm(3, 768, 384), vm(4, 256, 128), vm(4, 512, 128), vf(4, 1, 512), vm(6, 128, 512), vf(512, 128), vf(512, 128), vf(4, 128, 512), vm(192, 2048),
         vm(4, 256, 128), vm(4, 256, 128), vm(4, 3, 256, 128), vm(6, 3, 128, 128), vm(2, 96, 768), vm(96, 768),
         vm(768, 256), vm(768, 256), *[vm(4, 48, 3072)] * 8,
         vm(2, 4, 48, 384), vm(4, 48, 384), vm(4, 48, 384), vm(4, 48, 384), vm(4, 48, 384), vm(3, 256, 384), vm(128, 768), vm(128, 768),
         vf(4, 8, 768), vf(8, 8, 768), vf(4, 8, 768), vf(8, 8, 768),
         dma(SLOTS), dma(3, 8), dma(3, 8), dma(3), dma(16), dma(12), dma(2), dma(8), dma(8), dma(2), dma(4), dma(3), dma(2, 4), dma(4),
-        dma(3), dma(2), dma(6), dma(1), dma(16), dma(16), dma(1), dma(4), dma(8), dma(4), dma(8),
+        dma(3), dma(2), dma(6), dma(1), dma(16), dma(16), dma(1), dma(4), dma(8), dma(4), dma(8), dma(4),
     ]
     args = (
         layer_input, doc_ids, cotangent, ln1_gain, ln1_bias, w_qkv.transpose(1, 0, 2), bias_qv, w_out, b_out, ln2_gain, ln2_bias, w_up,
         b_up, w_down.T, b_down, jnp.asarray(count_table()),
     )
     found = pl.pallas_call(
-        kernel, out_shape=raw, in_specs=in_vmem(len(args)), out_specs=tuple(in_vmem(len(raw))), scratch_shapes=scratch,
+        kernel, out_shape=raw,
+        in_specs=[pl.BlockSpec(memory_space=pl.ANY) if i in (5, 7, 11, 13) else in_vmem(1)[0] for i in range(len(args))],
+        out_specs=tuple(in_vmem(len(raw))), scratch_shapes=scratch,
         compiler_params=pltpu.CompilerParams(collective_id=0, has_side_effects=True, vmem_limit_bytes=LIMIT),
     )(*args)
     outs = pl.pallas_call(

time: 156 us -> 155 us (level)
  no operation moved by 1% of the time
where the time goes in v7:
time: 155 us
  Pallas kernels  154 us (99%)
    pallas_call x1, Pallas kernels, fast(): pl.pallas_call(kernel, out_shape=raw, in_specs=[pl.BlockSpec(memory_space...  148 us
    pallas_call x1, Pallas kernels, fast(): pl.pallas_call(write_out, out_shape=shapes, in_specs=in_vmem(len(raw)), o...  5.46 us

profile of v7, /device:TPU:0, one launch (start us, length us, event | category | flops | bytes accessed | tf_op | source)
XLA Modules:
  0.0 154.7 jit_solution(4905242301236022297)
XLA Ops:
  0.7 148.4 %shard_map.263 = (bf16[128,768]{1,0:T(8,128)(2,1)}, f32[128,768]{1,0:T(8,128)}, bf16[16,96,768]{2,1,0:T(8,128)(2,1)}, bf16[16,48,384]{2,1,0:T(8,128)(2,1)}, f32[...) custom-call(bf16[128,768]{1,0:T(8,128)(2,1)} %x_ref.1, s32[128]{0:T(128)} %doc_ref.1, bf16[128,768]{1,0:T(8,128)(2,1)} %cot_ref.1, ...), custom_call_target="tpu_custom_call" | custom-call | tf_op jit(solution)/shard_map/pallas_call | solution.py:1055
  149.1 5.5 %shard_map.264 = (bf16[128,768]{1,0:T(8,128)(2,1)}, f32[128,768]{1,0:T(8,128)}, f32[768]{0:T(1024)}, f32[768]{0:T(1024)}, f32[3,768,384]{2,1,0:T(8,128)}, /*inde...) custom-call(bf16[128,768]{1,0:T(8,128)(2,1)} %get-tuple-element.34.l, ...), custom_call_target="tpu_custom_call" | custom-call | tf_op jit(solution)/shard_map/pallas_call | solution.py:1061
